TPU v7x, 128 devices: a whole 4x4x4 slice. The times are simulated.
128 devices in a mesh: lon: 8 (over z, x_lo), lat: 16 (over y, x_hi, core).
Axes of the slice: x: 4 (x_hi: 2, x_lo: 2; x = x_hi * 2 + x_lo), y: 4, z: 4, core: 2. Of those that a mesh axis runs over, the one named last changes fastest.
Arguments:
- monthly_field: bfloat16 [512, 240, 1440], P(('lon', 'lat')), may hold values from -8 to 8
- half_width: int32 [240], P('lat'), may hold values from 1 to 64, as said below
- land_mask: int32 [240, 1440], P('lat', 'lon'), may hold values 0 or 1
Outputs:
- patterns: bfloat16 [512, 240, 1440], P(None, 'lat', 'lon')
- whitener: float32 [512, 512], replicated
Inputs may be any that keep to these rules, and one draw needn't show every extreme that they name: `half_width`: some grid row has a half-width of exactly 64.
All inputs are finite; a program needn't handle non-finite values. No bound on the sum of `land_mask` on one device may be relied on, other than what follows from the above.
Results may differ from a plain program's by a relative error of at most 0.0079.
Values may be sent and summed in bfloat16 or wider, within the bound.
No kernel may reach another device: no remote copies, remote signals or barrier semaphores. Data moves between devices by JAX's collectives and lax.ppermute only.
A program may use at most 128 MiB of HBM per device.

v0:
```python
import math

import jax
import jax.numpy as jnp
from jax import lax
from jax.sharding import PartitionSpec as P

HMAX = 64
HL = 2
ITERS = 8


def extended(x, sides, width, wrap):
    for axis, dim in sides:
        peers, length = (lax.axis_size(axis), x.shape[dim])
        up = [(i, (i + 1) % peers) for i in range(peers if wrap else peers - 1)]
        down = [(j, i) for i, j in up]
        last = lax.slice_in_dim(x, length - width, length, axis=dim)
        leading = lax.slice_in_dim(x, 0, width, axis=dim)
        before = lax.ppermute(last, axis, up)
        after = lax.ppermute(leading, axis, down)
        x = jnp.concatenate([before, x, after], axis=dim)
    return x


def gauss_band(widths, half_span, band_cols):
    offsets = (
        jnp.arange(band_cols + 2 * half_span)[:, None] - half_span - jnp.arange(band_cols)[None, :]
    ).astype(jnp.float32)
    reach = widths.astype(jnp.float32)
    spread = 0.5 * reach
    tap_offsets = jnp.arange(-half_span, half_span + 1).astype(jnp.float32)
    tap_values = jnp.exp(
        -(tap_offsets[None, :] * tap_offsets[None, :]) / (2.0 * spread[:, None] * spread[:, None])
    )
    tap_values = tap_values * (jnp.abs(tap_offsets)[None, :] <= reach[:, None]).astype(jnp.float32)
    tap_total = jnp.sum(tap_values, axis=1)
    inside = (jnp.abs(offsets)[None] <= reach[:, None, None]).astype(jnp.float32)
    square = offsets[None] * offsets[None]
    band = (
        jnp.exp(-square / (2.0 * spread[:, None, None] * spread[:, None, None]))
        * inside
        / tap_total[:, None, None]
    )
    return band.astype(jnp.bfloat16)


def regroup(months_block, n_lon, n_lat):
    month_count, lat_cells, lon_cells = months_block.shape
    lat_dev = lat_cells // n_lat
    lon_dev = lon_cells // n_lon
    pieces = months_block.reshape(month_count, n_lat, lat_dev, n_lon, lon_dev).transpose(
        3, 1, 0, 2, 4
    )
    flat_pieces = pieces.reshape(n_lon * n_lat, month_count, lat_dev, lon_dev)
    landed = lax.all_to_all(flat_pieces, ("lon", "lat"), split_axis=0, concat_axis=0, tiled=True)
    return landed.reshape(-1, lat_dev, lon_dev)


def replicated_root(gram, scale_cells):
    frobenius = jnp.sqrt(jnp.sum(gram * gram) + 1e-06)
    identity = jnp.eye(gram.shape[0], dtype=jnp.float32)
    iterate_y = gram / frobenius
    iterate_z = identity
    for sweep in range(ITERS):
        factor = 1.5 * identity - 0.5 * jnp.dot(
            iterate_z, iterate_y, precision=lax.Precision.HIGHEST
        )
        iterate_y = jnp.dot(iterate_y, factor, precision=lax.Precision.HIGHEST)
        iterate_z = jnp.dot(factor, iterate_z, precision=lax.Precision.HIGHEST)
    return iterate_z * jnp.sqrt(scale_cells / frobenius)


def local(monthly_field, half_width, land_mask):
    n_lon = lax.axis_size("lon")
    n_lat = lax.axis_size("lat")
    regrouped = regroup(monthly_field, n_lon, n_lat)
    band_lon = gauss_band(half_width, HMAX, regrouped.shape[2])
    rimmed = extended(regrouped, (("lon", 2),), HMAX, True)
    lonpass = jnp.einsum(
        "mrj,rjk->mrk", rimmed, band_lon, preferred_element_type=jnp.float32
    ).astype(jnp.bfloat16)
    band_lat = gauss_band(jnp.full((1,), HL, jnp.int32), HL, regrouped.shape[1])[0]
    lat_rimmed = extended(lonpass, (("lat", 1),), HL, False)
    smoothed = jnp.einsum(
        "mik,io->mok", lat_rimmed, band_lat, preferred_element_type=jnp.float32
    ).astype(jnp.bfloat16)
    month_total, lat_dev, lon_dev = smoothed.shape
    mean_field = jnp.mean(smoothed, axis=0, dtype=jnp.float32)
    lat_cells = lat_dev * n_lat
    row_index = lax.axis_index("lat") * lat_dev + jnp.arange(lat_dev)
    latitude = math.pi * ((row_index.astype(jnp.float32) + 0.5) / lat_cells - 0.5)
    weight = jnp.sqrt(jnp.cos(latitude))[:, None] * land_mask.astype(jnp.float32)
    anomaly = ((smoothed.astype(jnp.float32) - mean_field) * weight).astype(jnp.bfloat16)
    flat_cells = anomaly.reshape(month_total, lat_dev * lon_dev)
    partial_gram = lax.dot_general(
        flat_cells, flat_cells, (((1,), (1,)), ((), ())), preferred_element_type=jnp.float32
    )
    scale_cells = float(lat_cells * lon_dev * n_lon)
    gram = lax.psum(partial_gram, ("lon", "lat"))
    whitener = replicated_root(gram, scale_cells)
    patterns = jnp.dot(
        whitener.astype(jnp.bfloat16), flat_cells, preferred_element_type=jnp.float32
    )
    patterns = patterns.astype(jnp.bfloat16).reshape(month_total, lat_dev, lon_dev)
    return (patterns, whitener)


def solution(mesh):
    placed = (P(("lon", "lat"), None, None), P("lat"), P("lat", "lon"))
    return jax.shard_map(
        local, mesh=mesh, in_specs=placed, out_specs=(P(None, "lat", "lon"), P()), check_vma=False
    )
```

profile of v0, /device:TPU:1, one launch (start us, length us, event | category | flops | bytes accessed | tf_op | source)
XLA Modules:
  0.0 378.2 jit_solution(5563230891432504196)
XLA Ops:
  7.2 8.8 %reshape.139 = bf16[4,16,15,8,180]{4,3,2,1,0:T(8,128)(2,1)} reshape(bf16[4,240,1440]{2,1,0:T(8,128)(2,1)} %param.3) | data formatting | bytes 5529600 | tf_op jit(solution)/shard_map/reshape | solution.py:52
  16.0 5.1 %copy.39 = bf16[4,16,15,8,180]{4,0,2,1,3:T(4,128)(2,1)S(1)} copy(bf16[4,16,15,8,180]{4,3,2,1,0:T(8,128)(2,1)} %reshape.139) | data formatting | bytes 5529600 | tf_op jit(solution)/shard_map/reshape | solution.py:52
  21.2 60.9 %all_to_all.5 = bf16[128,4,15,180]{3,1,2,0:T(4,128)(2,1)S(1)} all-to-all(bf16[128,4,15,180]{3,1,2,0:T(4,128)(2,1)S(1)} %bitcast.68), channel_id=1, replica_groups=mesh['lon'=8,'lat'=16] {'lon','lat'}, dimensions={0} | all-to-all | bytes 5529600 | tf_op jit(solution)/shard_map/all_to_all | solution.py:56
  82.1 3.7 copy.40
  85.8 7.2 %reshape.141 = bf16[512,15,180]{2,0,1:T(8,128)(2,1)} reshape(bf16[128,4,15,180]{3,1,0,2:T(4,128)(2,1)} %copy.40) | data formatting | bytes 5529600 | tf_op jit(solution)/shard_map/reshape | solution.py:57
  93.0 4.2 %copy.41 = bf16[512,15,180]{0,2,1:T(8,128)(2,1)S(1)} copy(bf16[512,15,180]{2,0,1:T(8,128)(2,1)} %reshape.141) | data formatting | bytes 5529600 | tf_op jit(solution)/shard_map/reshape | solution.py:57
  98.2 3.1 collective-permute-start.1
  101.5 20.7 %collective-permute-done = bf16[512,15,64]{0,2,1:T(8,128)(2,1)S(1)} collective-permute-done((bf16[512,15,64]{0,2,1:T(8,128)(2,1)S(1)}, bf16[512,15,64]{0,2,1:T(8,128)(2,1)S(1)}, u32[]{:S(2)}, u32[]{:S(2)}) %collective-permute-start) | collective-permute-done | bytes 983072 | tf_op jit(solution)/shard_map/ppermute | solution.py:20
  122.2 19.5 %collective-permute-done.1 = bf16[512,15,64]{0,2,1:T(8,128)(2,1)S(1)} collective-permute-done((bf16[512,15,64]{0,2,1:T(8,128)(2,1)S(1)}, bf16[512,15,64]{0,2,1:T(8,128)(2,1)S(1)}, u32[]{:S(2)}, u32[]{:S(2)}) %collective-permute-start.1) | collective-permute-done | bytes 983072 | tf_op jit(solution)/shard_map/ppermute | solution.py:21
  141.8 2.7 convert_bitcast_fusion
  146.1 4.8 %collective-permute-start.2 = (bf16[512,2,180]{0,2,1:T(8,128)(2,1)S(1)}, bf16[512,2,180]{0,2,1:T(8,128)(2,1)S(1)}, u32[]{:S(2)}, u32[]{:S(2)}) collective-permute-start(bf16[512,2,180]{0,2,1:T(8,128)(2,1)S(1)} %get-tuple-element.2), channel_id=1, source_target_pairs={{0,1},{1,2},{2,3},{3,4},{4,5},{5,6},{6,7},{7,8},{8,9},{9,10},{10,1... | collective-permute-start | bytes 1105928 | tf_op jit(solution)/shard_map/ppermute | solution.py:20
  150.9 2.1 collective-permute-start.3
  155.4 5.9 %collective-permute-done.3 = bf16[512,2,180]{0,2,1:T(8,128)(2,1)S(1)} collective-permute-done((bf16[512,2,180]{0,2,1:T(8,128)(2,1)S(1)}, bf16[512,2,180]{0,2,1:T(8,128)(2,1)S(1)}, u32[]{:S(2)}, u32[]{:S(2)}) %collective-permute-start.3) | collective-permute-done | bytes 368672 | tf_op jit(solution)/shard_map/ppermute | solution.py:21
  161.3 2.0 pad_maximum_fusion
  163.3 2.3 fusion.8
  165.7 3.0 bitcast_reduce_fusion
  168.7 2.4 fusion.1
  171.1 2.7 convolution_bitcast_fusion
  173.8 2.0 reshape.142
  175.8 144.5 %all-reduce.2.cloned.1.call-done = f32[512,512]{1,0:T(8,128)} async-done(((f32[512,512]{1,0:T(8,128)}), f32[512,512]{1,0:T(8,128)}) %all-reduce.2.cloned.1.call-update) | async-done | bytes 1048592 | tf_op jit(solution)/shard_map/psum | solution.py:100
  320.2 2.1 multiply_reduce_fusion
  323.0 2.4 select_subtract_fusion.7
  326.5 1.9 fusion.24
  328.3 1.9 select_subtract_fusion.6
  333.9 2.0 select_subtract_fusion.5
  345.2 1.8 select_subtract_fusion.3
  347.1 2.1 fusion.49
  351.0 1.8 select_subtract_fusion.2
  360.3 2.1 fusion.52
  362.5 1.9 select_subtract_fusion
  364.4 1.9 convolution_multiply_fusion
  369.0 2.0 reshape.143
  (43 shorter events, 31.1 us)
Async XLA Ops:
  7.2 313.1 %all-reduce.2.cloned.1.call-start = ((), (), s32[]{:S(2)}) async-start(), calls=%async_computation.1 | async-start | bytes 2097152 | tf_op jit(solution)/shard_map/psum | solution.py:100
  97.2 4.1 %copy-start.5 = (s32[15]{0:T(128)S(1)}, s32[15]{0:T(128)}, u32[]{:S(2)}) copy-start(s32[15]{0:T(128)} %param.4) | copy-start | bytes 184
  97.6 24.6 %collective-permute-start = (bf16[512,15,64]{0,2,1:T(8,128)(2,1)S(1)}, bf16[512,15,64]{0,2,1:T(8,128)(2,1)S(1)}, u32[]{:S(2)}, u32[]{:S(2)}) collective-permute-start(bf16[512,15,64]{0,2,1:T(8,128)(2,1)S(1)} %get-tuple-element.4), channel_id=1, source_target_pairs={{0,16},{16,32},{32,48},{48,64},{64,80},{80,96},{96,112},{112,0},{1... | collective-permute-start | bytes 2949128 | tf_op jit(solution)/shard_map/ppermute | solution.py:20
  98.2 43.6 %collective-permute-start.1 = (bf16[512,15,64]{0,2,1:T(8,128)(2,1)S(1)}, bf16[512,15,64]{0,2,1:T(8,128)(2,1)S(1)}, u32[]{:S(2)}, u32[]{:S(2)}) collective-permute-start(bf16[512,15,64]{0,2,1:T(8,128)(2,1)S(1)} %get-tuple-element.5), channel_id=1, source_target_pairs={{16,0},{32,16},{48,32},{64,48},{80,64},{96,80},{112,96},{0,112},{1... | collective-permute-start | bytes 2949128 | tf_op jit(solution)/shard_map/ppermute | solution.py:21
  141.7 12.0 %copy-start.4 = (s32[15,180]{1,0:T(8,128)S(1)}, s32[15,180]{1,0:T(8,128)}, u32[]{:S(2)}) copy-start(s32[15,180]{1,0:T(8,128)} %param.5) | copy-start | bytes 32404
  144.5 1.6 copy-start
  146.1 9.3 %collective-permute-start.2 = (bf16[512,2,180]{0,2,1:T(8,128)(2,1)S(1)}, bf16[512,2,180]{0,2,1:T(8,128)(2,1)S(1)}, u32[]{:S(2)}, u32[]{:S(2)}) collective-permute-start(bf16[512,2,180]{0,2,1:T(8,128)(2,1)S(1)} %get-tuple-element.2), channel_id=1, source_target_pairs={{0,1},{1,2},{2,3},{3,4},{4,5},{5,6},{6,7},{7,8},{8,9},{9,10},{10,1... | collective-permute-start | bytes 1105928 | tf_op jit(solution)/shard_map/ppermute | solution.py:20
  150.9 10.4 %collective-permute-start.3 = (bf16[512,2,180]{0,2,1:T(8,128)(2,1)S(1)}, bf16[512,2,180]{0,2,1:T(8,128)(2,1)S(1)}, u32[]{:S(2)}, u32[]{:S(2)}) collective-permute-start(bf16[512,2,180]{0,2,1:T(8,128)(2,1)S(1)} %get-tuple-element.3), channel_id=1, source_target_pairs={{1,0},{2,1},{3,2},{4,3},{5,4},{6,5},{7,6},{8,7},{9,8},{10,9},{11,1... | collective-permute-start | bytes 1105928 | tf_op jit(solution)/shard_map/ppermute | solution.py:21
  323.0 3.4 copy-start.2
  362.5 4.7 %copy-start.1 = (bf16[512,2700]{0,1:T(8,128)(2,1)S(1)}, bf16[512,2700]{0,1:T(8,128)(2,1)}, u32[]{:S(2)}) copy-start(bf16[512,2700]{0,1:T(8,128)(2,1)} %reshape.142) | copy-start | bytes 8294404
  366.3 1.0 copy-start.3
Sparse Core Ops, SparseCore 0:
  173.9 146.2 all-reduce.1
where the time goes:
time: 386 us; the launch traced here: 378 us
  waiting for transfers between devices  192 us (50%)
  blocking collectives  60.9 us (16%)
  matrix products  52.4 us (14%)
  local copies, waits for them, and re-layouts  36 us (9%)
  between operations  15.6 us (4%)
  starting transfers between devices  10.6 us (3%)
  other arithmetic  10.5 us (3%)
    psum x1, waiting for transfers between devices, local(): gram = lax.psum(partial_gram, ('lon', 'lat'))  144 us
    all_to_all x1, blocking collectives, regroup(): lax.all_to_all(flat_pieces, ('lon', 'lat'), split_axis=0, concat_axis=0,...  60.9 us
    ppermute x2, waiting for transfers between devices, extended(): after = lax.ppermute(leading, axis, down)  25.4 us
    ppermute x2, waiting for transfers between devices, extended(): before = lax.ppermute(last, axis, up)  22.3 us
    dot_general x8, matrix products, replicated_root(): jnp.dot(iterate_z, iterate_y, precision=lax.Precision.HIGHEST)  15.5 us
    dot_general x8, matrix products, replicated_root(): iterate_z = jnp.dot(factor, iterate_z, precision=lax.Precision.HIGHEST)  14.2 us
    reshape x2, local copies, waits for them, and re-layouts, regroup(): months_block.reshape(month_count, n_lat, lat_dev, n_lon, lon_dev)  13.9 us
    dot_general x7, matrix products, replicated_root(): iterate_y = jnp.dot(iterate_y, factor, precision=lax.Precision.HIGHEST)  13.2 us
  transfers between devices with their start and end apart: 5, of which 5 were waited for; matrix products, arithmetic and copies ran while one was open for 1% of the time, Pallas kernels for 0%

commit v1 on v0

v1 whole, which is shorter than its diff:
```python
import math

import jax
import jax.numpy as jnp
import numpy as np
from jax import lax
from jax.experimental import pallas as pl
from jax.experimental.pallas import tpu as pltpu
from jax.sharding import PartitionSpec as P

HMAX = 64
HL = 2
ITERS = 8
BOTH = ("lon", "lat")
N_LON = 8
N_LAT = 16
NLAT = 240
NLON = 1440
MONTHS = 512
MON_DEV = 4
LAT_DEV = 15
LON_DEV = 180
LANES = 128
GROUPS = 22
SECOND = 56
TAIL = 112
CHUNK = MON_DEV * GROUPS
WINDOWS = MON_DEV * N_LON
SROWS = 3 * WINDOWS
SSTRIDE = 97
VSTRIDE = 89
BLOCKS = [(i, j) for i in range(4) for j in range(i, 4)]
PACK = len(BLOCKS)
VMEM_LIMIT = 60 * 1024 * 1024


def lat_taps():
    offsets = np.arange(-HL, HL + 1).astype(np.float32)
    taps = np.exp(-(offsets * offsets) / np.float32(2.0)).astype(np.float32)
    taps = taps / taps.sum(dtype=np.float32)
    return [float(t) for t in taps.astype(jnp.bfloat16).astype(np.float32)]


def smooth_kernel(widths, field, out, taps, windows, passed, staged):
    lane8 = lax.broadcasted_iota(jnp.int32, (8, LANES), 1)
    sub8 = lax.broadcasted_iota(jnp.int32, (8, LANES), 0)

    def build_taps(i, carry):
        reach = jnp.zeros((8, LANES), jnp.int32)
        for s in range(8):
            reach = jnp.where(sub8 == s, widths[i * 8 + s], reach)
        reach = reach.astype(jnp.float32)
        spread = 0.5 * reach
        offset = (lane8 - HMAX).astype(jnp.float32)
        value = jnp.exp(-(offset * offset) / (2.0 * spread * spread))
        value = jnp.where(jnp.abs(offset) <= reach, value, 0.0)
        total = jnp.sum(value, axis=1, keepdims=True) + value[:, 0:1]
        value = (value / total).astype(jnp.bfloat16).astype(jnp.float32)
        taps[pl.ds(pl.multiple_of(i * 8, 8), 8), :] = value
        return carry

    lax.fori_loop(0, NLAT // 8, build_taps, 0)

    def build_windows(i, carry):
        for m in range(MON_DEV):
            rows = field[m, pl.ds(pl.multiple_of(i * 16, 16), 16), :].astype(jnp.float32)
            ring = jnp.concatenate([rows, rows[:, :224]], axis=1)
            for l in range(N_LON):
                for j in range(3):
                    start = LON_DEV * l - HMAX + LANES * j
                    start = start + NLON if start < 0 else start
                    piece = ring[:, start : start + LANES]
                    for half in range(2):
                        first = (i * 16 + half * 8) * SSTRIDE + j * WINDOWS + m * N_LON + l
                        windows[pl.ds(first, 8, stride=SSTRIDE), :] = piece[half * 8 : half * 8 + 8]
        return carry

    lax.fori_loop(0, NLAT // 16, build_windows, 0)

    edge = jnp.zeros((HL, 2 * WINDOWS, LANES), jnp.float32)
    passed[0:HL] = edge
    passed[NLAT + HL : NLAT + 2 * HL] = edge
    sub = lax.broadcasted_iota(jnp.int32, (LANES, LANES), 0)
    lane = lax.broadcasted_iota(jnp.int32, (LANES, LANES), 1)

    def lon_row(r, carry):
        lhs = windows[pl.ds(r * SSTRIDE, SROWS), :].astype(jnp.bfloat16)
        spread_taps = jnp.broadcast_to(taps[pl.ds(r, 1), :], (LANES, LANES))
        ring = pltpu.roll(spread_taps, 0, 1, stride=1, stride_axis=0)
        top = jnp.where(sub >= lane, ring, 0.0).astype(jnp.bfloat16)
        bottom = jnp.where(sub <= lane, ring, 0.0).astype(jnp.bfloat16)
        left = jnp.concatenate([lhs[: 2 * WINDOWS], lhs[WINDOWS:]], axis=1)
        right = jnp.concatenate([top, bottom], axis=0)
        res = jnp.dot(left, right, preferred_element_type=jnp.float32)
        passed[r + HL] = res.astype(jnp.bfloat16).astype(jnp.float32)
        return carry

    lax.fori_loop(0, NLAT, lon_row, 0, unroll=4)

    w0, w1, w2 = lat_taps()[:3]
    laneb = lax.broadcasted_iota(jnp.int32, (WINDOWS, LANES), 1)

    def lat_band(b, carry):
        def smoothed(rr, lo, hi):
            r = b * LAT_DEV + rr
            outer = passed[r, lo:hi] + passed[r + 4, lo:hi]
            inner = passed[r + 1, lo:hi] + passed[r + 3, lo:hi]
            return w0 * outer + w1 * inner + w2 * passed[r + 2, lo:hi]

        def put(g, value):
            for m in range(MON_DEV):
                staged[pl.ds(m * GROUPS + g, N_LON, stride=VSTRIDE), :] = value[8 * m : 8 * m + 8]

        for rr in range(LAT_DEV):
            put(rr, smoothed(rr, 0, WINDOWS))
        last = smoothed(LAT_DEV - 1, WINDOWS, 2 * WINDOWS)
        for q in range(7):
            even = smoothed(2 * q, WINDOWS, 2 * WINDOWS)
            odd = smoothed(2 * q + 1, WINDOWS, 2 * WINDOWS)
            value = jnp.where(laneb < SECOND, even, pltpu.roll(odd, SECOND, 1))
            if q < 4:
                tail = pltpu.roll(last, TAIL - 16 * q, 1)
                value = jnp.where(laneb < TAIL, value, tail)
            put(LAT_DEV + q, value)
        for l in range(N_LON):
            out[l * N_LAT + b] = staged[l * VSTRIDE : l * VSTRIDE + CHUNK, :].astype(jnp.bfloat16)
        return carry

    lax.fori_loop(0, N_LAT, lat_band, 0)


def smooth(widths, field):
    return pl.pallas_call(
        smooth_kernel,
        out_shape=jax.ShapeDtypeStruct((N_LON * N_LAT, CHUNK, LANES), jnp.bfloat16),
        in_specs=[
            pl.BlockSpec(memory_space=pltpu.SMEM),
            pl.BlockSpec(memory_space=pltpu.VMEM),
        ],
        out_specs=pl.BlockSpec(memory_space=pltpu.VMEM),
        scratch_shapes=[
            pltpu.VMEM((NLAT, LANES), jnp.float32),
            pltpu.VMEM((NLAT * SSTRIDE + 8, LANES), jnp.float32),
            pltpu.VMEM((NLAT + 2 * HL, 2 * WINDOWS, LANES), jnp.float32),
            pltpu.VMEM((N_LON * VSTRIDE + 8, LANES), jnp.float32),
        ],
        compiler_params=pltpu.CompilerParams(vmem_limit_bytes=VMEM_LIMIT),
        name="smooth",
    )(widths, field)


def gram_kernel(landed, weight, packed, anomaly, wide):
    def widen(s, carry):
        wide[pl.ds(pl.multiple_of(s * CHUNK, 8), CHUNK), :] = landed[s].astype(jnp.float32)
        return carry

    lax.fori_loop(0, N_LON * N_LAT, widen, 0, unroll=4)
    lane = lax.broadcasted_iota(jnp.int32, (1, LANES), 1)
    for g in range(GROUPS):
        if g < LAT_DEV:
            scale = weight[g : g + 1, :LANES]
        else:
            q = g - LAT_DEV
            scale = weight[2 * q : 2 * q + 1, LANES:]
            scale = scale + pltpu.roll(weight[2 * q + 1 : 2 * q + 2, LANES:], SECOND, 1)
            if q < 4:
                last = weight[LAT_DEV - 1 : LAT_DEV, LANES:]
                last = jnp.where((lane >= 16 * q) & (lane < 16 * q + 16), last, 0.0)
                scale = scale + pltpu.roll(last, TAIL - 16 * q, 1)
        cells = wide[pl.ds(g, MONTHS, stride=GROUPS), :]
        mean = jnp.sum(cells, axis=0, keepdims=True) * (1.0 / MONTHS)
        anomaly[:, g * LANES : (g + 1) * LANES] = ((cells - mean) * scale).astype(jnp.bfloat16)
    half = MONTHS // 2
    for i, j in ((0, 0), (0, 1), (1, 1)):
        block = lax.dot_general(
            anomaly[i * half : (i + 1) * half, :],
            anomaly[j * half : (j + 1) * half, :],
            (((1,), (1,)), ((), ())),
            preferred_element_type=jnp.float32,
        )
        for n, (bi, bj) in enumerate(BLOCKS):
            if bi // 2 == i and bj // 2 == j:
                a, c = (bi % 2) * LANES, (bj % 2) * LANES
                packed[pl.ds(n, LANES, stride=PACK), :] = block[a : a + LANES, c : c + LANES]


def gram_terms(landed, weight):
    return pl.pallas_call(
        gram_kernel,
        out_shape=(
            jax.ShapeDtypeStruct((LANES * PACK, LANES), jnp.float32),
            jax.ShapeDtypeStruct((MONTHS, GROUPS * LANES), jnp.bfloat16),
        ),
        in_specs=[pl.BlockSpec(memory_space=pltpu.VMEM)] * 2,
        out_specs=(pl.BlockSpec(memory_space=pltpu.VMEM),) * 2,
        scratch_shapes=[pltpu.VMEM((N_LON * N_LAT * CHUNK, LANES), jnp.float32)],
        compiler_params=pltpu.CompilerParams(vmem_limit_bytes=VMEM_LIMIT),
        name="gram_terms",
    )(landed, weight)


def add_kernel(terms, out):
    step = 4 * PACK
    total = terms[0:step, :]
    for s in range(1, LANES // 4):
        total = total + terms[s * step : (s + 1) * step, :]
    row = total[0:PACK] + total[PACK : 2 * PACK] + total[2 * PACK : 3 * PACK] + total[3 * PACK :]
    total = jnp.concatenate([row] * 4, axis=0)
    for s in range(LANES // 4):
        out[s * step : (s + 1) * step, :] = total


def add_terms(terms):
    return pl.pallas_call(
        add_kernel,
        out_shape=jax.ShapeDtypeStruct(terms.shape, jnp.float32),
        in_specs=[pl.BlockSpec(memory_space=pltpu.VMEM)],
        out_specs=pl.BlockSpec(memory_space=pltpu.VMEM),
        name="add_terms",
    )(terms)


STEP = (2.25, -2.4375, 1.6875, -0.5625, 0.0625)
ROWB = 256


def root_kernel(packed, anomaly, patterns, whitener, *scratch):
    (wh, wl), (sh, sl), (hh, hl), (ph, pl_), (zh, zl) = [scratch[2 * k : 2 * k + 2] for k in range(5)]
    for n, (bi, bj) in enumerate(BLOCKS):
        block = packed[pl.ds(n, LANES, stride=PACK), :]
        whitener[bi * LANES : (bi + 1) * LANES, bj * LANES : (bj + 1) * LANES] = block
        if bi != bj:
            whitener[bj * LANES : (bj + 1) * LANES, bi * LANES : (bi + 1) * LANES] = block.T
    gram = whitener[...]
    squares = jnp.sum(gram * gram, axis=0, keepdims=True)
    frobenius = jnp.sqrt(jnp.sum(squares, axis=1, keepdims=True) + 1e-06)
    final_scale = jnp.sqrt(float(NLAT * NLON) / frobenius)

    def split(hi, lo, rows, value):
        high = value.astype(jnp.bfloat16)
        hi[rows, :] = high
        lo[rows, :] = (value - high.astype(jnp.float32)).astype(jnp.bfloat16)

    def join(hi, lo, rows):
        return hi[rows, :].astype(jnp.float32) + lo[rows, :].astype(jnp.float32)

    def product(ah, al, bh, bl, rows):
        return (
            jnp.dot(ah[rows, :], bh[...], preferred_element_type=jnp.float32)
            + jnp.dot(ah[rows, :], bl[...], preferred_element_type=jnp.float32)
            + jnp.dot(al[rows, :], bh[...], preferred_element_type=jnp.float32)
        )

    def plus_eye(value, start, scale):
        row = lax.broadcasted_iota(jnp.int32, value.shape, 0) + start
        column = lax.broadcasted_iota(jnp.int32, value.shape, 1)
        return jnp.where(row == column, value + scale, value)

    split(wh, wl, pl.ds(0, MONTHS), gram / frobenius)
    starts = [k * ROWB for k in range(MONTHS // ROWB)]
    c0, c1, c2, c3, c4 = STEP
    last = ITERS // 2 - 1

    def double_step(k, carry):
        for start in starts:
            rows = pl.ds(start, ROWB)
            square = product(wh, wl, wh, wl, rows)
            split(sh, sl, rows, square)
            split(hh, hl, rows, plus_eye(c3 * join(wh, wl, rows) + c4 * square, start, c2))
        for start in starts:
            rows = pl.ds(start, ROWB)
            value = product(sh, sl, hh, hl, rows) + c1 * join(wh, wl, rows)
            split(ph, pl_, rows, plus_eye(value, start, c0))

        @pl.when(k == 0)
        def _():
            zh[...] = ph[...]
            zl[...] = pl_[...]

        @pl.when(k > 0)
        def _():
            for start in starts:
                rows = pl.ds(start, ROWB)
                value = product(zh, zl, ph, pl_, rows)
                split(zh, zl, rows, value)
                whitener[rows, :] = value * final_scale

        @pl.when(k < last)
        def _():
            for start in starts:
                rows = pl.ds(start, ROWB)
                split(sh, sl, rows, product(wh, wl, ph, pl_, rows))
            for start in starts:
                rows = pl.ds(start, ROWB)
                split(wh, wl, rows, product(sh, sl, ph, pl_, rows))

        return carry

    lax.fori_loop(0, last + 1, double_step, 0)

    sh[...] = whitener[...].astype(jnp.bfloat16)
    for g in range(GROUPS):
        value = lax.dot_general(
            anomaly[:, g * LANES : (g + 1) * LANES],
            sh[...],
            (((0,), (1,)), ((), ())),
            preferred_element_type=jnp.float32,
        ).astype(jnp.bfloat16)
        if g < LAT_DEV:
            patterns[g, 0:LANES, :] = value
        else:
            q = g - LAT_DEV
            patterns[2 * q, LANES:, :] = value[0 : LON_DEV - LANES]
            patterns[2 * q + 1, LANES:, :] = value[SECOND : SECOND + LON_DEV - LANES]
            if q < 4:
                first = LANES + 16 * q
                size = min(16, LON_DEV - first)
                patterns[LAT_DEV - 1, first : first + size, :] = value[TAIL : TAIL + size]


def root_and_patterns(packed, anomaly):
    return pl.pallas_call(
        root_kernel,
        out_shape=(
            jax.ShapeDtypeStruct((LAT_DEV, LON_DEV, MONTHS), jnp.bfloat16),
            jax.ShapeDtypeStruct((MONTHS, MONTHS), jnp.float32),
        ),
        in_specs=[pl.BlockSpec(memory_space=pltpu.VMEM)] * 2,
        out_specs=(pl.BlockSpec(memory_space=pltpu.VMEM),) * 2,
        scratch_shapes=[pltpu.VMEM((MONTHS, MONTHS), jnp.bfloat16)] * 10,
        compiler_params=pltpu.CompilerParams(vmem_limit_bytes=VMEM_LIMIT),
        name="root_and_patterns",
    )(packed, anomaly)


def exchange(pieces):
    return lax.all_to_all(pieces, BOTH, split_axis=0, concat_axis=0, tiled=True)


def exchange_packed(packed):
    pieces = packed.reshape(N_LON * N_LAT, PACK // 2, 2, LANES)
    return exchange(pieces).reshape(packed.shape)


def local(monthly_field, half_width, land_mask):
    widths = lax.all_gather(half_width, "lat", axis=0, tiled=True)
    landed = exchange(smooth(widths, monthly_field))
    row_index = lax.axis_index("lat") * LAT_DEV + jnp.arange(LAT_DEV)
    latitude = math.pi * ((row_index.astype(jnp.float32) + 0.5) / NLAT - 0.5)
    weight = jnp.sqrt(jnp.cos(latitude))[:, None] * land_mask.astype(jnp.float32)
    weight = jnp.pad(weight, ((0, 0), (0, 2 * LANES - LON_DEV)))
    packed, anomaly = gram_terms(landed, weight)
    packed = exchange_packed(packed)
    packed = exchange_packed(add_terms(packed))
    patterns, whitener = root_and_patterns(packed, anomaly)
    return (jnp.transpose(patterns, (2, 0, 1)), whitener)


def solution(mesh):
    placed = (P(("lon", "lat"), None, None), P("lat"), P("lat", "lon"))
    return jax.shard_map(
        local, mesh=mesh, in_specs=placed, out_specs=(P(None, "lat", "lon"), P()), check_vma=False
    )
```

time: 386 us -> 172 us (0.45); the launches traced: 378 us -> 172 us
  waiting for transfers between devices: 192 us -> 37.8 us
  Pallas kernels: 0 us -> 64.6 us
  matrix products: 52.4 us -> 0 us
  local copies, waits for them, and re-layouts: 36 us -> 4.35 us
  between operations: 15.6 us -> 1.33 us
  other arithmetic: 10.5 us -> 0.12 us
  blocking collectives: 60.9 us -> 53.8 us
    psum x1 -> x0, waiting for transfers between devices: 144 us -> none  [local(): gram = lax.psum(partial_gram, ('lon', 'lat'))]
    pallas_call x0 -> x4, Pallas kernels: none -> 64.6 us  [the longest x1 32.1 us: smooth(): pl.pallas_call(smooth_kernel, out_shape=jax.ShapeDtypeStruct((N_LON * N_L...]
    dot_general x27 -> x0, matrix products: 52.4 us -> none  [the longest x8 15.5 us: replicated_root(): jnp.dot(iterate_z, iterate_y, precision=lax.Precision.HIGHEST)]
    ppermute x4 -> x0, waiting for transfers between devices: 47.7 us -> none  [the longest x2 25.4 us: extended(): after = lax.ppermute(leading, axis, down)]
    all_to_all x0 -> x1, waiting for transfers between devices: none -> 37.8 us  [exchange(): return lax.all_to_all(pieces, BOTH, split_axis=0, concat_axis=0, tiled=True)]
    reshape x6 -> x0, local copies, waits for them, and re-layouts: 29.3 us -> none  [the longest x2 13.9 us: regroup(): months_block.reshape(month_count, n_lat, lat_dev, n_lon, lon_dev)]
    all_to_all x1 -> x2, blocking collectives: 60.9 us -> 40.7 us  [exchange(): return lax.all_to_all(pieces, BOTH, split_axis=0, concat_axis=0, tiled=True)]
    unnamed x0 -> x1, blocking collectives: none -> 13.1 us
  transfers between devices with their start and end apart: 5 -> 1, of which waited for: 5 -> 1; matrix products, arithmetic and copies ran while one was open for 1% -> 0% of each run, Pallas kernels for 0% -> 0%
where the time goes in v1:
time: 172 us
  Pallas kernels  64.6 us (38%)
  blocking collectives  53.8 us (31%)
  waiting for transfers between devices  37.8 us (22%)
  starting transfers between devices  9.86 us (6%)
  local copies, waits for them, and re-layouts  4.35 us (3%)
    all_to_all x2, blocking collectives, exchange(): return lax.all_to_all(pieces, BOTH, split_axis=0, concat_axis=0, tiled=True)  40.7 us
    all_to_all x1, waiting for transfers between devices, exchange(): return lax.all_to_all(pieces, BOTH, split_axis=0, concat_axis=0, tiled=True)  37.8 us
    pallas_call x1, Pallas kernels, smooth(): pl.pallas_call(smooth_kernel, out_shape=jax.ShapeDtypeStruct((N_LON * N_L...  32.1 us
    pallas_call x1, Pallas kernels, root_and_patterns(): pl.pallas_call(root_kernel, out_shape=(jax.ShapeDtypeStruct((LAT_DEV, LON...  25.2 us
    unnamed x1, blocking collectives  13.1 us
    all_to_all x1, starting transfers between devices, exchange(): return lax.all_to_all(pieces, BOTH, split_axis=0, concat_axis=0, tiled=True)  9.86 us
    pallas_call x1, Pallas kernels, gram_terms(): pl.pallas_call(gram_kernel, out_shape=(jax.ShapeDtypeStruct((LANES * PACK...  5.31 us
    unnamed x7, local copies, waits for them, and re-layouts  3.74 us
  transfers between devices with their start and end apart: 1, of which 1 were waited for; matrix products, arithmetic and copies ran while one was open for 0% of the time, Pallas kernels for 0%

profile of v1, /device:TPU:1, one launch (start us, length us, event | category | flops | bytes accessed | tf_op | source)
XLA Modules:
  0.0 171.8 jit_solution(11567603750816953137)
XLA Ops:
  0.6 1.2 dynamic-slice
  2.5 0.9 dynamic-update-slice
  3.4 13.1 %all-reduce.1.widths = s32[240]{0:T(256)} all-reduce(s32[240]{0:T(256)S(1)} %dynamic-update-slice), channel_id=1, replica_groups=mesh['lon'=8,'lat'=16] {'lat'}, use_global_device_ids=true, to_apply=%add.1 | all-reduce | flops 240 | bytes 1920
  16.5 32.1 %smooth.1 = bf16[128,88,128]{2,1,0:T(8,128)(2,1)} custom-call(s32[240]{0:T(256)} %all-reduce.1.widths, bf16[4,240,1440]{2,1,0:T(8,128)(2,1)} %field.1), custom_call_target="tpu_custom_call" | custom-call | tf_op jit(solution)/shard_map/smooth/pallas_call | solution.py:133
  48.6 0.0 copy-start.1
  48.6 9.9 %all-to-all-start = ((bf16[128,88,128]{2,1,0:T(8,128)(2,1)}), bf16[128,88,128]{2,1,0:T(8,128)(2,1)S(1)}, u32[]{:S(2)}, u32[]{:S(2)}) async-start(bf16[128,88,128]{2,1,0:T(8,128)(2,1)} %smooth.1), calls=%async_computation | async-start | bytes 5767168 | tf_op jit(solution)/shard_map/all_to_all | solution.py:337
  58.5 0.1 cosine_sqrt_fusion
  58.5 0.0 copy-done.1
  58.5 0.1 convert_multiply_fusion
  58.6 0.6 pad.4.weight
  59.2 37.8 %all-to-all-done.landed = bf16[128,88,128]{2,1,0:T(8,128)(2,1)S(1)} async-done(((bf16[128,88,128]{2,1,0:T(8,128)(2,1)}), bf16[128,88,128]{2,1,0:T(8,128)(2,1)S(1)}, u32[]{:S(2)}, u32[]{:S(2)}) %all-to-all-start) | async-done | bytes 2883616 | tf_op jit(solution)/shard_map/all_to_all | solution.py:337
  97.0 0.0 copy-start
  97.0 1.6 copy-done
  98.6 5.3 %gram_terms.1 = (f32[1280,128]{1,0:T(8,128)}, bf16[512,2816]{1,0:T(8,128)(2,1)}) custom-call(bf16[128,88,128]{2,1,0:T(8,128)(2,1)} %copy-done, f32[15,256]{1,0:T(8,128)} %pad.4.weight), custom_call_target="tpu_custom_call" | custom-call | tf_op jit(solution)/shard_map/gram_terms/pallas_call | solution.py:188
  103.9 20.2 %all_to_all.15 = f32[128,5,2,128]{3,2,1,0:T(2,128)} all-to-all(f32[128,5,2,128]{3,2,1,0:T(2,128)} %bitcast.9), channel_id=1, replica_groups=mesh['lon'=8,'lat'=16] {'lon','lat'}, dimensions={0} | all-to-all | bytes 1310720 | tf_op jit(solution)/shard_map/all_to_all | solution.py:337
  124.1 2.0 %add_terms.1 = f32[1280,128]{1,0:T(8,128)} custom-call(f32[1280,128]{1,0:T(8,128)} %bitcast.7), custom_call_target="tpu_custom_call" | custom-call | tf_op jit(solution)/shard_map/add_terms/pallas_call | solution.py:214
  126.2 20.5 %all_to_all.16 = f32[128,5,2,128]{3,2,1,0:T(2,128)} all-to-all(f32[128,5,2,128]{3,2,1,0:T(2,128)} %bitcast.8), channel_id=1, replica_groups=mesh['lon'=8,'lat'=16] {'lon','lat'}, dimensions={0} | all-to-all | bytes 1310720 | tf_op jit(solution)/shard_map/all_to_all | solution.py:337
  146.6 25.2 %root_and_patterns.1 = (bf16[15,180,512]{2,1,0:T(8,128)(2,1)}, f32[512,512]{1,0:T(8,128)}) custom-call(f32[1280,128]{1,0:T(8,128)} %bitcast.6, bf16[512,2816]{1,0:T(8,128)(2,1)} %get-tuple-element.7.anomaly), custom_call_target="tpu_custom_call" | custom-call | tf_op jit(solution)/shard_map/root_and_patterns/pallas_call | solution.py:322
  (1 shorter events, 0.0 us)
Async XLA Ops:
  48.6 9.9 %copy-start.1 = (s32[15,180]{1,0:T(8,128)S(1)}, s32[15,180]{1,0:T(8,128)}, u32[]{:S(2)}) copy-start(s32[15,180]{1,0:T(8,128)} %param.5) | copy-start | bytes 32404
  48.6 48.4 %all-to-all-start = ((bf16[128,88,128]{2,1,0:T(8,128)(2,1)}), bf16[128,88,128]{2,1,0:T(8,128)(2,1)S(1)}, u32[]{:S(2)}, u32[]{:S(2)}) async-start(bf16[128,88,128]{2,1,0:T(8,128)(2,1)} %smooth.1), calls=%async_computation | async-start | bytes 5767168 | tf_op jit(solution)/shard_map/all_to_all | solution.py:337
  97.0 1.6 copy-start

commit v2 on v1

v2 whole, which is shorter than its diff:
```python
import math

import jax
import jax.numpy as jnp
import numpy as np
from jax import lax
from jax.experimental import pallas as pl
from jax.experimental.pallas import tpu as pltpu
from jax.sharding import PartitionSpec as P

HMAX = 64
HL = 2
ITERS = 8
BOTH = ("lon", "lat")
N_LON = 8
N_LAT = 16
NLAT = 240
NLON = 1440
MONTHS = 512
MON_DEV = 4
LAT_DEV = 15
LON_DEV = 180
LANES = 128
GROUPS = 22
SECOND = 56
TAIL = 112
CHUNK = MON_DEV * GROUPS
WINDOWS = MON_DEV * N_LON
SROWS = 3 * WINDOWS
SSTRIDE = 97
VSTRIDE = 89
BLOCKS = [(i, j) for i in range(4) for j in range(i, 4)]
PACK = len(BLOCKS)
VMEM_LIMIT = 60 * 1024 * 1024


def lat_taps():
    offsets = np.arange(-HL, HL + 1).astype(np.float32)
    taps = np.exp(-(offsets * offsets) / np.float32(2.0)).astype(np.float32)
    taps = taps / taps.sum(dtype=np.float32)
    return [float(t) for t in taps.astype(jnp.bfloat16).astype(np.float32)]


def windows_kernel(field, out, staged):
    for m in range(MON_DEV):
        rows = field[m].astype(jnp.float32)
        ring = jnp.concatenate([rows, rows[:, :224]], axis=1)
        for l in range(N_LON):
            for j in range(3):
                start = LON_DEV * l - HMAX + LANES * j
                start = start + NLON if start < 0 else start
                piece = ring[:, start : start + LANES]
                for half in range(2):
                    first = half * 8 * SSTRIDE + j * WINDOWS + m * N_LON + l
                    staged[pl.ds(first, 8, stride=SSTRIDE), :] = piece[half * 8 : half * 8 + 8]
    for r in range(16):
        out[r] = staged[r * SSTRIDE : r * SSTRIDE + SROWS, :].astype(jnp.bfloat16)


def cut_windows(field):
    return pl.pallas_call(
        windows_kernel,
        grid=(NLAT // 16,),
        out_shape=jax.ShapeDtypeStruct((NLAT, SROWS, LANES), jnp.bfloat16),
        in_specs=[pl.BlockSpec((MON_DEV, 16, NLON), lambda i: (0, i, 0))],
        out_specs=pl.BlockSpec((16, SROWS, LANES), lambda i: (i, 0, 0)),
        scratch_shapes=[pltpu.VMEM((16 * SSTRIDE + 8, LANES), jnp.float32)],
        compiler_params=pltpu.CompilerParams(vmem_limit_bytes=VMEM_LIMIT),
        cost_estimate=pl.CostEstimate(flops=30000000, bytes_accessed=9000000, transcendentals=0),
        name="cut_windows",
    )(field)


def smooth_kernel(widths, windows, out, taps, passed, staged):
    b = pl.program_id(0)

    @pl.when(b == 0)
    def _():
        lane8 = lax.broadcasted_iota(jnp.int32, (8, LANES), 1)
        sub8 = lax.broadcasted_iota(jnp.int32, (8, LANES), 0)
        offset = (lane8 - HMAX).astype(jnp.float32)

        def build_taps(i, carry):
            reach = jnp.zeros((8, LANES), jnp.int32)
            for s in range(8):
                r = i * 8 + s
                reach = jnp.where(sub8 == s, widths[r // LAT_DEV, r % LAT_DEV], reach)
            reach = reach.astype(jnp.float32)
            spread = 0.5 * reach
            value = jnp.exp(-(offset * offset) / (2.0 * spread * spread))
            value = jnp.where(jnp.abs(offset) <= reach, value, 0.0)
            total = jnp.sum(value, axis=1, keepdims=True) + value[:, 0:1]
            value = (value / total).astype(jnp.bfloat16).astype(jnp.float32)
            taps[pl.ds(pl.multiple_of(i * 8, 8), 8), :] = value
            return carry

        lax.fori_loop(0, NLAT // 8, build_taps, 0, unroll=10)
        edge = jnp.zeros((HL, 2 * WINDOWS, LANES), jnp.float32)
        passed[0:HL] = edge
        passed[NLAT + HL : NLAT + 2 * HL] = edge

    @pl.when(b < N_LAT)
    def _():
        sub = lax.broadcasted_iota(jnp.int32, (LANES, LANES), 0)
        lane = lax.broadcasted_iota(jnp.int32, (LANES, LANES), 1)
        upper = jnp.where(sub >= lane, 1.0, 0.0).astype(jnp.bfloat16)
        lower = jnp.where(sub <= lane, 1.0, 0.0).astype(jnp.bfloat16)
        for rr in range(LAT_DEV):
            r = b * LAT_DEV + rr
            lhs = windows[rr]
            spread_taps = jnp.broadcast_to(taps[pl.ds(r, 1), :], (LANES, LANES))
            ring = pltpu.roll(spread_taps, 0, 1, stride=1, stride_axis=0).astype(jnp.bfloat16)
            left = jnp.concatenate([lhs[: 2 * WINDOWS], lhs[WINDOWS:]], axis=1)
            right = jnp.concatenate([ring * upper, ring * lower], axis=0)
            res = jnp.dot(left, right, preferred_element_type=jnp.float32)
            passed[r + HL] = res.astype(jnp.bfloat16).astype(jnp.float32)

    @pl.when(b > 0)
    def _():
        w0, w1, w2 = lat_taps()[:3]
        laneb = lax.broadcasted_iota(jnp.int32, (WINDOWS, LANES), 1)

        def smoothed(rr, lo, hi):
            r = (b - 1) * LAT_DEV + rr
            outer = passed[r, lo:hi] + passed[r + 4, lo:hi]
            inner = passed[r + 1, lo:hi] + passed[r + 3, lo:hi]
            return w0 * outer + w1 * inner + w2 * passed[r + 2, lo:hi]

        def put(g, value):
            for m in range(MON_DEV):
                staged[pl.ds(m * GROUPS + g, N_LON, stride=VSTRIDE), :] = value[8 * m : 8 * m + 8]

        for rr in range(LAT_DEV):
            put(rr, smoothed(rr, 0, WINDOWS))
        last = smoothed(LAT_DEV - 1, WINDOWS, 2 * WINDOWS)
        for q in range(7):
            even = smoothed(2 * q, WINDOWS, 2 * WINDOWS)
            odd = smoothed(2 * q + 1, WINDOWS, 2 * WINDOWS)
            value = jnp.where(laneb < SECOND, even, pltpu.roll(odd, SECOND, 1))
            if q < 4:
                tail = pltpu.roll(last, TAIL - 16 * q, 1)
                value = jnp.where(laneb < TAIL, value, tail)
            put(LAT_DEV + q, value)
        for l in range(N_LON):
            out[l, 0] = staged[l * VSTRIDE : l * VSTRIDE + CHUNK, :].astype(jnp.bfloat16)


def smooth(widths, windows):
    out = pl.pallas_call(
        smooth_kernel,
        grid=(N_LAT + 1,),
        out_shape=jax.ShapeDtypeStruct((N_LON, N_LAT, CHUNK, LANES), jnp.bfloat16),
        in_specs=[
            pl.BlockSpec(memory_space=pltpu.SMEM),
            pl.BlockSpec((LAT_DEV, SROWS, LANES), lambda b: (jnp.minimum(b, N_LAT - 1), 0, 0)),
        ],
        out_specs=pl.BlockSpec((N_LON, 1, CHUNK, LANES), lambda b: (0, jnp.maximum(b - 1, 0), 0, 0)),
        scratch_shapes=[
            pltpu.VMEM((NLAT, LANES), jnp.float32),
            pltpu.VMEM((NLAT + 2 * HL, 2 * WINDOWS, LANES), jnp.float32),
            pltpu.VMEM((N_LON * VSTRIDE + 8, LANES), jnp.float32),
        ],
        compiler_params=pltpu.CompilerParams(vmem_limit_bytes=VMEM_LIMIT),
        name="smooth",
    )(widths, windows)
    return out.reshape(N_LON * N_LAT, CHUNK, LANES)


def gram_kernel(landed_hbm, weight, packed, anomaly_hbm, landed, wide, anomaly, in_sems, out_sem):
    parts = 4
    size = N_LON * N_LAT // parts
    copies = [
        pltpu.make_async_copy(
            landed_hbm.at[k * size : (k + 1) * size], landed.at[k * size : (k + 1) * size], in_sems.at[k]
        )
        for k in range(parts)
    ]
    for copy in copies:
        copy.start()

    def widen(s, carry):
        wide[pl.ds(pl.multiple_of(s * CHUNK, 8), CHUNK), :] = landed[s].astype(jnp.float32)
        return carry

    for k in range(parts):
        copies[k].wait()
        lax.fori_loop(k * size, (k + 1) * size, widen, 0, unroll=4)
    lane = lax.broadcasted_iota(jnp.int32, (1, LANES), 1)
    for g in range(GROUPS):
        if g < LAT_DEV:
            scale = weight[g : g + 1, :LANES]
        else:
            q = g - LAT_DEV
            scale = weight[2 * q : 2 * q + 1, LANES:]
            scale = scale + pltpu.roll(weight[2 * q + 1 : 2 * q + 2, LANES:], SECOND, 1)
            if q < 4:
                last = weight[LAT_DEV - 1 : LAT_DEV, LANES:]
                last = jnp.where((lane >= 16 * q) & (lane < 16 * q + 16), last, 0.0)
                scale = scale + pltpu.roll(last, TAIL - 16 * q, 1)
        cells = wide[pl.ds(g, MONTHS, stride=GROUPS), :]
        mean = jnp.sum(cells, axis=0, keepdims=True) * (1.0 / MONTHS)
        anomaly[:, g * LANES : (g + 1) * LANES] = ((cells - mean) * scale).astype(jnp.bfloat16)
    store = pltpu.make_async_copy(anomaly, anomaly_hbm, out_sem)
    store.start()
    half = MONTHS // 2
    for i, j in ((0, 0), (0, 1), (1, 1)):
        block = lax.dot_general(
            anomaly[i * half : (i + 1) * half, :],
            anomaly[j * half : (j + 1) * half, :],
            (((1,), (1,)), ((), ())),
            preferred_element_type=jnp.float32,
        )
        for n, (bi, bj) in enumerate(BLOCKS):
            if bi // 2 == i and bj // 2 == j:
                a, c = (bi % 2) * LANES, (bj % 2) * LANES
                packed[pl.ds(n, LANES, stride=PACK), :] = block[a : a + LANES, c : c + LANES]
    store.wait()


def gram_terms(landed, weight):
    return pl.pallas_call(
        gram_kernel,
        out_shape=(
            jax.ShapeDtypeStruct((LANES * PACK, LANES), jnp.float32),
            jax.ShapeDtypeStruct((MONTHS, GROUPS * LANES), jnp.bfloat16),
        ),
        in_specs=[pl.BlockSpec(memory_space=pl.ANY), pl.BlockSpec(memory_space=pltpu.VMEM)],
        out_specs=(pl.BlockSpec(memory_space=pltpu.VMEM), pl.BlockSpec(memory_space=pl.ANY)),
        scratch_shapes=[
            pltpu.VMEM((N_LON * N_LAT, CHUNK, LANES), jnp.bfloat16),
            pltpu.VMEM((N_LON * N_LAT * CHUNK, LANES), jnp.float32),
            pltpu.VMEM((MONTHS, GROUPS * LANES), jnp.bfloat16),
            pltpu.SemaphoreType.DMA((4,)),
            pltpu.SemaphoreType.DMA,
        ],
        compiler_params=pltpu.CompilerParams(vmem_limit_bytes=32 * 1024 * 1024),
        name="gram_terms",
    )(landed, weight)


def add_kernel(terms, out):
    step = 4 * PACK
    total = terms[0:step, :]
    for s in range(1, LANES // 4):
        total = total + terms[s * step : (s + 1) * step, :]
    row = total[0:PACK] + total[PACK : 2 * PACK] + total[2 * PACK : 3 * PACK] + total[3 * PACK :]
    total = jnp.concatenate([row] * 4, axis=0)
    for s in range(LANES // 4):
        out[s * step : (s + 1) * step, :] = total


def add_terms(terms):
    return pl.pallas_call(
        add_kernel,
        out_shape=jax.ShapeDtypeStruct(terms.shape, jnp.float32),
        in_specs=[pl.BlockSpec(memory_space=pltpu.VMEM)],
        out_specs=pl.BlockSpec(memory_space=pltpu.VMEM),
        compiler_params=pltpu.CompilerParams(vmem_limit_bytes=8 * 1024 * 1024),
        name="add_terms",
    )(terms)


STEP = (2.25, -2.4375, 1.6875, -0.5625, 0.0625)
ROWB = 256
MIRROR = True


def root_kernel(packed, anomaly_hbm, patterns_hbm, whitener_hbm, anomaly, patterns, whitener, ws, hs, ps, ss, zs, wb, in_sem, out_sems):
    fetch = pltpu.make_async_copy(anomaly_hbm, anomaly, in_sem)
    fetch.start()
    for n, (bi, bj) in enumerate(BLOCKS):
        block = packed[pl.ds(n, LANES, stride=PACK), :]
        whitener[bi * LANES : (bi + 1) * LANES, bj * LANES : (bj + 1) * LANES] = block
        if bi != bj:
            whitener[bj * LANES : (bj + 1) * LANES, bi * LANES : (bi + 1) * LANES] = block.T
    gram = whitener[...]
    squares = jnp.sum(gram * gram, axis=0, keepdims=True)
    frobenius = jnp.sqrt(jnp.sum(squares, axis=1, keepdims=True) + 1e-06)
    final_scale = jnp.sqrt(float(NLAT * NLON) / frobenius)

    def split(ref, start, value):
        size = value.shape[0]
        high = value.astype(jnp.bfloat16)
        ref[start : start + size, :] = high
        ref[MONTHS + start : MONTHS + start + size, :] = (value - high.astype(jnp.float32)).astype(jnp.bfloat16)
        if ref.shape[0] == 3 * MONTHS:
            ref[2 * MONTHS + start : 2 * MONTHS + start + size, :] = high

    def join(ref, start):
        high = ref[start : start + ROWB, :].astype(jnp.float32)
        return high + ref[MONTHS + start : MONTHS + start + ROWB, :].astype(jnp.float32)

    def product(left, right):
        def rows(start):
            high = left[start : start + ROWB, :]
            low = left[MONTHS + start : MONTHS + start + ROWB, :]
            return jnp.concatenate([high, high, low], axis=1)

        upper = jnp.dot(rows(0), right[...], preferred_element_type=jnp.float32)
        if not MIRROR:
            return upper, jnp.dot(rows(ROWB), right[...], preferred_element_type=jnp.float32)
        corner = jnp.dot(rows(ROWB), right[:, ROWB:], preferred_element_type=jnp.float32)
        return upper, jnp.concatenate([upper[:, ROWB:].T, corner], axis=1)

    def plus_eye(value, start, scale):
        row = lax.broadcasted_iota(jnp.int32, value.shape, 0) + start
        column = lax.broadcasted_iota(jnp.int32, value.shape, 1)
        return jnp.where(row == column, value + scale, value)

    split(ws, 0, gram / frobenius)
    c0, c1, c2, c3, c4 = STEP
    last = ITERS // 2 - 1

    def double_step(k, carry):
        for n, square in enumerate(product(ws, ws)):
            start = n * ROWB
            split(ss, start, square)
            split(hs, start, plus_eye(c3 * join(ws, start) + c4 * square, start, c2))
        for n, value in enumerate(product(ss, hs)):
            start = n * ROWB
            split(ps, start, plus_eye(value + c1 * join(ws, start), start, c0))

        @pl.when(k == 0)
        def _():
            zs[...] = ps[0 : 2 * MONTHS, :]

        @pl.when(k > 0)
        def _():
            for n, value in enumerate(product(zs, ps)):
                split(zs, n * ROWB, value)
                whitener[n * ROWB : (n + 1) * ROWB, :] = value * final_scale

        @pl.when(k < last)
        def _():
            for n, value in enumerate(product(ws, ps)):
                split(ss, n * ROWB, value)
            for n, value in enumerate(product(ss, ps)):
                split(ws, n * ROWB, value)

        return carry

    lax.fori_loop(0, last + 1, double_step, 0)
    copies = [pltpu.make_async_copy(whitener, whitener_hbm, out_sems.at[LAT_DEV])]
    copies[0].start()
    wb[...] = whitener[...].astype(jnp.bfloat16)
    fetch.wait()

    def group(g):
        return lax.dot_general(
            anomaly[:, g * LANES : (g + 1) * LANES],
            wb[...],
            (((0,), (1,)), ((), ())),
            preferred_element_type=jnp.float32,
        ).astype(jnp.bfloat16)

    def finish(r):
        copy = pltpu.make_async_copy(patterns.at[r], patterns_hbm.at[r], out_sems.at[r])
        copy.start()
        copies.append(copy)

    for q in range(7):
        value = group(LAT_DEV + q)
        patterns[2 * q, LANES:, :] = value[0 : LON_DEV - LANES]
        patterns[2 * q + 1, LANES:, :] = value[SECOND : SECOND + LON_DEV - LANES]
        if q < 4:
            first = LANES + 16 * q
            size = min(16, LON_DEV - first)
            patterns[LAT_DEV - 1, first : first + size, :] = value[TAIL : TAIL + size]
        for r in (2 * q, 2 * q + 1):
            patterns[r, 0:LANES, :] = group(r)
            finish(r)
    patterns[LAT_DEV - 1, 0:LANES, :] = group(LAT_DEV - 1)
    finish(LAT_DEV - 1)
    for copy in copies:
        copy.wait()


def root_and_patterns(packed, anomaly):
    return pl.pallas_call(
        root_kernel,
        out_shape=(
            jax.ShapeDtypeStruct((LAT_DEV, LON_DEV, MONTHS), jnp.bfloat16),
            jax.ShapeDtypeStruct((MONTHS, MONTHS), jnp.float32),
        ),
        in_specs=[pl.BlockSpec(memory_space=pltpu.VMEM), pl.BlockSpec(memory_space=pl.ANY)],
        out_specs=(pl.BlockSpec(memory_space=pl.ANY),) * 2,
        scratch_shapes=[
            pltpu.VMEM((MONTHS, GROUPS * LANES), jnp.bfloat16),
            pltpu.VMEM((LAT_DEV, LON_DEV, MONTHS), jnp.bfloat16),
            pltpu.VMEM((MONTHS, MONTHS), jnp.float32),
            pltpu.VMEM((3 * MONTHS, MONTHS), jnp.bfloat16),
            pltpu.VMEM((3 * MONTHS, MONTHS), jnp.bfloat16),
            pltpu.VMEM((3 * MONTHS, MONTHS), jnp.bfloat16),
            pltpu.VMEM((2 * MONTHS, MONTHS), jnp.bfloat16),
            pltpu.VMEM((2 * MONTHS, MONTHS), jnp.bfloat16),
            pltpu.VMEM((MONTHS, MONTHS), jnp.bfloat16),
            pltpu.SemaphoreType.DMA,
            pltpu.SemaphoreType.DMA((LAT_DEV + 1,)),
        ],
        compiler_params=pltpu.CompilerParams(vmem_limit_bytes=32 * 1024 * 1024),
        name="root_and_patterns",
    )(packed, anomaly)


def exchange(pieces):
    return lax.all_to_all(pieces, BOTH, split_axis=0, concat_axis=0, tiled=True)


def exchange_packed(packed):
    pieces = packed.reshape(N_LON * N_LAT, PACK // 2, 2, LANES)
    return exchange(pieces).reshape(packed.shape)


def local(monthly_field, half_width, land_mask):
    widths = jnp.pad(half_width, (0, LANES - LAT_DEV))
    widths = jnp.broadcast_to(widths, (N_LAT, 1, LANES))
    widths = lax.all_to_all(widths, "lat", split_axis=0, concat_axis=0, tiled=True)
    windows = cut_windows(monthly_field)
    landed = exchange(smooth(widths.reshape(N_LAT, LANES), windows))
    row_index = lax.axis_index("lat") * LAT_DEV + jnp.arange(LAT_DEV)
    latitude = math.pi * ((row_index.astype(jnp.float32) + 0.5) / NLAT - 0.5)
    weight = jnp.sqrt(jnp.cos(latitude))[:, None] * land_mask.astype(jnp.float32)
    weight = jnp.pad(weight, ((0, 0), (0, 2 * LANES - LON_DEV)))
    packed, anomaly = gram_terms(landed, weight)
    packed = exchange_packed(packed)
    packed = exchange_packed(add_terms(packed))
    patterns, whitener = root_and_patterns(packed, anomaly)
    return (jnp.transpose(patterns, (2, 0, 1)), whitener)


def solution(mesh):
    placed = (P(("lon", "lat"), None, None), P("lat"), P("lat", "lon"))
    return jax.shard_map(
        local, mesh=mesh, in_specs=placed, out_specs=(P(None, "lat", "lon"), P()), check_vma=False
    )
```

time: 172 us -> 153 us (0.89)
  blocking collectives: 53.8 us -> 38.9 us
  Pallas kernels: 64.6 us -> 53.1 us
  starting transfers between devices: 9.86 us -> 18.7 us
  local copies, waits for them, and re-layouts: 4.35 us -> 1.88 us
    unnamed x1 -> x0, blocking collectives: 13.1 us -> none
    all_to_all x0 -> x1, starting transfers between devices: none -> 8.45 us  [local(): lax.all_to_all(widths, 'lat', split_axis=0, concat_axis=0, tiled=True)]
    pallas_call x1, Pallas kernels: 25.2 us -> 19.2 us  [root_and_patterns(): pl.pallas_call(root_kernel, out_shape=(jax.ShapeDtypeStruct((LAT_DEV, LON...]
    unnamed x7 -> x4, local copies, waits for them, and re-layouts: 3.74 us -> 0.6 us
    pallas_call x1 -> x2, Pallas kernels: 32.1 us -> 29.3 us  [the longest x1 16.5 us: smooth(): pl.pallas_call(smooth_kernel, grid=(N_LAT + 1,), out_shape=jax.ShapeDtype...]
    pallas_call x1, Pallas kernels: 2 us -> 0.08 us  [add_terms(): pl.pallas_call(add_kernel, out_shape=jax.ShapeDtypeStruct(terms.shape, jn...]
    all_to_all x2, blocking collectives: 40.7 us -> 38.9 us  [exchange(): return lax.all_to_all(pieces, BOTH, split_axis=0, concat_axis=0, tiled=True)]
  transfers between devices with their start and end apart: 1 -> 2, of which waited for: 1 -> 1; matrix products, arithmetic and copies ran while one was open for 0% -> 0% of each run, Pallas kernels for 0% -> 8%
where the time goes in v2:
time: 153 us; the launch traced here: 152 us
  Pallas kernels  53.1 us (35%)
  blocking collectives  38.9 us (25%)
  waiting for transfers between devices  38.4 us (25%)
  starting transfers between devices  18.7 us (12%)
  local copies, waits for them, and re-layouts  1.88 us (1%)
    all_to_all x2, blocking collectives, exchange(): return lax.all_to_all(pieces, BOTH, split_axis=0, concat_axis=0, tiled=True)  38.9 us
    all_to_all x1, waiting for transfers between devices, exchange(): return lax.all_to_all(pieces, BOTH, split_axis=0, concat_axis=0, tiled=True)  38.4 us
    pallas_call x1, Pallas kernels, root_and_patterns(): pl.pallas_call(root_kernel, out_shape=(jax.ShapeDtypeStruct((LAT_DEV, LON...  19.2 us
    pallas_call x1, Pallas kernels, smooth(): pl.pallas_call(smooth_kernel, grid=(N_LAT + 1,), out_shape=jax.ShapeDtype...  16.5 us
    pallas_call x1, Pallas kernels, cut_windows(): pl.pallas_call(windows_kernel, grid=(NLAT // 16,), out_shape=jax.ShapeDty...  12.8 us
    all_to_all x1, starting transfers between devices, exchange(): return lax.all_to_all(pieces, BOTH, split_axis=0, concat_axis=0, tiled=True)  10.3 us
    all_to_all x1, starting transfers between devices, local(): lax.all_to_all(widths, 'lat', split_axis=0, concat_axis=0, tiled=True)  8.45 us
    pallas_call x1, Pallas kernels, gram_terms(): pl.pallas_call(gram_kernel, out_shape=(jax.ShapeDtypeStruct((LANES * PACK...  4.5 us
  transfers between devices with their start and end apart: 2, of which 1 were waited for; matrix products, arithmetic and copies ran while one was open for 0% of the time, Pallas kernels for 8%

profile of v2, /device:TPU:1, one launch (start us, length us, event | category | flops | bytes accessed | tf_op | source)
XLA Modules:
  0.0 151.9 jit_solution(8791703787503958567)
XLA Ops:
  0.6 0.7 pad.8
  1.3 0.6 broadcast_in_dim.4
  1.9 8.4 %all-to-all-start = ((s32[16,1,128]{2,1,0:T(1,128)}), s32[16,1,128]{2,1,0:T(1,128)S(1)}, u32[]{:S(2)}, u32[]{:S(2)}) async-start(s32[16,1,128]{2,1,0:T(1,128)} %broadcast_in_dim.4), calls=%async_computation | async-start | bytes 16384 | tf_op jit(solution)/shard_map/all_to_all | solution.py:417
  10.3 12.8 %cut_windows.1.windows = bf16[240,96,128]{2,1,0:T(8,128)(2,1)} custom-call(bf16[4,240,1440]{2,1,0:T(8,128)(2,1)} %field.1), custom_call_target="tpu_custom_call" | custom-call | flops 30000000 | bytes 9000000 | tf_op jit(solution)/shard_map/cut_windows/pallas_call | solution.py:61
  23.1 0.0 all-to-all-done
  23.1 0.0 copy-start
  23.1 0.6 copy-done
  23.7 16.5 %smooth.1 = bf16[8,16,88,128]{3,2,1,0:T(8,128)(2,1)} custom-call(s32[16,128]{1,0:T(8,128)} %bitcast.12, bf16[240,96,128]{2,1,0:T(8,128)(2,1)} %cut_windows.1.windows), custom_call_target="tpu_custom_call" | custom-call | tf_op jit(solution)/shard_map/smooth/pallas_call | solution.py:149
  40.3 0.0 copy-start.1
  40.3 10.3 %all-to-all-start.1 = ((bf16[128,88,128]{2,1,0:T(8,128)(2,1)}), bf16[128,88,128]{2,1,0:T(8,128)(2,1)S(1)}, u32[]{:S(2)}, u32[]{:S(2)}) async-start(bf16[128,88,128]{2,1,0:T(8,128)(2,1)} %bitcast.11), calls=%async_computation.1 | async-start | bytes 5767168 | tf_op jit(solution)/shard_map/all_to_all | solution.py:406
  50.5 0.1 cosine_sqrt_fusion
  50.6 0.0 copy-done.1
  50.6 0.1 convert_multiply_fusion
  50.7 38.4 %all-to-all-done.1.landed_hbm = bf16[128,88,128]{2,1,0:T(8,128)(2,1)S(1)} async-done(((bf16[128,88,128]{2,1,0:T(8,128)(2,1)}), bf16[128,88,128]{2,1,0:T(8,128)(2,1)S(1)}, u32[]{:S(2)}, u32[]{:S(2)}) %all-to-all-start.1) | async-done | bytes 2883616 | tf_op jit(solution)/shard_map/all_to_all | solution.py:406
  89.0 4.5 %gram_terms.1 = (f32[1280,128]{1,0:T(8,128)S(1)}, bf16[512,2816]{1,0:T(8,128)(2,1)S(1)}) custom-call(bf16[128,88,128]{2,1,0:T(8,128)(2,1)S(1)} %all-to-all-done.1.landed_hbm, f32[15,256]{1,0:T(8,128)S(1)} %pad.9.weight), custom_call_target="tpu_custom_call" | custom-call | tf_op jit(solution)/shard_map/gram_terms/pallas_call | solution.py:221
  93.6 19.9 %all_to_all.20 = f32[128,5,2,128]{3,2,1,0:T(2,128)S(1)} all-to-all(f32[128,5,2,128]{3,2,1,0:T(2,128)S(1)} %bitcast.10), channel_id=1, replica_groups=mesh['lon'=8,'lat'=16] {'lon','lat'}, dimensions={0} | all-to-all | bytes 1310720 | tf_op jit(solution)/shard_map/all_to_all | solution.py:406
  113.5 0.1 add_terms.1
  113.6 19.0 %all_to_all.21 = f32[128,5,2,128]{3,2,1,0:T(2,128)S(1)} all-to-all(f32[128,5,2,128]{3,2,1,0:T(2,128)S(1)} %bitcast.9), channel_id=1, replica_groups=mesh['lon'=8,'lat'=16] {'lon','lat'}, dimensions={0} | all-to-all | bytes 1310720 | tf_op jit(solution)/shard_map/all_to_all | solution.py:406
  132.6 19.2 %root_and_patterns.1 = (bf16[15,180,512]{2,1,0:T(8,128)(2,1)}, f32[512,512]{1,0:T(8,128)}) custom-call(f32[1280,128]{1,0:T(8,128)S(1)} %bitcast.7, bf16[512,2816]{1,0:T(8,128)(2,1)S(1)} %get-tuple-element.7.anomaly_hbm), custom_call_target="tpu_custom_call" | custom-call | tf_op jit(solution)/shard_map/root_and_patterns/pallas_call | solution.py:379
  (1 shorter events, 0.0 us)
Async XLA Ops:
  1.9 21.2 %all-to-all-start = ((s32[16,1,128]{2,1,0:T(1,128)}), s32[16,1,128]{2,1,0:T(1,128)S(1)}, u32[]{:S(2)}, u32[]{:S(2)}) async-start(s32[16,1,128]{2,1,0:T(1,128)} %broadcast_in_dim.4), calls=%async_computation | async-start | bytes 16384 | tf_op jit(solution)/shard_map/all_to_all | solution.py:417
  23.1 0.6 copy-start
  40.3 10.3 %copy-start.1 = (s32[15,180]{1,0:T(8,128)S(1)}, s32[15,180]{1,0:T(8,128)}, u32[]{:S(2)}) copy-start(s32[15,180]{1,0:T(8,128)} %param.5) | copy-start | bytes 32404
  40.3 48.8 %all-to-all-start.1 = ((bf16[128,88,128]{2,1,0:T(8,128)(2,1)}), bf16[128,88,128]{2,1,0:T(8,128)(2,1)S(1)}, u32[]{:S(2)}, u32[]{:S(2)}) async-start(bf16[128,88,128]{2,1,0:T(8,128)(2,1)} %bitcast.11), calls=%async_computation.1 | async-start | bytes 5767168 | tf_op jit(solution)/shard_map/all_to_all | solution.py:406

commit v3 on v2

--- a/solution.py
+++ b/solution.py
@@ -1,3 +1,4 @@
+import functools
 import math
 
 import jax
@@ -29,6 +30,7 @@
 SROWS = 3 * WINDOWS
 SSTRIDE = 97
 VSTRIDE = 89
+FRONT = 8
 BLOCKS = [(i, j) for i in range(4) for j in range(i, 4)]
 PACK = len(BLOCKS)
 VMEM_LIMIT = 60 * 1024 * 1024
@@ -41,73 +43,118 @@
     return [float(t) for t in taps.astype(jnp.bfloat16).astype(np.float32)]
 
 
-def windows_kernel(field, out, staged):
-    for m in range(MON_DEV):
-        rows = field[m].astype(jnp.float32)
-        ring = jnp.concatenate([rows, rows[:, :224]], axis=1)
-        for l in range(N_LON):
-            for j in range(3):
-                start = LON_DEV * l - HMAX + LANES * j
-                start = start + NLON if start < 0 else start
-                piece = ring[:, start : start + LANES]
-                for half in range(2):
-                    first = half * 8 * SSTRIDE + j * WINDOWS + m * N_LON + l
-                    staged[pl.ds(first, 8, stride=SSTRIDE), :] = piece[half * 8 : half * 8 + 8]
-    for r in range(16):
-        out[r] = staged[r * SSTRIDE : r * SSTRIDE + SROWS, :].astype(jnp.bfloat16)
-
-
-def cut_windows(field):
+def windows_kernel(first_step, field_hbm, out_hbm, field, windows, staged, in_sems, out_sems):
+    steps = windows.shape[0] // 16
+
+    def fetch(i):
+        rows = pl.ds(pl.multiple_of(i * 16, 16), 16)
+        source = pl.ds(pl.multiple_of((first_step + i) * 16, 16), 16)
+        return pltpu.make_async_copy(field_hbm.at[:, source, :], field.at[:, rows, :], in_sems.at[i])
+
+    def store(i):
+        rows = pl.ds(pl.multiple_of(i * 16, 16), 16)
+        return pltpu.make_async_copy(windows.at[rows], out_hbm.at[rows], out_sems.at[i])
+
+    for i in range(steps):
+        fetch(i).start()
+
+    def step(i, carry):
+        fetch(i).wait()
+        for m in range(MON_DEV):
+            rows = field[m, pl.ds(pl.multiple_of(i * 16, 16), 16), :].astype(jnp.float32)
+            ring = jnp.concatenate([rows, rows[:, :224]], axis=1)
+            for l in range(N_LON):
+                for j in range(3):
+                    start = LON_DEV * l - HMAX + LANES * j
+                    start = start + NLON if start < 0 else start
+                    piece = ring[:, start : start + LANES]
+                    for half in range(2):
+                        first = half * 8 * SSTRIDE + j * WINDOWS + m * N_LON + l
+                        staged[pl.ds(first, 8, stride=SSTRIDE), :] = piece[half * 8 : half * 8 + 8]
+        for r in range(16):
+            windows[i * 16 + r] = staged[r * SSTRIDE : r * SSTRIDE + SROWS, :].astype(jnp.bfloat16)
+        store(i).start()
+        return carry
+
+    lax.fori_loop(0, steps, step, 0)
+    for i in range(steps):
+        store(i).wait()
+
+
+def cut_windows(field, first_step, steps):
     return pl.pallas_call(
-        windows_kernel,
-        grid=(NLAT // 16,),
-        out_shape=jax.ShapeDtypeStruct((NLAT, SROWS, LANES), jnp.bfloat16),
-        in_specs=[pl.BlockSpec((MON_DEV, 16, NLON), lambda i: (0, i, 0))],
-        out_specs=pl.BlockSpec((16, SROWS, LANES), lambda i: (i, 0, 0)),
-        scratch_shapes=[pltpu.VMEM((16 * SSTRIDE + 8, LANES), jnp.float32)],
+        functools.partial(windows_kernel, first_step),
+        out_shape=jax.ShapeDtypeStruct((steps * 16, SROWS, LANES), jnp.bfloat16),
+        in_specs=[pl.BlockSpec(memory_space=pl.ANY)],
+        out_specs=pl.BlockSpec(memory_space=pl.ANY),
+        scratch_shapes=[
+            pltpu.VMEM((MON_DEV, steps * 16, NLON), jnp.bfloat16),
+            pltpu.VMEM((steps * 16, SROWS, LANES), jnp.bfloat16),
+            pltpu.VMEM((16 * SSTRIDE + 8, LANES), jnp.float32),
+            pltpu.SemaphoreType.DMA((steps,)),
+            pltpu.SemaphoreType.DMA((steps,)),
+        ],
         compiler_params=pltpu.CompilerParams(vmem_limit_bytes=VMEM_LIMIT),
-        cost_estimate=pl.CostEstimate(flops=30000000, bytes_accessed=9000000, transcendentals=0),
+        cost_estimate=pl.CostEstimate(flops=3000000000, bytes_accessed=9000000, transcendentals=0),
         name="cut_windows",
     )(field)
 
 
-def smooth_kernel(widths, windows, out, taps, passed, staged):
-    b = pl.program_id(0)
-
-    @pl.when(b == 0)
-    def _():
-        lane8 = lax.broadcasted_iota(jnp.int32, (8, LANES), 1)
-        sub8 = lax.broadcasted_iota(jnp.int32, (8, LANES), 0)
-        offset = (lane8 - HMAX).astype(jnp.float32)
-
-        def build_taps(i, carry):
-            reach = jnp.zeros((8, LANES), jnp.int32)
-            for s in range(8):
-                r = i * 8 + s
-                reach = jnp.where(sub8 == s, widths[r // LAT_DEV, r % LAT_DEV], reach)
-            reach = reach.astype(jnp.float32)
-            spread = 0.5 * reach
-            value = jnp.exp(-(offset * offset) / (2.0 * spread * spread))
-            value = jnp.where(jnp.abs(offset) <= reach, value, 0.0)
-            total = jnp.sum(value, axis=1, keepdims=True) + value[:, 0:1]
-            value = (value / total).astype(jnp.bfloat16).astype(jnp.float32)
-            taps[pl.ds(pl.multiple_of(i * 8, 8), 8), :] = value
-            return carry
-
-        lax.fori_loop(0, NLAT // 8, build_taps, 0, unroll=10)
-        edge = jnp.zeros((HL, 2 * WINDOWS, LANES), jnp.float32)
-        passed[0:HL] = edge
-        passed[NLAT + HL : NLAT + 2 * HL] = edge
-
-    @pl.when(b < N_LAT)
-    def _():
-        sub = lax.broadcasted_iota(jnp.int32, (LANES, LANES), 0)
-        lane = lax.broadcasted_iota(jnp.int32, (LANES, LANES), 1)
-        upper = jnp.where(sub >= lane, 1.0, 0.0).astype(jnp.bfloat16)
-        lower = jnp.where(sub <= lane, 1.0, 0.0).astype(jnp.bfloat16)
+def smooth_kernel(chip, *refs):
+    quads, refs = refs[:4], refs[4:]
+    (front, back, out_hbm, windows, out, taps, passed, staged, widths, in_sems, out_sems) = refs
+
+    def fetch(i):
+        rows = pl.ds(i * 16, 16)
+        if i < FRONT:
+            return pltpu.make_async_copy(front.at[rows], windows.at[rows], in_sems.at[i])
+        return pltpu.make_async_copy(back.at[pl.ds((i - FRONT) * 16, 16)], windows.at[rows], in_sems.at[i])
+
+    def arrived(i):
+        rows = pl.ds(pl.multiple_of(i * 16, 16), 16)
+        pltpu.make_async_copy(windows.at[rows], windows.at[rows], in_sems.at[i]).wait()
+
+    def store(b):
+        return pltpu.make_async_copy(out.at[:, b], out_hbm.at[:, b], out_sems.at[b])
+
+    for i in range(NLAT // 16):
+        fetch(i).start()
+    for k in range(4):
+        for j in range(4):
+            first = ((k ^ chip[0]) * 4 + j) * LAT_DEV
+            for rr in range(LAT_DEV):
+                widths[first + rr] = quads[k][j, rr]
+    lane8 = lax.broadcasted_iota(jnp.int32, (8, LANES), 1)
+    sub8 = lax.broadcasted_iota(jnp.int32, (8, LANES), 0)
+    offset = (lane8 - HMAX).astype(jnp.float32)
+
+    def build_taps(i, carry):
+        reach = jnp.zeros((8, LANES), jnp.int32)
+        for s in range(8):
+            r = i * 8 + s
+            reach = jnp.where(sub8 == s, widths[r], reach)
+        reach = reach.astype(jnp.float32)
+        spread = 0.5 * reach
+        value = jnp.exp(-(offset * offset) / (2.0 * spread * spread))
+        value = jnp.where(jnp.abs(offset) <= reach, value, 0.0)
+        total = jnp.sum(value, axis=1, keepdims=True) + value[:, 0:1]
+        value = (value / total).astype(jnp.bfloat16).astype(jnp.float32)
+        taps[pl.ds(pl.multiple_of(i * 8, 8), 8), :] = value
+        return carry
+
+    lax.fori_loop(0, NLAT // 8, build_taps, 0, unroll=10)
+    edge = jnp.zeros((HL, 2 * WINDOWS, LANES), jnp.float32)
+    passed[0:HL] = edge
+    passed[NLAT + HL : NLAT + 2 * HL] = edge
+    sub = lax.broadcasted_iota(jnp.int32, (LANES, LANES), 0)
+    lane = lax.broadcasted_iota(jnp.int32, (LANES, LANES), 1)
+    upper = jnp.where(sub >= lane, 1.0, 0.0).astype(jnp.bfloat16)
+    lower = jnp.where(sub <= lane, 1.0, 0.0).astype(jnp.bfloat16)
+
+    def lon_band(b):
         for rr in range(LAT_DEV):
             r = b * LAT_DEV + rr
-            lhs = windows[rr]
+            lhs = windows[r]
             spread_taps = jnp.broadcast_to(taps[pl.ds(r, 1), :], (LANES, LANES))
             ring = pltpu.roll(spread_taps, 0, 1, stride=1, stride_axis=0).astype(jnp.bfloat16)
             left = jnp.concatenate([lhs[: 2 * WINDOWS], lhs[WINDOWS:]], axis=1)
@@ -115,13 +162,12 @@
             res = jnp.dot(left, right, preferred_element_type=jnp.float32)
             passed[r + HL] = res.astype(jnp.bfloat16).astype(jnp.float32)
 
-    @pl.when(b > 0)
-    def _():
-        w0, w1, w2 = lat_taps()[:3]
-        laneb = lax.broadcasted_iota(jnp.int32, (WINDOWS, LANES), 1)
-
+    w0, w1, w2 = lat_taps()[:3]
+    laneb = lax.broadcasted_iota(jnp.int32, (WINDOWS, LANES), 1)
+
+    def lat_band(b):
         def smoothed(rr, lo, hi):
-            r = (b - 1) * LAT_DEV + rr
+            r = b * LAT_DEV + rr
             outer = passed[r, lo:hi] + passed[r + 4, lo:hi]
             inner = passed[r + 1, lo:hi] + passed[r + 3, lo:hi]
             return w0 * outer + w1 * inner + w2 * passed[r + 2, lo:hi]
@@ -142,27 +188,46 @@
                 value = jnp.where(laneb < TAIL, value, tail)
             put(LAT_DEV + q, value)
         for l in range(N_LON):
-            out[l, 0] = staged[l * VSTRIDE : l * VSTRIDE + CHUNK, :].astype(jnp.bfloat16)
-
-
-def smooth(widths, windows):
+            out[l, b] = staged[l * VSTRIDE : l * VSTRIDE + CHUNK, :].astype(jnp.bfloat16)
+
+    arrived(0)
+    lon_band(0)
+
+    def band(b, carry):
+        arrived(b)
+        lon_band(b)
+        lat_band(b - 1)
+        store(b - 1).start()
+        return carry
+
+    lax.fori_loop(1, N_LAT - 1, band, 0)
+    lon_band(N_LAT - 1)
+    for b in (N_LAT - 2, N_LAT - 1):
+        lat_band(b)
+        store(b).start()
+    for b in range(N_LAT):
+        store(b).wait()
+
+
+def smooth(chip, quads, front, back):
     out = pl.pallas_call(
         smooth_kernel,
-        grid=(N_LAT + 1,),
         out_shape=jax.ShapeDtypeStruct((N_LON, N_LAT, CHUNK, LANES), jnp.bfloat16),
-        in_specs=[
-            pl.BlockSpec(memory_space=pltpu.SMEM),
-            pl.BlockSpec((LAT_DEV, SROWS, LANES), lambda b: (jnp.minimum(b, N_LAT - 1), 0, 0)),
-        ],
-        out_specs=pl.BlockSpec((N_LON, 1, CHUNK, LANES), lambda b: (0, jnp.maximum(b - 1, 0), 0, 0)),
+        in_specs=[pl.BlockSpec(memory_space=pltpu.SMEM)] * 5 + [pl.BlockSpec(memory_space=pl.ANY)] * 2,
+        out_specs=pl.BlockSpec(memory_space=pl.ANY),
         scratch_shapes=[
+            pltpu.VMEM((NLAT, SROWS, LANES), jnp.bfloat16),
+            pltpu.VMEM((N_LON, N_LAT, CHUNK, LANES), jnp.bfloat16),
             pltpu.VMEM((NLAT, LANES), jnp.float32),
             pltpu.VMEM((NLAT + 2 * HL, 2 * WINDOWS, LANES), jnp.float32),
             pltpu.VMEM((N_LON * VSTRIDE + 8, LANES), jnp.float32),
+            pltpu.SMEM((NLAT,), jnp.int32),
+            pltpu.SemaphoreType.DMA((NLAT // 16,)),
+            pltpu.SemaphoreType.DMA((N_LAT,)),
         ],
         compiler_params=pltpu.CompilerParams(vmem_limit_bytes=VMEM_LIMIT),
         name="smooth",
-    )(widths, windows)
+    )(chip, *quads, front, back)
     return out.reshape(N_LON * N_LAT, CHUNK, LANES)
 
 
@@ -411,12 +476,29 @@
     return exchange(pieces).reshape(packed.shape)
 
 
+def swap(x, k):
+    return lax.ppermute(x, "lat", [(i, i ^ k) for i in range(N_LAT)])
+
+
+def gather_widths(half_width):
+    own = jnp.pad(half_width, (0, LANES - LAT_DEV)).reshape(1, LANES)
+    rows = [own] + [swap(own, k) for k in (1, 2, 3)]
+    place = lax.axis_index("lat") & 3
+    at = jnp.arange(4, dtype=jnp.int32).reshape(4, 1)
+    quad = jnp.zeros((4, LANES), jnp.int32)
+    for k in range(4):
+        quad = jnp.where(at == (place ^ k), rows[k], quad)
+    return quad
+
+
 def local(monthly_field, half_width, land_mask):
-    widths = jnp.pad(half_width, (0, LANES - LAT_DEV))
-    widths = jnp.broadcast_to(widths, (N_LAT, 1, LANES))
-    widths = lax.all_to_all(widths, "lat", split_axis=0, concat_axis=0, tiled=True)
-    windows = cut_windows(monthly_field)
-    landed = exchange(smooth(widths.reshape(N_LAT, LANES), windows))
+    quad = gather_widths(half_width)
+    front = cut_windows(monthly_field, 0, FRONT)
+    field, quad = lax.optimization_barrier((monthly_field, quad))
+    quads = [quad] + [swap(quad, 4 * k) for k in (1, 2, 3)]
+    back = cut_windows(field, FRONT, NLAT // 16 - FRONT)
+    chip = (lax.axis_index("lat") >> 2).reshape(1)
+    landed = exchange(smooth(chip, quads, front, back))
     row_index = lax.axis_index("lat") * LAT_DEV + jnp.arange(LAT_DEV)
     latitude = math.pi * ((row_index.astype(jnp.float32) + 0.5) / NLAT - 0.5)
     weight = jnp.sqrt(jnp.cos(latitude))[:, None] * land_mask.astype(jnp.float32)

time: 153 us -> 144 us (0.941)
  Pallas kernels: 53.1 us -> 44.8 us
    ppermute x0 -> x6, starting transfers between devices: none -> 8.51 us  [swap(): return lax.ppermute(x, 'lat', [(i, i ^ k) for i in range(N_LAT)])]
    all_to_all x1 -> x0, starting transfers between devices: 8.45 us -> none  [local(): lax.all_to_all(widths, 'lat', split_axis=0, concat_axis=0, tiled=True)]
    pallas_call x2 -> x3, Pallas kernels: 29.3 us -> 21 us  [the longest x1 11 us: smooth(): pl.pallas_call(smooth_kernel, out_shape=jax.ShapeDtypeStruct((N_LON, N_LA...]
  transfers between devices with their start and end apart: 2 -> 7, of which waited for: 1 -> 1; matrix products, arithmetic and copies ran while one was open for 0% -> 0% of each run, Pallas kernels for 8% -> 7%
where the time goes in v3:
time: 144 us
  Pallas kernels  44.8 us (31%)
  blocking collectives  38.9 us (27%)
  waiting for transfers between devices  38.4 us (27%)
  starting transfers between devices  19.4 us (13%)
    all_to_all x2, blocking collectives, exchange(): return lax.all_to_all(pieces, BOTH, split_axis=0, concat_axis=0, tiled=True)  38.9 us
    all_to_all x1, waiting for transfers between devices, exchange(): return lax.all_to_all(pieces, BOTH, split_axis=0, concat_axis=0, tiled=True)  38.4 us
    pallas_call x1, Pallas kernels, root_and_patterns(): pl.pallas_call(root_kernel, out_shape=(jax.ShapeDtypeStruct((LAT_DEV, LON...  19.2 us
    pallas_call x1, Pallas kernels, smooth(): pl.pallas_call(smooth_kernel, out_shape=jax.ShapeDtypeStruct((N_LON, N_LA...  11 us
    all_to_all x1, starting transfers between devices, exchange(): return lax.all_to_all(pieces, BOTH, split_axis=0, concat_axis=0, tiled=True)  10.9 us
    pallas_call x2, Pallas kernels, cut_windows(): pl.pallas_call(functools.partial(windows_kernel, first_step), out_shape=j...  10 us
    ppermute x6, starting transfers between devices, swap(): return lax.ppermute(x, 'lat', [(i, i ^ k) for i in range(N_LAT)])  8.51 us
    pallas_call x1, Pallas kernels, gram_terms(): pl.pallas_call(gram_kernel, out_shape=(jax.ShapeDtypeStruct((LANES * PACK...  4.49 us
  transfers between devices with their start and end apart: 7, of which 1 were waited for; matrix products, arithmetic and copies ran while one was open for 0% of the time, Pallas kernels for 7%

profile of v3, /device:TPU:1, one launch (start us, length us, event | category | flops | bytes accessed | tf_op | source)
XLA Modules:
  0.0 144.0 jit_solution(12222946643022170373)
XLA Ops:
  0.6 0.7 pad_bitcast_fusion
  1.3 4.1 %collective-permute-start = (s32[1,128]{1,0:T(1,128)S(1)}, s32[1,128]{1,0:T(1,128)S(1)}, u32[]{:S(2)}, u32[]{:S(2)}) collective-permute-start(s32[1,128]{1,0:T(1,128)S(1)} %get-tuple-element.14), channel_id=1, source_target_pairs={{0,3},{1,2},{2,1},{3,0},{4,7},{5,6},{6,5},{7,4},{8,11},{9,10},{10,... | collective-permute-start | bytes 1544 | tf_op jit(solution)/shard_map/ppermute | solution.py:480
  5.4 0.1 collective-permute-start.1
  5.6 0.3 collective-permute-start.2
  5.9 5.2 %cut_windows.2.refs_4_ = bf16[128,96,128]{2,1,0:T(8,128)(2,1)} custom-call(bf16[4,240,1440]{2,1,0:T(8,128)(2,1)} %field_hbm.2), custom_call_target="tpu_custom_call" | custom-call | flops 3000000000 | bytes 9000000 | tf_op jit(solution)/shard_map/cut_windows/pallas_call | solution.py:85
  11.1 0.0 collective-permute-done
  11.1 0.0 collective-permute-done.1
  11.1 0.0 collective-permute-done.2
  11.2 0.1 select_select_fusion.refs_0_
  11.2 1.3 collective-permute-start.3
  12.6 2.6 %collective-permute-start.4 = (s32[4,128]{1,0:T(4,128)S(1)}, s32[4,128]{1,0:T(4,128)S(1)}, u32[]{:S(2)}, u32[]{:S(2)}) collective-permute-start(s32[4,128]{1,0:T(4,128)S(1)} %select_select_fusion.refs_0_), channel_id=1, source_target_pairs={{0,8},{1,9},{2,10},{3,11},{4,12},{5,13},{6,14},{7,15},{8,0},{9,1},... | collective-permute-start | bytes 6152 | tf_op jit(solution)/shard_map/ppermute | solution.py:480
  15.2 0.0 collective-permute-start.5
  15.2 4.8 %cut_windows.3.refs_5_ = bf16[112,96,128]{2,1,0:T(8,128)(2,1)} custom-call(bf16[4,240,1440]{2,1,0:T(8,128)(2,1)} %field_hbm.2), custom_call_target="tpu_custom_call" | custom-call | flops 3000000000 | bytes 9000000 | tf_op jit(solution)/shard_map/cut_windows/pallas_call | solution.py:85
  20.0 0.0 copy-done.1
  20.0 0.0 collective-permute-done.3.refs_1_
  20.0 0.0 copy-start.2
  20.0 0.0 collective-permute-done.4.refs_2_
  20.0 0.0 collective-permute-done.5.refs_3_
  20.1 0.5 copy-done.2
  20.6 0.0 copy-done.3
  20.6 0.0 copy-done.4
  20.6 11.0 %smooth.1 = bf16[8,16,88,128]{3,2,1,0:T(8,128)(2,1)} custom-call(s32[1]{0:T(128)} %bitcast.chip, s32[4,128]{1,0:T(4,128)} %copy-done.1, s32[4,128]{1,0:T(4,128)} %copy-done.2, s32[4,128]{1,0:T(4,128)} %copy-done.3, s32[4,128]{1,0:T(4,128)} %copy-done.4, bf16[128,96,128]{2,1,0:T(8,128)(2,1)} %cut_windows.2.refs_4_, bf16[112,96,128]{2,1,0:T(8,128)(2,1)} %cut_windows.3.refs_5_), custom_call_target="tpu_custom_call" | custom-call | tf_op jit(solution)/shard_map/smooth/pallas_call | solution.py:213
  31.7 0.0 copy-start
  31.7 10.9 %all-to-all-start = ((bf16[128,88,128]{2,1,0:T(8,128)(2,1)}), bf16[128,88,128]{2,1,0:T(8,128)(2,1)S(1)}, u32[]{:S(2)}, u32[]{:S(2)}) async-start(bf16[128,88,128]{2,1,0:T(8,128)(2,1)} %bitcast.16), calls=%async_computation | async-start | bytes 5767168 | tf_op jit(solution)/shard_map/all_to_all | solution.py:471
  42.6 0.1 cosine_sqrt_fusion
  42.7 0.1 convert_multiply_fusion
  42.7 38.4 %all-to-all-done.landed_hbm = bf16[128,88,128]{2,1,0:T(8,128)(2,1)S(1)} async-done(((bf16[128,88,128]{2,1,0:T(8,128)(2,1)}), bf16[128,88,128]{2,1,0:T(8,128)(2,1)S(1)}, u32[]{:S(2)}, u32[]{:S(2)}) %all-to-all-start) | async-done | bytes 2883616 | tf_op jit(solution)/shard_map/all_to_all | solution.py:471
  81.1 4.5 %gram_terms.1 = (f32[1280,128]{1,0:T(8,128)S(1)}, bf16[512,2816]{1,0:T(8,128)(2,1)S(1)}) custom-call(bf16[128,88,128]{2,1,0:T(8,128)(2,1)S(1)} %all-to-all-done.landed_hbm, f32[15,256]{1,0:T(8,128)S(1)} %pad.9.weight), custom_call_target="tpu_custom_call" | custom-call | tf_op jit(solution)/shard_map/gram_terms/pallas_call | solution.py:286
  85.6 19.9 %all_to_all.15 = f32[128,5,2,128]{3,2,1,0:T(2,128)S(1)} all-to-all(f32[128,5,2,128]{3,2,1,0:T(2,128)S(1)} %bitcast.15), channel_id=1, replica_groups=mesh['lon'=8,'lat'=16] {'lon','lat'}, dimensions={0} | all-to-all | bytes 1310720 | tf_op jit(solution)/shard_map/all_to_all | solution.py:471
  105.5 0.1 add_terms.1
  105.6 19.0 %all_to_all.16 = f32[128,5,2,128]{3,2,1,0:T(2,128)S(1)} all-to-all(f32[128,5,2,128]{3,2,1,0:T(2,128)S(1)} %bitcast.14), channel_id=1, replica_groups=mesh['lon'=8,'lat'=16] {'lon','lat'}, dimensions={0} | all-to-all | bytes 1310720 | tf_op jit(solution)/shard_map/all_to_all | solution.py:471
  124.6 19.2 %root_and_patterns.1 = (bf16[15,180,512]{2,1,0:T(8,128)(2,1)}, f32[512,512]{1,0:T(8,128)}) custom-call(f32[1280,128]{1,0:T(8,128)S(1)} %bitcast.12, bf16[512,2816]{1,0:T(8,128)(2,1)S(1)} %get-tuple-element.11.anomaly_hbm), custom_call_target="tpu_custom_call" | custom-call | tf_op jit(solution)/shard_map/root_and_patterns/pallas_call | solution.py:444
  (7 shorter events, 0.0 us)
Async XLA Ops:
  1.3 9.8 %collective-permute-start = (s32[1,128]{1,0:T(1,128)S(1)}, s32[1,128]{1,0:T(1,128)S(1)}, u32[]{:S(2)}, u32[]{:S(2)}) collective-permute-start(s32[1,128]{1,0:T(1,128)S(1)} %get-tuple-element.14), channel_id=1, source_target_pairs={{0,3},{1,2},{2,1},{3,0},{4,7},{5,6},{6,5},{7,4},{8,11},{9,10},{10,... | collective-permute-start | bytes 1544 | tf_op jit(solution)/shard_map/ppermute | solution.py:480
  5.4 5.7 %collective-permute-start.1 = (s32[1,128]{1,0:T(1,128)S(1)}, s32[1,128]{1,0:T(1,128)S(1)}, u32[]{:S(2)}, u32[]{:S(2)}) collective-permute-start(s32[1,128]{1,0:T(1,128)S(1)} %get-tuple-element.14), channel_id=1, source_target_pairs={{0,2},{1,3},{2,0},{3,1},{4,6},{5,7},{6,4},{7,5},{8,10},{9,11},{10,... | collective-permute-start | bytes 1544 | tf_op jit(solution)/shard_map/ppermute | solution.py:480
  5.6 5.6 %collective-permute-start.2 = (s32[1,128]{1,0:T(1,128)S(1)}, s32[1,128]{1,0:T(1,128)S(1)}, u32[]{:S(2)}, u32[]{:S(2)}) collective-permute-start(s32[1,128]{1,0:T(1,128)S(1)} %get-tuple-element.14), channel_id=1, source_target_pairs={{0,1},{1,0},{2,3},{3,2},{4,5},{5,4},{6,7},{7,6},{8,9},{9,8},{10,11... | collective-permute-start | bytes 1544 | tf_op jit(solution)/shard_map/ppermute | solution.py:480
  11.2 8.7 %copy-start.1 = (s32[4,128]{1,0:T(4,128)}, s32[4,128]{1,0:T(4,128)S(1)}, u32[]{:S(2)}) copy-start(s32[4,128]{1,0:T(4,128)S(1)} %select_select_fusion.refs_0_) | copy-start | bytes 6148
  11.2 8.8 %collective-permute-start.3 = (s32[4,128]{1,0:T(4,128)S(1)}, s32[4,128]{1,0:T(4,128)S(1)}, u32[]{:S(2)}, u32[]{:S(2)}) collective-permute-start(s32[4,128]{1,0:T(4,128)S(1)} %select_select_fusion.refs_0_), channel_id=1, source_target_pairs={{0,4},{1,5},{2,6},{3,7},{4,0},{5,1},{6,2},{7,3},{8,12},{9,13},{10,... | collective-permute-start | bytes 6152 | tf_op jit(solution)/shard_map/ppermute | solution.py:480
  12.6 7.4 %collective-permute-start.4 = (s32[4,128]{1,0:T(4,128)S(1)}, s32[4,128]{1,0:T(4,128)S(1)}, u32[]{:S(2)}, u32[]{:S(2)}) collective-permute-start(s32[4,128]{1,0:T(4,128)S(1)} %select_select_fusion.refs_0_), channel_id=1, source_target_pairs={{0,8},{1,9},{2,10},{3,11},{4,12},{5,13},{6,14},{7,15},{8,0},{9,1},... | collective-permute-start | bytes 6152 | tf_op jit(solution)/shard_map/ppermute | solution.py:480
  15.2 4.8 %collective-permute-start.5 = (s32[4,128]{1,0:T(4,128)S(1)}, s32[4,128]{1,0:T(4,128)S(1)}, u32[]{:S(2)}, u32[]{:S(2)}) collective-permute-start(s32[4,128]{1,0:T(4,128)S(1)} %select_select_fusion.refs_0_), channel_id=1, source_target_pairs={{0,12},{1,13},{2,14},{3,15},{4,8},{5,9},{6,10},{7,11},{8,4},{9,5},... | collective-permute-start | bytes 6152 | tf_op jit(solution)/shard_map/ppermute | solution.py:480
  20.0 0.6 copy-start.2
  20.0 0.6 copy-start.3
  20.0 0.6 copy-start.4
  31.7 11.0 %copy-start = (s32[15,180]{1,0:T(8,128)S(1)}, s32[15,180]{1,0:T(8,128)}, u32[]{:S(2)}) copy-start(s32[15,180]{1,0:T(8,128)} %param.5) | copy-start | bytes 32404
  31.7 49.4 %all-to-all-start = ((bf16[128,88,128]{2,1,0:T(8,128)(2,1)}), bf16[128,88,128]{2,1,0:T(8,128)(2,1)S(1)}, u32[]{:S(2)}, u32[]{:S(2)}) async-start(bf16[128,88,128]{2,1,0:T(8,128)(2,1)} %bitcast.16), calls=%async_computation | async-start | bytes 5767168 | tf_op jit(solution)/shard_map/all_to_all | solution.py:471

commit v4 on v3

--- a/solution.py
+++ b/solution.py
@@ -7,12 +7,16 @@
 from jax import lax
 from jax.experimental import pallas as pl
 from jax.experimental.pallas import tpu as pltpu
+from jax.sharding import Mesh
 from jax.sharding import PartitionSpec as P
 
 HMAX = 64
 HL = 2
 ITERS = 8
-BOTH = ("lon", "lat")
+LAT = ("chip", "core")
+BOTH = ("lon", "chip", "core")
+SAME_CORE = ("lon", "chip")
+HALF = 64
 N_LON = 8
 N_LAT = 16
 NLAT = 240
@@ -45,6 +49,7 @@
 
 def windows_kernel(first_step, field_hbm, out_hbm, field, windows, staged, in_sems, out_sems):
     steps = windows.shape[0] // 16
+    lane16 = lax.broadcasted_iota(jnp.int32, (16, LANES), 1)
 
     def fetch(i):
         rows = pl.ds(pl.multiple_of(i * 16, 16), 16)
@@ -61,13 +66,17 @@
     def step(i, carry):
         fetch(i).wait()
         for m in range(MON_DEV):
-            rows = field[m, pl.ds(pl.multiple_of(i * 16, 16), 16), :].astype(jnp.float32)
-            ring = jnp.concatenate([rows, rows[:, :224]], axis=1)
+            rows = field[m, pl.ds(pl.multiple_of(i * 16, 16), 16), :]
+            ring = jnp.concatenate([rows, rows[:, :352]], axis=1)
             for l in range(N_LON):
+                start = (LON_DEV * l - HMAX) % NLON
+                first_tile, shift = start // LANES, start % LANES
+                tiles = [ring[:, t * LANES : (t + 1) * LANES] for t in range(first_tile, first_tile + 4)]
+                if shift:
+                    tiles = [pltpu.roll(t, LANES - shift, 1) for t in tiles]
                 for j in range(3):
-                    start = LON_DEV * l - HMAX + LANES * j
-                    start = start + NLON if start < 0 else start
-                    piece = ring[:, start : start + LANES]
+                    piece = jnp.where(lane16 < LANES - shift, tiles[j], tiles[j + 1]) if shift else tiles[j]
+                    piece = piece.astype(jnp.float32)
                     for half in range(2):
                         first = half * 8 * SSTRIDE + j * WINDOWS + m * N_LON + l
                         staged[pl.ds(first, 8, stride=SSTRIDE), :] = piece[half * 8 : half * 8 + 8]
@@ -231,7 +240,7 @@
     return out.reshape(N_LON * N_LAT, CHUNK, LANES)
 
 
-def gram_kernel(landed_hbm, weight, packed, anomaly_hbm, landed, wide, anomaly, in_sems, out_sem):
+def gram_kernel(core, landed_hbm, weight, mine, theirs, anomaly_hbm, landed, wide, anomaly, square, in_sems, out_sem):
     parts = 4
     size = N_LON * N_LAT // parts
     copies = [
@@ -267,50 +276,72 @@
         anomaly[:, g * LANES : (g + 1) * LANES] = ((cells - mean) * scale).astype(jnp.bfloat16)
     store = pltpu.make_async_copy(anomaly, anomaly_hbm, out_sem)
     store.start()
-    half = MONTHS // 2
     for i, j in ((0, 0), (0, 1), (1, 1)):
         block = lax.dot_general(
-            anomaly[i * half : (i + 1) * half, :],
-            anomaly[j * half : (j + 1) * half, :],
+            anomaly[i * ROWB : (i + 1) * ROWB, :],
+            anomaly[j * ROWB : (j + 1) * ROWB, :],
             (((1,), (1,)), ((), ())),
             preferred_element_type=jnp.float32,
         )
         for n, (bi, bj) in enumerate(BLOCKS):
             if bi // 2 == i and bj // 2 == j:
                 a, c = (bi % 2) * LANES, (bj % 2) * LANES
-                packed[pl.ds(n, LANES, stride=PACK), :] = block[a : a + LANES, c : c + LANES]
+                square[...] = block[a : a + LANES, c : c + LANES]
+                for ref, half in ((mine, core[0]), (theirs, 1 - core[0])):
+                    rows = pl.ds(pl.multiple_of(half * HALF, HALF), HALF)
+                    ref[pl.ds(n, HALF, stride=PACK), :] = square[rows, :]
     store.wait()
 
 
-def gram_terms(landed, weight):
+def gram_terms(core, landed, weight):
+    part = jax.ShapeDtypeStruct((HALF * PACK, LANES), jnp.float32)
     return pl.pallas_call(
         gram_kernel,
-        out_shape=(
-            jax.ShapeDtypeStruct((LANES * PACK, LANES), jnp.float32),
-            jax.ShapeDtypeStruct((MONTHS, GROUPS * LANES), jnp.bfloat16),
-        ),
-        in_specs=[pl.BlockSpec(memory_space=pl.ANY), pl.BlockSpec(memory_space=pltpu.VMEM)],
-        out_specs=(pl.BlockSpec(memory_space=pltpu.VMEM), pl.BlockSpec(memory_space=pl.ANY)),
+        out_shape=(part, part, jax.ShapeDtypeStruct((MONTHS, GROUPS * LANES), jnp.bfloat16)),
+        in_specs=[
+            pl.BlockSpec(memory_space=pltpu.SMEM),
+            pl.BlockSpec(memory_space=pl.ANY),
+            pl.BlockSpec(memory_space=pltpu.VMEM),
+        ],
+        out_specs=(pl.BlockSpec(memory_space=pltpu.VMEM),) * 2 + (pl.BlockSpec(memory_space=pl.ANY),),
         scratch_shapes=[
             pltpu.VMEM((N_LON * N_LAT, CHUNK, LANES), jnp.bfloat16),
             pltpu.VMEM((N_LON * N_LAT * CHUNK, LANES), jnp.float32),
             pltpu.VMEM((MONTHS, GROUPS * LANES), jnp.bfloat16),
+            pltpu.VMEM((LANES, LANES), jnp.float32),
             pltpu.SemaphoreType.DMA((4,)),
             pltpu.SemaphoreType.DMA,
         ],
         compiler_params=pltpu.CompilerParams(vmem_limit_bytes=32 * 1024 * 1024),
         name="gram_terms",
-    )(landed, weight)
+    )(core, landed, weight)
+
+
+def turn_kernel(anomaly, turned):
+    for g in range(GROUPS):
+        turned[g * LANES : (g + 1) * LANES, :] = anomaly[:, g * LANES : (g + 1) * LANES].T
+
+
+def turn(anomaly):
+    return pl.pallas_call(
+        turn_kernel,
+        out_shape=jax.ShapeDtypeStruct((GROUPS * LANES, MONTHS), jnp.bfloat16),
+        in_specs=[pl.BlockSpec(memory_space=pltpu.VMEM)],
+        out_specs=pl.BlockSpec(memory_space=pltpu.VMEM),
+        compiler_params=pltpu.CompilerParams(vmem_limit_bytes=16 * 1024 * 1024),
+        cost_estimate=pl.CostEstimate(flops=2000000000, bytes_accessed=6000000, transcendentals=0),
+        name="turn",
+    )(anomaly)
 
 
 def add_kernel(terms, out):
     step = 4 * PACK
     total = terms[0:step, :]
-    for s in range(1, LANES // 4):
+    for s in range(1, HALF // 4):
         total = total + terms[s * step : (s + 1) * step, :]
     row = total[0:PACK] + total[PACK : 2 * PACK] + total[2 * PACK : 3 * PACK] + total[3 * PACK :]
     total = jnp.concatenate([row] * 4, axis=0)
-    for s in range(LANES // 4):
+    for s in range(HALF // 4):
         out[s * step : (s + 1) * step, :] = total
 
 
@@ -330,13 +361,15 @@
 MIRROR = True
 
 
-def root_kernel(packed, anomaly_hbm, patterns_hbm, whitener_hbm, anomaly, patterns, whitener, ws, hs, ps, ss, zs, wb, in_sem, out_sems):
+def root_kernel(core, mine, theirs, anomaly_hbm, patterns_hbm, whitener_hbm, anomaly, patterns, whitener, ws, hs, ps, ss, zs, wb, in_sem, out_sems):
     fetch = pltpu.make_async_copy(anomaly_hbm, anomaly, in_sem)
     fetch.start()
     for n, (bi, bj) in enumerate(BLOCKS):
-        block = packed[pl.ds(n, LANES, stride=PACK), :]
-        whitener[bi * LANES : (bi + 1) * LANES, bj * LANES : (bj + 1) * LANES] = block
+        for ref, half in ((mine, core[0]), (theirs, 1 - core[0])):
+            rows = pl.ds(pl.multiple_of(bi * LANES + half * HALF, HALF), HALF)
+            whitener[rows, bj * LANES : (bj + 1) * LANES] = ref[pl.ds(n, HALF, stride=PACK), :]
         if bi != bj:
+            block = whitener[bi * LANES : (bi + 1) * LANES, bj * LANES : (bj + 1) * LANES]
             whitener[bj * LANES : (bj + 1) * LANES, bi * LANES : (bi + 1) * LANES] = block.T
     gram = whitener[...]
     squares = jnp.sum(gram * gram, axis=0, keepdims=True)
@@ -376,7 +409,7 @@
     c0, c1, c2, c3, c4 = STEP
     last = ITERS // 2 - 1
 
-    def double_step(k, carry):
+    def double_step(k):
         for n, square in enumerate(product(ws, ws)):
             start = n * ROWB
             split(ss, start, square)
@@ -385,26 +418,22 @@
             start = n * ROWB
             split(ps, start, plus_eye(value + c1 * join(ws, start), start, c0))
 
-        @pl.when(k == 0)
-        def _():
+        if k == 0:
             zs[...] = ps[0 : 2 * MONTHS, :]
 
-        @pl.when(k > 0)
-        def _():
+        if k > 0:
             for n, value in enumerate(product(zs, ps)):
                 split(zs, n * ROWB, value)
                 whitener[n * ROWB : (n + 1) * ROWB, :] = value * final_scale
 
-        @pl.when(k < last)
-        def _():
+        if k < last:
             for n, value in enumerate(product(ws, ps)):
                 split(ss, n * ROWB, value)
             for n, value in enumerate(product(ss, ps)):
                 split(ws, n * ROWB, value)
 
-        return carry
-
-    lax.fori_loop(0, last + 1, double_step, 0)
+    for k in range(last + 1):
+        double_step(k)
     copies = [pltpu.make_async_copy(whitener, whitener_hbm, out_sems.at[LAT_DEV])]
     copies[0].start()
     wb[...] = whitener[...].astype(jnp.bfloat16)
@@ -412,9 +441,9 @@
 
     def group(g):
         return lax.dot_general(
-            anomaly[:, g * LANES : (g + 1) * LANES],
+            anomaly[g * LANES : (g + 1) * LANES, :],
             wb[...],
-            (((0,), (1,)), ((), ())),
+            (((1,), (1,)), ((), ())),
             preferred_element_type=jnp.float32,
         ).astype(jnp.bfloat16)
 
@@ -440,17 +469,22 @@
         copy.wait()
 
 
-def root_and_patterns(packed, anomaly):
+def root_and_patterns(core, mine, theirs, turned):
     return pl.pallas_call(
         root_kernel,
         out_shape=(
             jax.ShapeDtypeStruct((LAT_DEV, LON_DEV, MONTHS), jnp.bfloat16),
             jax.ShapeDtypeStruct((MONTHS, MONTHS), jnp.float32),
         ),
-        in_specs=[pl.BlockSpec(memory_space=pltpu.VMEM), pl.BlockSpec(memory_space=pl.ANY)],
+        in_specs=[
+            pl.BlockSpec(memory_space=pltpu.SMEM),
+            pl.BlockSpec(memory_space=pltpu.VMEM),
+            pl.BlockSpec(memory_space=pltpu.VMEM),
+            pl.BlockSpec(memory_space=pl.ANY),
+        ],
         out_specs=(pl.BlockSpec(memory_space=pl.ANY),) * 2,
         scratch_shapes=[
-            pltpu.VMEM((MONTHS, GROUPS * LANES), jnp.bfloat16),
+            pltpu.VMEM((GROUPS * LANES, MONTHS), jnp.bfloat16),
             pltpu.VMEM((LAT_DEV, LON_DEV, MONTHS), jnp.bfloat16),
             pltpu.VMEM((MONTHS, MONTHS), jnp.float32),
             pltpu.VMEM((3 * MONTHS, MONTHS), jnp.bfloat16),
@@ -464,26 +498,30 @@
         ],
         compiler_params=pltpu.CompilerParams(vmem_limit_bytes=32 * 1024 * 1024),
         name="root_and_patterns",
-    )(packed, anomaly)
-
-
-def exchange(pieces):
-    return lax.all_to_all(pieces, BOTH, split_axis=0, concat_axis=0, tiled=True)
+    )(core, mine, theirs, turned)
+
+
+def exchange(pieces, axes):
+    return lax.all_to_all(pieces, axes, split_axis=0, concat_axis=0, tiled=True)
 
 
 def exchange_packed(packed):
-    pieces = packed.reshape(N_LON * N_LAT, PACK // 2, 2, LANES)
-    return exchange(pieces).reshape(packed.shape)
+    pieces = packed.reshape(HALF, PACK // 2, 2, LANES)
+    return exchange(pieces, SAME_CORE).reshape(packed.shape)
+
+
+def swap_cores(x):
+    return lax.ppermute(x, "core", [(0, 1), (1, 0)])
 
 
 def swap(x, k):
-    return lax.ppermute(x, "lat", [(i, i ^ k) for i in range(N_LAT)])
+    return lax.ppermute(x, LAT, [(i, i ^ k) for i in range(N_LAT)])
 
 
 def gather_widths(half_width):
     own = jnp.pad(half_width, (0, LANES - LAT_DEV)).reshape(1, LANES)
     rows = [own] + [swap(own, k) for k in (1, 2, 3)]
-    place = lax.axis_index("lat") & 3
+    place = lax.axis_index(LAT) & 3
     at = jnp.arange(4, dtype=jnp.int32).reshape(4, 1)
     quad = jnp.zeros((4, LANES), jnp.int32)
     for k in range(4):
@@ -497,21 +535,24 @@
     field, quad = lax.optimization_barrier((monthly_field, quad))
     quads = [quad] + [swap(quad, 4 * k) for k in (1, 2, 3)]
     back = cut_windows(field, FRONT, NLAT // 16 - FRONT)
-    chip = (lax.axis_index("lat") >> 2).reshape(1)
-    landed = exchange(smooth(chip, quads, front, back))
-    row_index = lax.axis_index("lat") * LAT_DEV + jnp.arange(LAT_DEV)
+    chip = (lax.axis_index(LAT) >> 2).reshape(1)
+    landed = exchange(smooth(chip, quads, front, back), BOTH)
+    row_index = lax.axis_index(LAT) * LAT_DEV + jnp.arange(LAT_DEV)
     latitude = math.pi * ((row_index.astype(jnp.float32) + 0.5) / NLAT - 0.5)
     weight = jnp.sqrt(jnp.cos(latitude))[:, None] * land_mask.astype(jnp.float32)
     weight = jnp.pad(weight, ((0, 0), (0, 2 * LANES - LON_DEV)))
-    packed, anomaly = gram_terms(landed, weight)
-    packed = exchange_packed(packed)
-    packed = exchange_packed(add_terms(packed))
-    patterns, whitener = root_and_patterns(packed, anomaly)
+    core = lax.axis_index("core").reshape(1)
+    mine, theirs, anomaly = gram_terms(core, landed, weight)
+    terms = exchange_packed(mine + swap_cores(theirs))
+    turned = turn(anomaly)
+    mine = exchange_packed(add_terms(terms))
+    patterns, whitener = root_and_patterns(core, mine, swap_cores(mine), turned)
     return (jnp.transpose(patterns, (2, 0, 1)), whitener)
 
 
 def solution(mesh):
-    placed = (P(("lon", "lat"), None, None), P("lat"), P("lat", "lon"))
+    fine = Mesh(mesh.devices.reshape(N_LON, N_LAT // 2, 2), BOTH)
+    placed = (P(BOTH, None, None), P(LAT), P(LAT, "lon"))
     return jax.shard_map(
-        local, mesh=mesh, in_specs=placed, out_specs=(P(None, "lat", "lon"), P()), check_vma=False
+        local, mesh=fine, in_specs=placed, out_specs=(P(None, LAT, "lon"), P()), check_vma=False
     )

time: 144 us -> 139 us (0.965)
  blocking collectives: 38.9 us -> 30.1 us
  starting transfers between devices: 19.4 us -> 23 us
  Pallas kernels: 44.8 us -> 42.5 us
  waiting for transfers between devices: 38.4 us -> 40.1 us
    all_to_all x2, blocking collectives: 38.9 us -> 30.1 us  [exchange(): return lax.all_to_all(pieces, axes, split_axis=0, concat_axis=0, tiled=True)]
    ppermute x6 -> x8, starting transfers between devices: 8.51 us -> 12.1 us  [the longest x6 8.51 us: swap(): return lax.ppermute(x, LAT, [(i, i ^ k) for i in range(N_LAT)])]
    pallas_call x1, Pallas kernels: 19.2 us -> 17.5 us  [root_and_patterns(): pl.pallas_call(root_kernel, out_shape=(jax.ShapeDtypeStruct((LAT_DEV, LON...]
    ppermute x6 -> x8, waiting for transfers between devices: 0.02 us -> 1.73 us  [the longest x2 1.72 us: swap_cores(): return lax.ppermute(x, 'core', [(0, 1), (1, 0)])]
    pallas_call x1 -> x2, Pallas kernels: 4.49 us -> 5.32 us  [the longest x1 4.53 us: gram_terms(): pl.pallas_call(gram_kernel, out_shape=(part, part, jax.ShapeDtypeStruct((...]
  transfers between devices with their start and end apart: 7 -> 9, of which waited for: 1 -> 3; matrix products, arithmetic and copies ran while one was open for 0% -> 0% of each run, Pallas kernels for 7% -> 7%
where the time goes in v4:
time: 139 us; the launch traced here: 138 us
  Pallas kernels  42.5 us (31%)
  waiting for transfers between devices  40.1 us (29%)
  blocking collectives  30.1 us (22%)
  starting transfers between devices  23 us (17%)
    all_to_all x1, waiting for transfers between devices, exchange(): return lax.all_to_all(pieces, axes, split_axis=0, concat_axis=0, tiled=True)  38.4 us
    all_to_all x2, blocking collectives, exchange(): return lax.all_to_all(pieces, axes, split_axis=0, concat_axis=0, tiled=True)  30.1 us
    pallas_call x1, Pallas kernels, root_and_patterns(): pl.pallas_call(root_kernel, out_shape=(jax.ShapeDtypeStruct((LAT_DEV, LON...  17.5 us
    pallas_call x1, Pallas kernels, smooth(): pl.pallas_call(smooth_kernel, out_shape=jax.ShapeDtypeStruct((N_LON, N_LA...  11 us
    all_to_all x1, starting transfers between devices, exchange(): return lax.all_to_all(pieces, axes, split_axis=0, concat_axis=0, tiled=True)  10.9 us
    pallas_call x2, Pallas kernels, cut_windows(): pl.pallas_call(functools.partial(windows_kernel, first_step), out_shape=j...  8.66 us
    ppermute x6, starting transfers between devices, swap(): return lax.ppermute(x, LAT, [(i, i ^ k) for i in range(N_LAT)])  8.51 us
    pallas_call x1, Pallas kernels, gram_terms(): pl.pallas_call(gram_kernel, out_shape=(part, part, jax.ShapeDtypeStruct((...  4.53 us
  transfers between devices with their start and end apart: 9, of which 3 were waited for; matrix products, arithmetic and copies ran while one was open for 0% of the time, Pallas kernels for 7%

profile of v4, /device:TPU:1, one launch (start us, length us, event | category | flops | bytes accessed | tf_op | source)
XLA Modules:
  0.0 138.2 jit_solution(13159372829606593629)
XLA Ops:
  0.6 0.7 pad_bitcast_fusion
  1.3 4.1 %collective-permute-start = (s32[1,128]{1,0:T(1,128)S(1)}, s32[1,128]{1,0:T(1,128)S(1)}, u32[]{:S(2)}, u32[]{:S(2)}) collective-permute-start(s32[1,128]{1,0:T(1,128)S(1)} %get-tuple-element.16), channel_id=1, source_target_pairs={{0,3},{1,2},{2,1},{3,0},{4,7},{5,6},{6,5},{7,4},{8,11},{9,10},{10,... | collective-permute-start | bytes 1544 | tf_op jit(solution)/shard_map/ppermute | solution.py:518
  5.4 0.1 collective-permute-start.1
  5.6 0.3 collective-permute-start.2
  5.9 4.5 %cut_windows.2.refs_4_ = bf16[128,96,128]{2,1,0:T(8,128)(2,1)} custom-call(bf16[4,240,1440]{2,1,0:T(8,128)(2,1)} %field_hbm.2), custom_call_target="tpu_custom_call" | custom-call | flops 3000000000 | bytes 9000000 | tf_op jit(solution)/shard_map/cut_windows/pallas_call | solution.py:94
  10.4 0.0 collective-permute-done
  10.4 0.0 collective-permute-done.1
  10.4 0.0 collective-permute-done.2
  10.4 0.1 select_select_fusion.refs_0_
  10.5 1.3 collective-permute-start.3
  11.8 2.6 %collective-permute-start.4 = (s32[4,128]{1,0:T(4,128)S(1)}, s32[4,128]{1,0:T(4,128)S(1)}, u32[]{:S(2)}, u32[]{:S(2)}) collective-permute-start(s32[4,128]{1,0:T(4,128)S(1)} %select_select_fusion.refs_0_), channel_id=1, source_target_pairs={{0,8},{1,9},{2,10},{3,11},{4,12},{5,13},{6,14},{7,15},{8,0},{9,1},... | collective-permute-start | bytes 6152 | tf_op jit(solution)/shard_map/ppermute | solution.py:518
  14.5 0.0 collective-permute-start.5
  14.5 4.1 %cut_windows.3.refs_5_ = bf16[112,96,128]{2,1,0:T(8,128)(2,1)} custom-call(bf16[4,240,1440]{2,1,0:T(8,128)(2,1)} %field_hbm.2), custom_call_target="tpu_custom_call" | custom-call | flops 3000000000 | bytes 9000000 | tf_op jit(solution)/shard_map/cut_windows/pallas_call | solution.py:94
  18.6 0.0 collective-permute-done.3.refs_1_
  18.6 0.0 collective-permute-done.4.refs_2_
  18.7 0.5 copy-done.2
  19.2 0.0 copy-done.3
  19.2 11.0 %smooth.1 = bf16[8,16,88,128]{3,2,1,0:T(8,128)(2,1)} custom-call(s32[1]{0:T(128)} %bitcast.1.chip, s32[4,128]{1,0:T(4,128)} %copy-done.1, s32[4,128]{1,0:T(4,128)} %copy-done.2, s32[4,128]{1,0:T(4,128)} %copy-done.3, s32[4,128]{1,0:T(4,128)} %copy-done.4, bf16[128,96,128]{2,1,0:T(8,128)(2,1)} %cut_windows.2.refs_4_, bf16[112,96,128]{2,1,0:T(8,128)(2,1)} %cut_windows.3.refs_5_), custom_call_target="tpu_custom_call" | custom-call | tf_op jit(solution)/shard_map/smooth/pallas_call | solution.py:222
  30.3 0.0 copy-start
  30.3 10.9 %all-to-all-start = ((bf16[128,88,128]{2,1,0:T(8,128)(2,1)}), bf16[128,88,128]{2,1,0:T(8,128)(2,1)S(1)}, u32[]{:S(2)}, u32[]{:S(2)}) async-start(bf16[128,88,128]{2,1,0:T(8,128)(2,1)} %bitcast.17), calls=%async_computation | async-start | bytes 5767168 | tf_op jit(solution)/shard_map/all_to_all | solution.py:505
  41.2 0.1 cosine_sqrt_fusion
  41.3 0.1 convert_multiply_fusion
  41.4 38.4 %all-to-all-done.landed_hbm = bf16[128,88,128]{2,1,0:T(8,128)(2,1)S(1)} async-done(((bf16[128,88,128]{2,1,0:T(8,128)(2,1)}), bf16[128,88,128]{2,1,0:T(8,128)(2,1)S(1)}, u32[]{:S(2)}, u32[]{:S(2)}) %all-to-all-start) | async-done | bytes 2883616 | tf_op jit(solution)/shard_map/all_to_all | solution.py:505
  79.7 4.5 %gram_terms.1 = (f32[640,128]{1,0:T(8,128)S(1)}, f32[640,128]{1,0:T(8,128)S(1)}, bf16[512,2816]{1,0:T(8,128)(2,1)S(1)}) custom-call(s32[1]{0:T(128)} %bitcast.core, bf16[128,88,128]{2,1,0:T(8,128)(2,1)S(1)} %all-to-all-done.landed_hbm, f32[15,256]{1,0:T(8,128)S(1)} %pad.9.weight), custom_call_target="tpu_custom_call" | custom-call | tf_op jit(solution)/shard_map/gram_terms/pallas_call | solution.py:298
  84.3 0.6 collective-permute-start.6
  84.9 1.3 collective-permute-done.6
  86.2 15.2 %all_to_all.15 = f32[64,5,2,128]{3,2,1,0:T(2,128)S(1)} all-to-all(f32[64,5,2,128]{3,2,1,0:T(2,128)S(1)} %bitcast.18), channel_id=1, replica_groups=mesh['lon'=8,'chip'=8,'core'=2] {'lon','chip'}, dimensions={0} | all-to-all | bytes 655360 | tf_op jit(solution)/shard_map/all_to_all | solution.py:505
  101.4 14.9 %all_to_all.16 = f32[64,5,2,128]{3,2,1,0:T(2,128)S(1)} all-to-all(f32[64,5,2,128]{3,2,1,0:T(2,128)S(1)} %bitcast.14), channel_id=1, replica_groups=mesh['lon'=8,'chip'=8,'core'=2] {'lon','chip'}, dimensions={0} | all-to-all | bytes 655360 | tf_op jit(solution)/shard_map/all_to_all | solution.py:505
  116.3 3.0 %collective-permute-start.7 = (f32[640,128]{1,0:T(8,128)S(1)}, f32[640,128]{1,0:T(8,128)S(1)}, u32[]{:S(2)}, u32[]{:S(2)}) collective-permute-start(f32[640,128]{1,0:T(8,128)S(1)} %bitcast.15), channel_id=1, source_target_pairs={{0,1},{1,0},{2,3},{3,2},{4,5},{5,4},{6,7},{7,6},{8,9},{9,8},{10,11... | collective-permute-start | bytes 983048 | tf_op jit(solution)/shard_map/ppermute | solution.py:514
  119.3 0.8 turn.1.anomaly_hbm
  120.1 0.5 collective-permute-done.7.theirs
  120.6 17.5 %root_and_patterns.1 = (bf16[15,180,512]{2,1,0:T(8,128)(2,1)}, f32[512,512]{1,0:T(8,128)}) custom-call(s32[1]{0:T(128)} %bitcast.core, f32[640,128]{1,0:T(8,128)S(1)} %bitcast.16, f32[640,128]{1,0:T(8,128)S(1)} %collective-permute-done.7.theirs, bf16[2816,512]{1,0:T(8,128)(2,1)S(1)} %turn.1.anomaly_hbm), custom_call_target="tpu_custom_call" | custom-call | tf_op jit(solution)/shard_map/root_and_patterns/pallas_call | solution.py:473
  (13 shorter events, 0.1 us)
Async XLA Ops:
  1.3 9.1 %collective-permute-start = (s32[1,128]{1,0:T(1,128)S(1)}, s32[1,128]{1,0:T(1,128)S(1)}, u32[]{:S(2)}, u32[]{:S(2)}) collective-permute-start(s32[1,128]{1,0:T(1,128)S(1)} %get-tuple-element.16), channel_id=1, source_target_pairs={{0,3},{1,2},{2,1},{3,0},{4,7},{5,6},{6,5},{7,4},{8,11},{9,10},{10,... | collective-permute-start | bytes 1544 | tf_op jit(solution)/shard_map/ppermute | solution.py:518
  5.4 5.0 %collective-permute-start.1 = (s32[1,128]{1,0:T(1,128)S(1)}, s32[1,128]{1,0:T(1,128)S(1)}, u32[]{:S(2)}, u32[]{:S(2)}) collective-permute-start(s32[1,128]{1,0:T(1,128)S(1)} %get-tuple-element.16), channel_id=1, source_target_pairs={{0,2},{1,3},{2,0},{3,1},{4,6},{5,7},{6,4},{7,5},{8,10},{9,11},{10,... | collective-permute-start | bytes 1544 | tf_op jit(solution)/shard_map/ppermute | solution.py:518
  5.6 4.9 %collective-permute-start.2 = (s32[1,128]{1,0:T(1,128)S(1)}, s32[1,128]{1,0:T(1,128)S(1)}, u32[]{:S(2)}, u32[]{:S(2)}) collective-permute-start(s32[1,128]{1,0:T(1,128)S(1)} %get-tuple-element.16), channel_id=1, source_target_pairs={{0,1},{1,0},{2,3},{3,2},{4,5},{5,4},{6,7},{7,6},{8,9},{9,8},{10,11... | collective-permute-start | bytes 1544 | tf_op jit(solution)/shard_map/ppermute | solution.py:518
  10.5 8.1 %copy-start.1 = (s32[4,128]{1,0:T(4,128)}, s32[4,128]{1,0:T(4,128)S(1)}, u32[]{:S(2)}) copy-start(s32[4,128]{1,0:T(4,128)S(1)} %select_select_fusion.refs_0_) | copy-start | bytes 6148
  10.5 8.1 %collective-permute-start.3 = (s32[4,128]{1,0:T(4,128)S(1)}, s32[4,128]{1,0:T(4,128)S(1)}, u32[]{:S(2)}, u32[]{:S(2)}) collective-permute-start(s32[4,128]{1,0:T(4,128)S(1)} %select_select_fusion.refs_0_), channel_id=1, source_target_pairs={{0,4},{1,5},{2,6},{3,7},{4,0},{5,1},{6,2},{7,3},{8,12},{9,13},{10,... | collective-permute-start | bytes 6152 | tf_op jit(solution)/shard_map/ppermute | solution.py:518
  11.8 6.8 %collective-permute-start.4 = (s32[4,128]{1,0:T(4,128)S(1)}, s32[4,128]{1,0:T(4,128)S(1)}, u32[]{:S(2)}, u32[]{:S(2)}) collective-permute-start(s32[4,128]{1,0:T(4,128)S(1)} %select_select_fusion.refs_0_), channel_id=1, source_target_pairs={{0,8},{1,9},{2,10},{3,11},{4,12},{5,13},{6,14},{7,15},{8,0},{9,1},... | collective-permute-start | bytes 6152 | tf_op jit(solution)/shard_map/ppermute | solution.py:518
  14.5 4.2 %collective-permute-start.5 = (s32[4,128]{1,0:T(4,128)S(1)}, s32[4,128]{1,0:T(4,128)S(1)}, u32[]{:S(2)}, u32[]{:S(2)}) collective-permute-start(s32[4,128]{1,0:T(4,128)S(1)} %select_select_fusion.refs_0_), channel_id=1, source_target_pairs={{0,12},{1,13},{2,14},{3,15},{4,8},{5,9},{6,10},{7,11},{8,4},{9,5},... | collective-permute-start | bytes 6152 | tf_op jit(solution)/shard_map/ppermute | solution.py:518
  18.6 0.6 copy-start.2
  18.7 0.6 copy-start.3
  18.7 0.6 copy-start.4
  30.3 11.0 %copy-start = (s32[15,180]{1,0:T(8,128)S(1)}, s32[15,180]{1,0:T(8,128)}, u32[]{:S(2)}) copy-start(s32[15,180]{1,0:T(8,128)} %param.5) | copy-start | bytes 32404
  30.3 49.4 %all-to-all-start = ((bf16[128,88,128]{2,1,0:T(8,128)(2,1)}), bf16[128,88,128]{2,1,0:T(8,128)(2,1)S(1)}, u32[]{:S(2)}, u32[]{:S(2)}) async-start(bf16[128,88,128]{2,1,0:T(8,128)(2,1)} %bitcast.17), calls=%async_computation | async-start | bytes 5767168 | tf_op jit(solution)/shard_map/all_to_all | solution.py:505
  84.3 1.9 %collective-permute-start.6 = (f32[640,128]{1,0:T(8,128)S(1)}, f32[640,128]{1,0:T(8,128)S(1)}, u32[]{:S(2)}, u32[]{:S(2)}) collective-permute-start(f32[640,128]{1,0:T(8,128)S(1)} %get-tuple-element.12), channel_id=1, source_target_pairs={{0,1},{1,0},{2,3},{3,2},{4,5},{5,4},{6,7},{7,6},{8,9},{9,8},{10,11... | collective-permute-start | bytes 983048 | tf_op jit(solution)/shard_map/ppermute | solution.py:514
  116.3 4.2 %collective-permute-start.7 = (f32[640,128]{1,0:T(8,128)S(1)}, f32[640,128]{1,0:T(8,128)S(1)}, u32[]{:S(2)}, u32[]{:S(2)}) collective-permute-start(f32[640,128]{1,0:T(8,128)S(1)} %bitcast.15), channel_id=1, source_target_pairs={{0,1},{1,0},{2,3},{3,2},{4,5},{5,4},{6,7},{7,6},{8,9},{9,8},{10,11... | collective-permute-start | bytes 983048 | tf_op jit(solution)/shard_map/ppermute | solution.py:514

commit v5 on v4

--- a/solution.py
+++ b/solution.py
@@ -1,4 +1,3 @@
-import functools
 import math
 
 import jax
@@ -34,7 +33,6 @@
 SROWS = 3 * WINDOWS
 SSTRIDE = 97
 VSTRIDE = 89
-FRONT = 8
 BLOCKS = [(i, j) for i in range(4) for j in range(i, 4)]
 PACK = len(BLOCKS)
 VMEM_LIMIT = 60 * 1024 * 1024
@@ -47,14 +45,13 @@
     return [float(t) for t in taps.astype(jnp.bfloat16).astype(np.float32)]
 
 
-def windows_kernel(first_step, field_hbm, out_hbm, field, windows, staged, in_sems, out_sems):
+def windows_kernel(field_hbm, out_hbm, field, windows, staged, in_sems, out_sems):
     steps = windows.shape[0] // 16
     lane16 = lax.broadcasted_iota(jnp.int32, (16, LANES), 1)
 
     def fetch(i):
         rows = pl.ds(pl.multiple_of(i * 16, 16), 16)
-        source = pl.ds(pl.multiple_of((first_step + i) * 16, 16), 16)
-        return pltpu.make_async_copy(field_hbm.at[:, source, :], field.at[:, rows, :], in_sems.at[i])
+        return pltpu.make_async_copy(field_hbm.at[:, rows, :], field.at[:, rows, :], in_sems.at[i])
 
     def store(i):
         rows = pl.ds(pl.multiple_of(i * 16, 16), 16)
@@ -90,9 +87,10 @@
         store(i).wait()
 
 
-def cut_windows(field, first_step, steps):
+def cut_windows(field):
+    steps = NLAT // 16
     return pl.pallas_call(
-        functools.partial(windows_kernel, first_step),
+        windows_kernel,
         out_shape=jax.ShapeDtypeStruct((steps * 16, SROWS, LANES), jnp.bfloat16),
         in_specs=[pl.BlockSpec(memory_space=pl.ANY)],
         out_specs=pl.BlockSpec(memory_space=pl.ANY),
@@ -109,30 +107,17 @@
     )(field)
 
 
-def smooth_kernel(chip, *refs):
-    quads, refs = refs[:4], refs[4:]
-    (front, back, out_hbm, windows, out, taps, passed, staged, widths, in_sems, out_sems) = refs
+def smooth_kernel(widths, windows_hbm, out_hbm, windows, out, taps, passed, staged, in_sems, out_sems):
 
     def fetch(i):
-        rows = pl.ds(i * 16, 16)
-        if i < FRONT:
-            return pltpu.make_async_copy(front.at[rows], windows.at[rows], in_sems.at[i])
-        return pltpu.make_async_copy(back.at[pl.ds((i - FRONT) * 16, 16)], windows.at[rows], in_sems.at[i])
-
-    def arrived(i):
         rows = pl.ds(pl.multiple_of(i * 16, 16), 16)
-        pltpu.make_async_copy(windows.at[rows], windows.at[rows], in_sems.at[i]).wait()
+        return pltpu.make_async_copy(windows_hbm.at[rows], windows.at[rows], in_sems.at[i])
 
     def store(b):
         return pltpu.make_async_copy(out.at[:, b], out_hbm.at[:, b], out_sems.at[b])
 
     for i in range(NLAT // 16):
         fetch(i).start()
-    for k in range(4):
-        for j in range(4):
-            first = ((k ^ chip[0]) * 4 + j) * LAT_DEV
-            for rr in range(LAT_DEV):
-                widths[first + rr] = quads[k][j, rr]
     lane8 = lax.broadcasted_iota(jnp.int32, (8, LANES), 1)
     sub8 = lax.broadcasted_iota(jnp.int32, (8, LANES), 0)
     offset = (lane8 - HMAX).astype(jnp.float32)
@@ -141,7 +126,7 @@
         reach = jnp.zeros((8, LANES), jnp.int32)
         for s in range(8):
             r = i * 8 + s
-            reach = jnp.where(sub8 == s, widths[r], reach)
+            reach = jnp.where(sub8 == s, widths[r // LAT_DEV, r % LAT_DEV], reach)
         reach = reach.astype(jnp.float32)
         spread = 0.5 * reach
         value = jnp.exp(-(offset * offset) / (2.0 * spread * spread))
@@ -199,11 +184,11 @@
         for l in range(N_LON):
             out[l, b] = staged[l * VSTRIDE : l * VSTRIDE + CHUNK, :].astype(jnp.bfloat16)
 
-    arrived(0)
+    fetch(0).wait()
     lon_band(0)
 
     def band(b, carry):
-        arrived(b)
+        fetch(b).wait()
         lon_band(b)
         lat_band(b - 1)
         store(b - 1).start()
@@ -218,11 +203,11 @@
         store(b).wait()
 
 
-def smooth(chip, quads, front, back):
+def smooth(widths, windows):
     out = pl.pallas_call(
         smooth_kernel,
         out_shape=jax.ShapeDtypeStruct((N_LON, N_LAT, CHUNK, LANES), jnp.bfloat16),
-        in_specs=[pl.BlockSpec(memory_space=pltpu.SMEM)] * 5 + [pl.BlockSpec(memory_space=pl.ANY)] * 2,
+        in_specs=[pl.BlockSpec(memory_space=pltpu.SMEM), pl.BlockSpec(memory_space=pl.ANY)],
         out_specs=pl.BlockSpec(memory_space=pl.ANY),
         scratch_shapes=[
             pltpu.VMEM((NLAT, SROWS, LANES), jnp.bfloat16),
@@ -230,35 +215,21 @@
             pltpu.VMEM((NLAT, LANES), jnp.float32),
             pltpu.VMEM((NLAT + 2 * HL, 2 * WINDOWS, LANES), jnp.float32),
             pltpu.VMEM((N_LON * VSTRIDE + 8, LANES), jnp.float32),
-            pltpu.SMEM((NLAT,), jnp.int32),
             pltpu.SemaphoreType.DMA((NLAT // 16,)),
             pltpu.SemaphoreType.DMA((N_LAT,)),
         ],
         compiler_params=pltpu.CompilerParams(vmem_limit_bytes=VMEM_LIMIT),
         name="smooth",
-    )(chip, *quads, front, back)
+    )(widths, windows)
     return out.reshape(N_LON * N_LAT, CHUNK, LANES)
 
 
-def gram_kernel(core, landed_hbm, weight, mine, theirs, anomaly_hbm, landed, wide, anomaly, square, in_sems, out_sem):
-    parts = 4
-    size = N_LON * N_LAT // parts
-    copies = [
-        pltpu.make_async_copy(
-            landed_hbm.at[k * size : (k + 1) * size], landed.at[k * size : (k + 1) * size], in_sems.at[k]
-        )
-        for k in range(parts)
-    ]
-    for copy in copies:
-        copy.start()
-
+def gram_kernel(core, landed, weight, mine, theirs, anomaly, wide, square):
     def widen(s, carry):
         wide[pl.ds(pl.multiple_of(s * CHUNK, 8), CHUNK), :] = landed[s].astype(jnp.float32)
         return carry
 
-    for k in range(parts):
-        copies[k].wait()
-        lax.fori_loop(k * size, (k + 1) * size, widen, 0, unroll=4)
+    lax.fori_loop(0, N_LON * N_LAT, widen, 0, unroll=4)
     lane = lax.broadcasted_iota(jnp.int32, (1, LANES), 1)
     for g in range(GROUPS):
         if g < LAT_DEV:
@@ -274,8 +245,6 @@
         cells = wide[pl.ds(g, MONTHS, stride=GROUPS), :]
         mean = jnp.sum(cells, axis=0, keepdims=True) * (1.0 / MONTHS)
         anomaly[:, g * LANES : (g + 1) * LANES] = ((cells - mean) * scale).astype(jnp.bfloat16)
-    store = pltpu.make_async_copy(anomaly, anomaly_hbm, out_sem)
-    store.start()
     for i, j in ((0, 0), (0, 1), (1, 1)):
         block = lax.dot_general(
             anomaly[i * ROWB : (i + 1) * ROWB, :],
@@ -290,7 +259,6 @@
                 for ref, half in ((mine, core[0]), (theirs, 1 - core[0])):
                     rows = pl.ds(pl.multiple_of(half * HALF, HALF), HALF)
                     ref[pl.ds(n, HALF, stride=PACK), :] = square[rows, :]
-    store.wait()
 
 
 def gram_terms(core, landed, weight):
@@ -300,17 +268,13 @@
         out_shape=(part, part, jax.ShapeDtypeStruct((MONTHS, GROUPS * LANES), jnp.bfloat16)),
         in_specs=[
             pl.BlockSpec(memory_space=pltpu.SMEM),
-            pl.BlockSpec(memory_space=pl.ANY),
             pl.BlockSpec(memory_space=pltpu.VMEM),
-        ],
-        out_specs=(pl.BlockSpec(memory_space=pltpu.VMEM),) * 2 + (pl.BlockSpec(memory_space=pl.ANY),),
+            pl.BlockSpec(memory_space=pltpu.VMEM),
+        ],
+        out_specs=(pl.BlockSpec(memory_space=pltpu.VMEM),) * 3,
         scratch_shapes=[
-            pltpu.VMEM((N_LON * N_LAT, CHUNK, LANES), jnp.bfloat16),
             pltpu.VMEM((N_LON * N_LAT * CHUNK, LANES), jnp.float32),
-            pltpu.VMEM((MONTHS, GROUPS * LANES), jnp.bfloat16),
             pltpu.VMEM((LANES, LANES), jnp.float32),
-            pltpu.SemaphoreType.DMA((4,)),
-            pltpu.SemaphoreType.DMA,
         ],
         compiler_params=pltpu.CompilerParams(vmem_limit_bytes=32 * 1024 * 1024),
         name="gram_terms",
@@ -361,9 +325,7 @@
 MIRROR = True
 
 
-def root_kernel(core, mine, theirs, anomaly_hbm, patterns_hbm, whitener_hbm, anomaly, patterns, whitener, ws, hs, ps, ss, zs, wb, in_sem, out_sems):
-    fetch = pltpu.make_async_copy(anomaly_hbm, anomaly, in_sem)
-    fetch.start()
+def root_kernel(core, mine, theirs, anomaly, patterns_hbm, whitener_hbm, patterns, whitener, ws, hs, ps, ss, zs, wb, out_sems):
     for n, (bi, bj) in enumerate(BLOCKS):
         for ref, half in ((mine, core[0]), (theirs, 1 - core[0])):
             rows = pl.ds(pl.multiple_of(bi * LANES + half * HALF, HALF), HALF)
@@ -437,13 +399,12 @@
     copies = [pltpu.make_async_copy(whitener, whitener_hbm, out_sems.at[LAT_DEV])]
     copies[0].start()
     wb[...] = whitener[...].astype(jnp.bfloat16)
-    fetch.wait()
 
     def group(g):
         return lax.dot_general(
             anomaly[g * LANES : (g + 1) * LANES, :],
             wb[...],
-            (((1,), (1,)), ((), ())),
+            (((1,), (0,)), ((), ())),
             preferred_element_type=jnp.float32,
         ).astype(jnp.bfloat16)
 
@@ -480,11 +441,10 @@
             pl.BlockSpec(memory_space=pltpu.SMEM),
             pl.BlockSpec(memory_space=pltpu.VMEM),
             pl.BlockSpec(memory_space=pltpu.VMEM),
-            pl.BlockSpec(memory_space=pl.ANY),
+            pl.BlockSpec(memory_space=pltpu.VMEM),
         ],
         out_specs=(pl.BlockSpec(memory_space=pl.ANY),) * 2,
         scratch_shapes=[
-            pltpu.VMEM((GROUPS * LANES, MONTHS), jnp.bfloat16),
             pltpu.VMEM((LAT_DEV, LON_DEV, MONTHS), jnp.bfloat16),
             pltpu.VMEM((MONTHS, MONTHS), jnp.float32),
             pltpu.VMEM((3 * MONTHS, MONTHS), jnp.bfloat16),
@@ -493,7 +453,6 @@
             pltpu.VMEM((2 * MONTHS, MONTHS), jnp.bfloat16),
             pltpu.VMEM((2 * MONTHS, MONTHS), jnp.bfloat16),
             pltpu.VMEM((MONTHS, MONTHS), jnp.bfloat16),
-            pltpu.SemaphoreType.DMA,
             pltpu.SemaphoreType.DMA((LAT_DEV + 1,)),
         ],
         compiler_params=pltpu.CompilerParams(vmem_limit_bytes=32 * 1024 * 1024),
@@ -514,29 +473,11 @@
     return lax.ppermute(x, "core", [(0, 1), (1, 0)])
 
 
-def swap(x, k):
-    return lax.ppermute(x, LAT, [(i, i ^ k) for i in range(N_LAT)])
-
-
-def gather_widths(half_width):
-    own = jnp.pad(half_width, (0, LANES - LAT_DEV)).reshape(1, LANES)
-    rows = [own] + [swap(own, k) for k in (1, 2, 3)]
-    place = lax.axis_index(LAT) & 3
-    at = jnp.arange(4, dtype=jnp.int32).reshape(4, 1)
-    quad = jnp.zeros((4, LANES), jnp.int32)
-    for k in range(4):
-        quad = jnp.where(at == (place ^ k), rows[k], quad)
-    return quad
-
-
 def local(monthly_field, half_width, land_mask):
-    quad = gather_widths(half_width)
-    front = cut_windows(monthly_field, 0, FRONT)
-    field, quad = lax.optimization_barrier((monthly_field, quad))
-    quads = [quad] + [swap(quad, 4 * k) for k in (1, 2, 3)]
-    back = cut_windows(field, FRONT, NLAT // 16 - FRONT)
-    chip = (lax.axis_index(LAT) >> 2).reshape(1)
-    landed = exchange(smooth(chip, quads, front, back), BOTH)
+    widths = jnp.broadcast_to(jnp.pad(half_width, (0, LANES - LAT_DEV)), (N_LAT, 1, LANES))
+    widths = exchange(widths, LAT).reshape(N_LAT, LANES)
+    windows = cut_windows(monthly_field)
+    landed = exchange(smooth(widths, windows), BOTH)
     row_index = lax.axis_index(LAT) * LAT_DEV + jnp.arange(LAT_DEV)
     latitude = math.pi * ((row_index.astype(jnp.float32) + 0.5) / NLAT - 0.5)
     weight = jnp.sqrt(jnp.cos(latitude))[:, None] * land_mask.astype(jnp.float32)

time: 139 us -> 134 us (0.964)
  Pallas kernels: 42.5 us -> 38 us
    ppermute x6 -> x0, starting transfers between devices: 8.51 us -> none  [swap(): return lax.ppermute(x, LAT, [(i, i ^ k) for i in range(N_LAT)])]
    all_to_all x1 -> x2, starting transfers between devices: 10.9 us -> 18.7 us  [exchange(): return lax.all_to_all(pieces, axes, split_axis=0, concat_axis=0, tiled=True)]
    pallas_call x1, Pallas kernels: 4.53 us -> 2.29 us  [gram_terms(): pl.pallas_call(gram_kernel, out_shape=(part, part, jax.ShapeDtypeStruct((...]
    pallas_call x1, Pallas kernels: 17.5 us -> 15.6 us  [root_and_patterns(): pl.pallas_call(root_kernel, out_shape=(jax.ShapeDtypeStruct((LAT_DEV, LON...]
    pallas_call x2 -> x1, Pallas kernels: 8.66 us -> 7 us  [cut_windows(): pl.pallas_call(windows_kernel, out_shape=jax.ShapeDtypeStruct((steps * 16...]
    all_to_all x1 -> x2, waiting for transfers between devices: 38.4 us -> 38.4 us  [exchange(): return lax.all_to_all(pieces, axes, split_axis=0, concat_axis=0, tiled=True)]
  transfers between devices with their start and end apart: 9 -> 4, of which waited for: 3 -> 3; matrix products, arithmetic and copies ran while one was open for 0% -> 0% of each run, Pallas kernels for 7% -> 6%
where the time goes in v5:
time: 134 us; the launch traced here: 133 us
  waiting for transfers between devices  40.1 us (30%)
  Pallas kernels  38 us (28%)
  blocking collectives  30.1 us (22%)
  starting transfers between devices  22.3 us (17%)
  local copies, waits for them, and re-layouts  1.87 us (1%)
    all_to_all x2, waiting for transfers between devices, exchange(): return lax.all_to_all(pieces, axes, split_axis=0, concat_axis=0, tiled=True)  38.4 us
    all_to_all x2, blocking collectives, exchange(): return lax.all_to_all(pieces, axes, split_axis=0, concat_axis=0, tiled=True)  30.1 us
    all_to_all x2, starting transfers between devices, exchange(): return lax.all_to_all(pieces, axes, split_axis=0, concat_axis=0, tiled=True)  18.7 us
    pallas_call x1, Pallas kernels, root_and_patterns(): pl.pallas_call(root_kernel, out_shape=(jax.ShapeDtypeStruct((LAT_DEV, LON...  15.6 us
    pallas_call x1, Pallas kernels, smooth(): pl.pallas_call(smooth_kernel, out_shape=jax.ShapeDtypeStruct((N_LON, N_LA...  12.3 us
    pallas_call x1, Pallas kernels, cut_windows(): pl.pallas_call(windows_kernel, out_shape=jax.ShapeDtypeStruct((steps * 16...  7 us
    ppermute x2, starting transfers between devices, swap_cores(): return lax.ppermute(x, 'core', [(0, 1), (1, 0)])  3.6 us
  transfers between devices with their start and end apart: 4, of which 3 were waited for; matrix products, arithmetic and copies ran while one was open for 0% of the time, Pallas kernels for 6%

profile of v5, /device:TPU:1, one launch (start us, length us, event | category | flops | bytes accessed | tf_op | source)
XLA Modules:
  0.0 133.4 jit_solution(12648963671401963593)
XLA Ops:
  0.6 0.7 pad.8
  1.3 0.6 broadcast_in_dim.4
  1.9 8.4 %all-to-all-start = ((s32[16,1,128]{2,1,0:T(1,128)}), s32[16,1,128]{2,1,0:T(1,128)S(1)}, u32[]{:S(2)}, u32[]{:S(2)}) async-start(s32[16,1,128]{2,1,0:T(1,128)} %broadcast_in_dim.4), calls=%async_computation | async-start | bytes 16384 | tf_op jit(solution)/shard_map/all_to_all | solution.py:464
  10.3 7.0 %cut_windows.1.windows_hbm = bf16[240,96,128]{2,1,0:T(8,128)(2,1)} custom-call(bf16[4,240,1440]{2,1,0:T(8,128)(2,1)} %field_hbm.1), custom_call_target="tpu_custom_call" | custom-call | flops 3000000000 | bytes 9000000 | tf_op jit(solution)/shard_map/cut_windows/pallas_call | solution.py:92
  17.3 0.0 all-to-all-done
  17.4 0.0 copy-start
  17.4 0.6 copy-done
  18.0 12.3 %smooth.1 = bf16[8,16,88,128]{3,2,1,0:T(8,128)(2,1)} custom-call(s32[16,128]{1,0:T(8,128)} %bitcast.14, bf16[240,96,128]{2,1,0:T(8,128)(2,1)} %cut_windows.1.windows_hbm), custom_call_target="tpu_custom_call" | custom-call | tf_op jit(solution)/shard_map/smooth/pallas_call | solution.py:207
  30.2 0.0 copy-start.1
  30.3 10.3 %all-to-all-start.1 = ((bf16[128,88,128]{2,1,0:T(8,128)(2,1)}), bf16[128,88,128]{2,1,0:T(8,128)(2,1)S(1)}, u32[]{:S(2)}, u32[]{:S(2)}) async-start(bf16[128,88,128]{2,1,0:T(8,128)(2,1)} %bitcast.12), calls=%async_computation.1 | async-start | bytes 5767168 | tf_op jit(solution)/shard_map/all_to_all | solution.py:464
  40.5 0.1 cosine_sqrt_fusion
  40.6 0.0 copy-done.1
  40.6 0.1 convert_multiply_fusion
  40.7 38.4 %all-to-all-done.1.landed = bf16[128,88,128]{2,1,0:T(8,128)(2,1)S(1)} async-done(((bf16[128,88,128]{2,1,0:T(8,128)(2,1)}), bf16[128,88,128]{2,1,0:T(8,128)(2,1)S(1)}, u32[]{:S(2)}, u32[]{:S(2)}) %all-to-all-start.1) | async-done | bytes 2883616 | tf_op jit(solution)/shard_map/all_to_all | solution.py:464
  79.0 2.3 %gram_terms.1 = (f32[640,128]{1,0:T(8,128)S(1)}, f32[640,128]{1,0:T(8,128)S(1)}, bf16[512,2816]{1,0:T(8,128)(2,1)S(1)}) custom-call(s32[1]{0:T(128)} %bitcast.core, bf16[128,88,128]{2,1,0:T(8,128)(2,1)S(1)} %all-to-all-done.1.landed, f32[15,256]{1,0:T(8,128)S(1)} %pad.9.weight), custom_call_target="tpu_custom_call" | custom-call | tf_op jit(solution)/shard_map/gram_terms/pallas_call | solution.py:266
  81.3 0.6 collective-permute-start
  82.0 1.3 collective-permute-done
  83.3 15.2 %all_to_all.20 = f32[64,5,2,128]{3,2,1,0:T(2,128)S(1)} all-to-all(f32[64,5,2,128]{3,2,1,0:T(2,128)S(1)} %bitcast.13), channel_id=1, replica_groups=mesh['lon'=8,'chip'=8,'core'=2] {'lon','chip'}, dimensions={0} | all-to-all | bytes 655360 | tf_op jit(solution)/shard_map/all_to_all | solution.py:464
  98.5 14.9 %all_to_all.21 = f32[64,5,2,128]{3,2,1,0:T(2,128)S(1)} all-to-all(f32[64,5,2,128]{3,2,1,0:T(2,128)S(1)} %bitcast.9), channel_id=1, replica_groups=mesh['lon'=8,'chip'=8,'core'=2] {'lon','chip'}, dimensions={0} | all-to-all | bytes 655360 | tf_op jit(solution)/shard_map/all_to_all | solution.py:464
  113.4 3.0 %collective-permute-start.1 = (f32[640,128]{1,0:T(8,128)S(1)}, f32[640,128]{1,0:T(8,128)S(1)}, u32[]{:S(2)}, u32[]{:S(2)}) collective-permute-start(f32[640,128]{1,0:T(8,128)S(1)} %bitcast.10), channel_id=1, source_target_pairs={{0,1},{1,0},{2,3},{3,2},{4,5},{5,4},{6,7},{7,6},{8,9},{9,8},{10,11... | collective-permute-start | bytes 983048 | tf_op jit(solution)/shard_map/ppermute | solution.py:473
  116.4 0.8 turn.1.anomaly
  117.2 0.5 collective-permute-done.1.theirs
  117.6 15.6 %root_and_patterns.1 = (bf16[15,180,512]{2,1,0:T(8,128)(2,1)}, f32[512,512]{1,0:T(8,128)}) custom-call(s32[1]{0:T(128)} %bitcast.core, f32[640,128]{1,0:T(8,128)S(1)} %bitcast.11, f32[640,128]{1,0:T(8,128)S(1)} %collective-permute-done.1.theirs, bf16[2816,512]{1,0:T(8,128)(2,1)S(1)} %turn.1.anomaly), custom_call_target="tpu_custom_call" | custom-call | tf_op jit(solution)/shard_map/root_and_patterns/pallas_call | solution.py:434
  (3 shorter events, 0.1 us)
Async XLA Ops:
  1.9 15.5 %all-to-all-start = ((s32[16,1,128]{2,1,0:T(1,128)}), s32[16,1,128]{2,1,0:T(1,128)S(1)}, u32[]{:S(2)}, u32[]{:S(2)}) async-start(s32[16,1,128]{2,1,0:T(1,128)} %broadcast_in_dim.4), calls=%async_computation | async-start | bytes 16384 | tf_op jit(solution)/shard_map/all_to_all | solution.py:464
  17.4 0.6 copy-start
  30.2 10.4 %copy-start.1 = (s32[15,180]{1,0:T(8,128)S(1)}, s32[15,180]{1,0:T(8,128)}, u32[]{:S(2)}) copy-start(s32[15,180]{1,0:T(8,128)} %param.5) | copy-start | bytes 32404
  30.3 48.8 %all-to-all-start.1 = ((bf16[128,88,128]{2,1,0:T(8,128)(2,1)}), bf16[128,88,128]{2,1,0:T(8,128)(2,1)S(1)}, u32[]{:S(2)}, u32[]{:S(2)}) async-start(bf16[128,88,128]{2,1,0:T(8,128)(2,1)} %bitcast.12), calls=%async_computation.1 | async-start | bytes 5767168 | tf_op jit(solution)/shard_map/all_to_all | solution.py:464
  81.3 1.9 %collective-permute-start = (f32[640,128]{1,0:T(8,128)S(1)}, f32[640,128]{1,0:T(8,128)S(1)}, u32[]{:S(2)}, u32[]{:S(2)}) collective-permute-start(f32[640,128]{1,0:T(8,128)S(1)} %get-tuple-element.8), channel_id=1, source_target_pairs={{0,1},{1,0},{2,3},{3,2},{4,5},{5,4},{6,7},{7,6},{8,9},{9,8},{10,11... | collective-permute-start | bytes 983048 | tf_op jit(solution)/shard_map/ppermute | solution.py:473
  113.4 4.2 %collective-permute-start.1 = (f32[640,128]{1,0:T(8,128)S(1)}, f32[640,128]{1,0:T(8,128)S(1)}, u32[]{:S(2)}, u32[]{:S(2)}) collective-permute-start(f32[640,128]{1,0:T(8,128)S(1)} %bitcast.10), channel_id=1, source_target_pairs={{0,1},{1,0},{2,3},{3,2},{4,5},{5,4},{6,7},{7,6},{8,9},{9,8},{10,11... | collective-permute-start | bytes 983048 | tf_op jit(solution)/shard_map/ppermute | solution.py:473

commit v6 on v5

--- a/solution.py
+++ b/solution.py
@@ -1,3 +1,4 @@
+import functools
 import math
 
 import jax
@@ -28,11 +29,9 @@
 GROUPS = 22
 SECOND = 56
 TAIL = 112
-CHUNK = MON_DEV * GROUPS
+EARLY = 12
+LATE = GROUPS - EARLY
 WINDOWS = MON_DEV * N_LON
-SROWS = 3 * WINDOWS
-SSTRIDE = 97
-VSTRIDE = 89
 BLOCKS = [(i, j) for i in range(4) for j in range(i, 4)]
 PACK = len(BLOCKS)
 VMEM_LIMIT = 60 * 1024 * 1024
@@ -45,8 +44,10 @@
     return [float(t) for t in taps.astype(jnp.bfloat16).astype(np.float32)]
 
 
-def windows_kernel(field_hbm, out_hbm, field, windows, staged, in_sems, out_sems):
-    steps = windows.shape[0] // 16
+def windows_kernel(tiles, field_hbm, out_hbm, field, windows, staged, in_sems, out_sems):
+    steps = NLAT // 16
+    count = len(tiles) * WINDOWS
+    stride = count + 1
     lane16 = lax.broadcasted_iota(jnp.int32, (16, LANES), 1)
 
     def fetch(i):
@@ -68,17 +69,18 @@
             for l in range(N_LON):
                 start = (LON_DEV * l - HMAX) % NLON
                 first_tile, shift = start // LANES, start % LANES
-                tiles = [ring[:, t * LANES : (t + 1) * LANES] for t in range(first_tile, first_tile + 4)]
+                near = range(tiles[0], tiles[-1] + 2)
+                rolled = {t: ring[:, (first_tile + t) * LANES : (first_tile + t + 1) * LANES] for t in near}
                 if shift:
-                    tiles = [pltpu.roll(t, LANES - shift, 1) for t in tiles]
-                for j in range(3):
-                    piece = jnp.where(lane16 < LANES - shift, tiles[j], tiles[j + 1]) if shift else tiles[j]
+                    rolled = {t: pltpu.roll(v, LANES - shift, 1) for t, v in rolled.items()}
+                for n, j in enumerate(tiles):
+                    piece = jnp.where(lane16 < LANES - shift, rolled[j], rolled[j + 1]) if shift else rolled[j]
                     piece = piece.astype(jnp.float32)
                     for half in range(2):
-                        first = half * 8 * SSTRIDE + j * WINDOWS + m * N_LON + l
-                        staged[pl.ds(first, 8, stride=SSTRIDE), :] = piece[half * 8 : half * 8 + 8]
+                        first = half * 8 * stride + n * WINDOWS + m * N_LON + l
+                        staged[pl.ds(first, 8, stride=stride), :] = piece[half * 8 : half * 8 + 8]
         for r in range(16):
-            windows[i * 16 + r] = staged[r * SSTRIDE : r * SSTRIDE + SROWS, :].astype(jnp.bfloat16)
+            windows[i * 16 + r] = staged[r * stride : r * stride + count, :].astype(jnp.bfloat16)
         store(i).start()
         return carry
 
@@ -87,17 +89,18 @@
         store(i).wait()
 
 
-def cut_windows(field):
+def cut_windows(field, tiles):
     steps = NLAT // 16
+    count = len(tiles) * WINDOWS
     return pl.pallas_call(
-        windows_kernel,
-        out_shape=jax.ShapeDtypeStruct((steps * 16, SROWS, LANES), jnp.bfloat16),
+        functools.partial(windows_kernel, tiles),
+        out_shape=jax.ShapeDtypeStruct((NLAT, count, LANES), jnp.bfloat16),
         in_specs=[pl.BlockSpec(memory_space=pl.ANY)],
         out_specs=pl.BlockSpec(memory_space=pl.ANY),
         scratch_shapes=[
-            pltpu.VMEM((MON_DEV, steps * 16, NLON), jnp.bfloat16),
-            pltpu.VMEM((steps * 16, SROWS, LANES), jnp.bfloat16),
-            pltpu.VMEM((16 * SSTRIDE + 8, LANES), jnp.float32),
+            pltpu.VMEM((MON_DEV, NLAT, NLON), jnp.bfloat16),
+            pltpu.VMEM((NLAT, count, LANES), jnp.bfloat16),
+            pltpu.VMEM((16 * (count + 1) + 8, LANES), jnp.float32),
             pltpu.SemaphoreType.DMA((steps,)),
             pltpu.SemaphoreType.DMA((steps,)),
         ],
@@ -107,129 +110,204 @@
     )(field)
 
 
-def smooth_kernel(widths, windows_hbm, out_hbm, windows, out, taps, passed, staged, in_sems, out_sems):
-
-    def fetch(i):
-        rows = pl.ds(pl.multiple_of(i * 16, 16), 16)
-        return pltpu.make_async_copy(windows_hbm.at[rows], windows.at[rows], in_sems.at[i])
-
-    def store(b):
-        return pltpu.make_async_copy(out.at[:, b], out_hbm.at[:, b], out_sems.at[b])
-
-    for i in range(NLAT // 16):
-        fetch(i).start()
+def build_taps(widths, taps):
     lane8 = lax.broadcasted_iota(jnp.int32, (8, LANES), 1)
     sub8 = lax.broadcasted_iota(jnp.int32, (8, LANES), 0)
     offset = (lane8 - HMAX).astype(jnp.float32)
 
-    def build_taps(i, carry):
-        reach = jnp.zeros((8, LANES), jnp.int32)
-        for s in range(8):
-            r = i * 8 + s
-            reach = jnp.where(sub8 == s, widths[r // LAT_DEV, r % LAT_DEV], reach)
-        reach = reach.astype(jnp.float32)
-        spread = 0.5 * reach
-        value = jnp.exp(-(offset * offset) / (2.0 * spread * spread))
-        value = jnp.where(jnp.abs(offset) <= reach, value, 0.0)
-        total = jnp.sum(value, axis=1, keepdims=True) + value[:, 0:1]
-        value = (value / total).astype(jnp.bfloat16).astype(jnp.float32)
-        taps[pl.ds(pl.multiple_of(i * 8, 8), 8), :] = value
+    def band(b, carry):
+        for half in range(2):
+            reach = jnp.ones((8, LANES), jnp.int32)
+            for s in range(min(8, LAT_DEV - 8 * half)):
+                reach = jnp.where(sub8 == s, widths[b, 8 * half + s], reach)
+            reach = reach.astype(jnp.float32)
+            spread = 0.5 * reach
+            value = jnp.exp(-(offset * offset) / (2.0 * spread * spread))
+            value = jnp.where(jnp.abs(offset) <= reach, value, 0.0)
+            total = jnp.sum(value, axis=1, keepdims=True) + value[:, 0:1]
+            value = (value / total).astype(jnp.bfloat16).astype(jnp.float32)
+            taps[pl.ds(pl.multiple_of(b * 16 + 8 * half, 8), 8), :] = value
         return carry
 
-    lax.fori_loop(0, NLAT // 8, build_taps, 0, unroll=10)
-    edge = jnp.zeros((HL, 2 * WINDOWS, LANES), jnp.float32)
+    lax.fori_loop(0, N_LAT, band, 0, unroll=4)
+
+
+def filter_rows(taps, passed, lhs_of, emit, fetch):
+    edge = jnp.zeros((HL, WINDOWS, LANES), jnp.float32)
     passed[0:HL] = edge
     passed[NLAT + HL : NLAT + 2 * HL] = edge
     sub = lax.broadcasted_iota(jnp.int32, (LANES, LANES), 0)
     lane = lax.broadcasted_iota(jnp.int32, (LANES, LANES), 1)
     upper = jnp.where(sub >= lane, 1.0, 0.0).astype(jnp.bfloat16)
     lower = jnp.where(sub <= lane, 1.0, 0.0).astype(jnp.bfloat16)
+    w0, w1, w2 = lat_taps()[:3]
 
     def lon_band(b):
         for rr in range(LAT_DEV):
             r = b * LAT_DEV + rr
-            lhs = windows[r]
-            spread_taps = jnp.broadcast_to(taps[pl.ds(r, 1), :], (LANES, LANES))
+            spread_taps = jnp.broadcast_to(taps[pl.ds(b * 16 + rr, 1), :], (LANES, LANES))
             ring = pltpu.roll(spread_taps, 0, 1, stride=1, stride_axis=0).astype(jnp.bfloat16)
-            left = jnp.concatenate([lhs[: 2 * WINDOWS], lhs[WINDOWS:]], axis=1)
             right = jnp.concatenate([ring * upper, ring * lower], axis=0)
-            res = jnp.dot(left, right, preferred_element_type=jnp.float32)
+            res = jnp.dot(lhs_of(r), right, preferred_element_type=jnp.float32)
             passed[r + HL] = res.astype(jnp.bfloat16).astype(jnp.float32)
 
-    w0, w1, w2 = lat_taps()[:3]
-    laneb = lax.broadcasted_iota(jnp.int32, (WINDOWS, LANES), 1)
-
     def lat_band(b):
-        def smoothed(rr, lo, hi):
+        def smoothed(rr):
             r = b * LAT_DEV + rr
-            outer = passed[r, lo:hi] + passed[r + 4, lo:hi]
-            inner = passed[r + 1, lo:hi] + passed[r + 3, lo:hi]
-            return w0 * outer + w1 * inner + w2 * passed[r + 2, lo:hi]
-
-        def put(g, value):
-            for m in range(MON_DEV):
-                staged[pl.ds(m * GROUPS + g, N_LON, stride=VSTRIDE), :] = value[8 * m : 8 * m + 8]
-
-        for rr in range(LAT_DEV):
-            put(rr, smoothed(rr, 0, WINDOWS))
-        last = smoothed(LAT_DEV - 1, WINDOWS, 2 * WINDOWS)
-        for q in range(7):
-            even = smoothed(2 * q, WINDOWS, 2 * WINDOWS)
-            odd = smoothed(2 * q + 1, WINDOWS, 2 * WINDOWS)
-            value = jnp.where(laneb < SECOND, even, pltpu.roll(odd, SECOND, 1))
-            if q < 4:
-                tail = pltpu.roll(last, TAIL - 16 * q, 1)
-                value = jnp.where(laneb < TAIL, value, tail)
-            put(LAT_DEV + q, value)
-        for l in range(N_LON):
-            out[l, b] = staged[l * VSTRIDE : l * VSTRIDE + CHUNK, :].astype(jnp.bfloat16)
-
-    fetch(0).wait()
+            outer = passed[r] + passed[r + 4]
+            inner = passed[r + 1] + passed[r + 3]
+            return w0 * outer + w1 * inner + w2 * passed[r + 2]
+
+        emit(b, smoothed)
+
+    fetch(0)
     lon_band(0)
 
     def band(b, carry):
-        fetch(b).wait()
+        fetch(b)
         lon_band(b)
         lat_band(b - 1)
-        store(b - 1).start()
         return carry
 
     lax.fori_loop(1, N_LAT - 1, band, 0)
     lon_band(N_LAT - 1)
-    for b in (N_LAT - 2, N_LAT - 1):
-        lat_band(b)
-        store(b).start()
+    lat_band(N_LAT - 2)
+    lat_band(N_LAT - 1)
+
+
+def chunk_copy(out, out_hbm, sems, b):
+    return pltpu.make_async_copy(out.at[:, b], out_hbm.at[:, b], sems.at[b])
+
+
+def put(staged, groups, g, value):
+    for m in range(MON_DEV):
+        rows = pl.ds(m * groups + g, N_LON, stride=MON_DEV * groups + 1)
+        staged[rows, :] = value[8 * m : 8 * m + 8]
+
+
+def pack(staged, groups, out, b):
+    size = MON_DEV * groups
+    for l in range(N_LON):
+        out[l, b] = staged[l * (size + 1) : l * (size + 1) + size, :].astype(jnp.bfloat16)
+
+
+def early_kernel(widths, windows_hbm, out_hbm, extra, taps, windows, out, passed, staged, in_sems, out_sems):
+    def fetch(i):
+        rows = pl.ds(pl.multiple_of(i * 16, 16), 16)
+        return pltpu.make_async_copy(windows_hbm.at[rows], windows.at[rows], in_sems.at[i])
+
+    for i in range(NLAT // 16):
+        fetch(i).start()
+    build_taps(widths, taps)
+
+    def lhs_of(r):
+        both = windows[r]
+        return jnp.concatenate([both[:WINDOWS], both[WINDOWS:]], axis=1)
+
+    def emit(b, smoothed):
+        for rr in range(EARLY):
+            put(staged, EARLY, rr, smoothed(rr))
+        for rr in range(EARLY, LAT_DEV):
+            extra[b, rr - EARLY] = smoothed(rr).astype(jnp.bfloat16)
+        pack(staged, EARLY, out, b)
+        chunk_copy(out, out_hbm, out_sems, b).start()
+
+    filter_rows(taps, passed, lhs_of, emit, lambda i: fetch(i).wait())
     for b in range(N_LAT):
-        store(b).wait()
-
-
-def smooth(widths, windows):
-    out = pl.pallas_call(
-        smooth_kernel,
-        out_shape=jax.ShapeDtypeStruct((N_LON, N_LAT, CHUNK, LANES), jnp.bfloat16),
+        chunk_copy(out, out_hbm, out_sems, b).wait()
+
+
+def late_kernel(taps, extra, windows_hbm, third_hbm, out_hbm, second, third, out, passed, staged, in_sems, out_sems):
+    def fetch(i):
+        rows = pl.ds(pl.multiple_of(i * 16, 16), 16)
+        middle = windows_hbm.at[rows, WINDOWS : 2 * WINDOWS]
+        return (
+            pltpu.make_async_copy(middle, second.at[rows], in_sems.at[i, 0]),
+            pltpu.make_async_copy(third_hbm.at[rows], third.at[rows], in_sems.at[i, 1]),
+        )
+
+    def arrived(i):
+        for copy in fetch(i):
+            copy.wait()
+
+    for i in range(NLAT // 16):
+        for copy in fetch(i):
+            copy.start()
+    lane = lax.broadcasted_iota(jnp.int32, (WINDOWS, LANES), 1)
+
+    def lhs_of(r):
+        return jnp.concatenate([second[r], third[r]], axis=1)
+
+    def emit(b, smoothed):
+        for rr in range(EARLY, LAT_DEV):
+            put(staged, LATE, rr - EARLY, extra[b, rr - EARLY].astype(jnp.float32))
+        last = smoothed(LAT_DEV - 1)
+        for q in range(7):
+            value = jnp.where(lane < SECOND, smoothed(2 * q), pltpu.roll(smoothed(2 * q + 1), SECOND, 1))
+            if q < 4:
+                value = jnp.where(lane < TAIL, value, pltpu.roll(last, TAIL - 16 * q, 1))
+            put(staged, LATE, LAT_DEV - EARLY + q, value)
+        pack(staged, LATE, out, b)
+        chunk_copy(out, out_hbm, out_sems, b).start()
+
+    filter_rows(taps, passed, lhs_of, emit, arrived)
+    for b in range(N_LAT):
+        chunk_copy(out, out_hbm, out_sems, b).wait()
+
+
+def filter_scratch(groups):
+    size = MON_DEV * groups
+    return [
+        pltpu.VMEM((N_LON, N_LAT, size, LANES), jnp.bfloat16),
+        pltpu.VMEM((NLAT + 2 * HL, WINDOWS, LANES), jnp.float32),
+        pltpu.VMEM((N_LON * (size + 1) + 8, LANES), jnp.float32),
+    ]
+
+
+def smooth_early(widths, windows):
+    pieces, extra, taps = pl.pallas_call(
+        early_kernel,
+        out_shape=(
+            jax.ShapeDtypeStruct((N_LON, N_LAT, MON_DEV * EARLY, LANES), jnp.bfloat16),
+            jax.ShapeDtypeStruct((N_LAT, LAT_DEV - EARLY, WINDOWS, LANES), jnp.bfloat16),
+            jax.ShapeDtypeStruct((N_LAT * 16, LANES), jnp.float32),
+        ),
         in_specs=[pl.BlockSpec(memory_space=pltpu.SMEM), pl.BlockSpec(memory_space=pl.ANY)],
+        out_specs=(pl.BlockSpec(memory_space=pl.ANY),) + (pl.BlockSpec(memory_space=pltpu.VMEM),) * 2,
+        scratch_shapes=[pltpu.VMEM((NLAT, 2 * WINDOWS, LANES), jnp.bfloat16)]
+        + filter_scratch(EARLY)
+        + [pltpu.SemaphoreType.DMA((NLAT // 16,)), pltpu.SemaphoreType.DMA((N_LAT,))],
+        compiler_params=pltpu.CompilerParams(vmem_limit_bytes=VMEM_LIMIT),
+        name="smooth_early",
+    )(widths, windows)
+    return pieces.reshape(N_LON * N_LAT, MON_DEV * EARLY, LANES), extra, taps
+
+
+def smooth_late(taps, extra, windows, third):
+    pieces = pl.pallas_call(
+        late_kernel,
+        out_shape=jax.ShapeDtypeStruct((N_LON, N_LAT, MON_DEV * LATE, LANES), jnp.bfloat16),
+        in_specs=[pl.BlockSpec(memory_space=pltpu.VMEM)] * 2 + [pl.BlockSpec(memory_space=pl.ANY)] * 2,
         out_specs=pl.BlockSpec(memory_space=pl.ANY),
-        scratch_shapes=[
-            pltpu.VMEM((NLAT, SROWS, LANES), jnp.bfloat16),
-            pltpu.VMEM((N_LON, N_LAT, CHUNK, LANES), jnp.bfloat16),
-            pltpu.VMEM((NLAT, LANES), jnp.float32),
-            pltpu.VMEM((NLAT + 2 * HL, 2 * WINDOWS, LANES), jnp.float32),
-            pltpu.VMEM((N_LON * VSTRIDE + 8, LANES), jnp.float32),
-            pltpu.SemaphoreType.DMA((NLAT // 16,)),
-            pltpu.SemaphoreType.DMA((N_LAT,)),
-        ],
+        scratch_shapes=[pltpu.VMEM((NLAT, WINDOWS, LANES), jnp.bfloat16)] * 2
+        + filter_scratch(LATE)
+        + [pltpu.SemaphoreType.DMA((NLAT // 16, 2)), pltpu.SemaphoreType.DMA((N_LAT,))],
         compiler_params=pltpu.CompilerParams(vmem_limit_bytes=VMEM_LIMIT),
-        name="smooth",
-    )(widths, windows)
-    return out.reshape(N_LON * N_LAT, CHUNK, LANES)
-
-
-def gram_kernel(core, landed, weight, mine, theirs, anomaly, wide, square):
-    def widen(s, carry):
-        wide[pl.ds(pl.multiple_of(s * CHUNK, 8), CHUNK), :] = landed[s].astype(jnp.float32)
-        return carry
-
-    lax.fori_loop(0, N_LON * N_LAT, widen, 0, unroll=4)
+        cost_estimate=pl.CostEstimate(flops=8000000000, bytes_accessed=9000000, transcendentals=0),
+        name="smooth_late",
+    )(taps, extra, windows, third)
+    return pieces.reshape(N_LON * N_LAT, MON_DEV * LATE, LANES)
+
+
+def gram_kernel(core, early, late, weight, mine, theirs, anomaly, wide_early, wide_late, square):
+    for landed, wide, groups in ((early, wide_early, EARLY), (late, wide_late, LATE)):
+        size = MON_DEV * groups
+
+        def widen(s, carry):
+            wide[pl.ds(pl.multiple_of(s * size, 8), size), :] = landed[s].astype(jnp.float32)
+            return carry
+
+        lax.fori_loop(0, N_LON * N_LAT, widen, 0, unroll=4)
     lane = lax.broadcasted_iota(jnp.int32, (1, LANES), 1)
     for g in range(GROUPS):
         if g < LAT_DEV:
@@ -242,7 +320,10 @@
                 last = weight[LAT_DEV - 1 : LAT_DEV, LANES:]
                 last = jnp.where((lane >= 16 * q) & (lane < 16 * q + 16), last, 0.0)
                 scale = scale + pltpu.roll(last, TAIL - 16 * q, 1)
-        cells = wide[pl.ds(g, MONTHS, stride=GROUPS), :]
+        if g < EARLY:
+            cells = wide_early[pl.ds(g, MONTHS, stride=EARLY), :]
+        else:
+            cells = wide_late[pl.ds(g - EARLY, MONTHS, stride=LATE), :]
         mean = jnp.sum(cells, axis=0, keepdims=True) * (1.0 / MONTHS)
         anomaly[:, g * LANES : (g + 1) * LANES] = ((cells - mean) * scale).astype(jnp.bfloat16)
     for i, j in ((0, 0), (0, 1), (1, 1)):
@@ -261,7 +342,7 @@
                     ref[pl.ds(n, HALF, stride=PACK), :] = square[rows, :]
 
 
-def gram_terms(core, landed, weight):
+def gram_terms(core, early, late, weight):
     part = jax.ShapeDtypeStruct((HALF * PACK, LANES), jnp.float32)
     return pl.pallas_call(
         gram_kernel,
@@ -270,15 +351,17 @@
             pl.BlockSpec(memory_space=pltpu.SMEM),
             pl.BlockSpec(memory_space=pltpu.VMEM),
             pl.BlockSpec(memory_space=pltpu.VMEM),
+            pl.BlockSpec(memory_space=pltpu.VMEM),
         ],
         out_specs=(pl.BlockSpec(memory_space=pltpu.VMEM),) * 3,
         scratch_shapes=[
-            pltpu.VMEM((N_LON * N_LAT * CHUNK, LANES), jnp.float32),
+            pltpu.VMEM((MONTHS * EARLY, LANES), jnp.float32),
+            pltpu.VMEM((MONTHS * LATE, LANES), jnp.float32),
             pltpu.VMEM((LANES, LANES), jnp.float32),
         ],
         compiler_params=pltpu.CompilerParams(vmem_limit_bytes=32 * 1024 * 1024),
         name="gram_terms",
-    )(core, landed, weight)
+    )(core, early, late, weight)
 
 
 def turn_kernel(anomaly, turned):
@@ -474,16 +557,21 @@
 
 
 def local(monthly_field, half_width, land_mask):
-    widths = jnp.broadcast_to(jnp.pad(half_width, (0, LANES - LAT_DEV)), (N_LAT, 1, LANES))
-    widths = exchange(widths, LAT).reshape(N_LAT, LANES)
-    windows = cut_windows(monthly_field)
-    landed = exchange(smooth(widths, windows), BOTH)
+    widths = exchange(jnp.broadcast_to(half_width, (N_LAT, 1, LAT_DEV)), LAT).reshape(N_LAT, LAT_DEV)
+    windows = cut_windows(monthly_field, (0, 1))
+    pieces, extra, taps = smooth_early(widths, windows)
+    early = exchange(pieces, BOTH)
+    field, extra = lax.optimization_barrier((monthly_field, extra))
+    third = cut_windows(field, (2,))
+    pieces = smooth_late(taps, extra, windows, third)
+    early, pieces = lax.optimization_barrier((early, pieces))
+    late = exchange(pieces, BOTH)
     row_index = lax.axis_index(LAT) * LAT_DEV + jnp.arange(LAT_DEV)
     latitude = math.pi * ((row_index.astype(jnp.float32) + 0.5) / NLAT - 0.5)
     weight = jnp.sqrt(jnp.cos(latitude))[:, None] * land_mask.astype(jnp.float32)
     weight = jnp.pad(weight, ((0, 0), (0, 2 * LANES - LON_DEV)))
     core = lax.axis_index("core").reshape(1)
-    mine, theirs, anomaly = gram_terms(core, landed, weight)
+    mine, theirs, anomaly = gram_terms(core, early, late, weight)
     terms = exchange_packed(mine + swap_cores(theirs))
     turned = turn(anomaly)
     mine = exchange_packed(add_terms(terms))

time: 134 us -> 142 us (1.060)
  Pallas kernels: 38 us -> 49.7 us
  waiting for transfers between devices: 40.1 us -> 34.4 us
  starting transfers between devices: 22.3 us -> 25.4 us
    pallas_call x2 -> x4, Pallas kernels: 19.3 us -> 30.8 us  [the longest x1 10.8 us: smooth_late(): pl.pallas_call(late_kernel, out_shape=jax.ShapeDtypeStruct((N_LON, N_LAT,...]
    all_to_all x2 -> x3, waiting for transfers between devices: 38.4 us -> 32.7 us  [exchange(): return lax.all_to_all(pieces, axes, split_axis=0, concat_axis=0, tiled=True)]
    all_to_all x2 -> x3, starting transfers between devices: 18.7 us -> 21.6 us  [exchange(): return lax.all_to_all(pieces, axes, split_axis=0, concat_axis=0, tiled=True)]
  transfers between devices with their start and end apart: 4 -> 5, of which waited for: 3 -> 5; matrix products, arithmetic and copies ran while one was open for 0% -> 0% of each run, Pallas kernels for 6% -> 15%
where the time goes in v6:
time: 142 us
  Pallas kernels  49.7 us (35%)
  waiting for transfers between devices  34.4 us (24%)
  blocking collectives  29 us (20%)
  starting transfers between devices  25.4 us (18%)
  local copies, waits for them, and re-layouts  1.87 us (1%)
    all_to_all x3, waiting for transfers between devices, exchange(): return lax.all_to_all(pieces, axes, split_axis=0, concat_axis=0, tiled=True)  32.7 us
    all_to_all x2, blocking collectives, exchange(): return lax.all_to_all(pieces, axes, split_axis=0, concat_axis=0, tiled=True)  29 us
    all_to_all x3, starting transfers between devices, exchange(): return lax.all_to_all(pieces, axes, split_axis=0, concat_axis=0, tiled=True)  21.6 us
    pallas_call x1, Pallas kernels, root_and_patterns(): pl.pallas_call(root_kernel, out_shape=(jax.ShapeDtypeStruct((LAT_DEV, LON...  15.6 us
    pallas_call x1, Pallas kernels, smooth_late(): pl.pallas_call(late_kernel, out_shape=jax.ShapeDtypeStruct((N_LON, N_LAT,...  10.8 us
    pallas_call x1, Pallas kernels, smooth_early(): pl.pallas_call(early_kernel, out_shape=(jax.ShapeDtypeStruct((N_LON, N_LA...  10 us
    pallas_call x2, Pallas kernels, cut_windows(): pl.pallas_call(functools.partial(windows_kernel, tiles), out_shape=jax.Sh...  10 us
    ppermute x2, starting transfers between devices, swap_cores(): return lax.ppermute(x, 'core', [(0, 1), (1, 0)])  3.77 us
  transfers between devices with their start and end apart: 5, of which 5 were waited for; matrix products, arithmetic and copies ran while one was open for 0% of the time, Pallas kernels for 15%

profile of v6, /device:TPU:1, one launch (start us, length us, event | category | flops | bytes accessed | tf_op | source)
XLA Modules:
  0.0 141.5 jit_solution(14186275262022016237)
XLA Ops:
  0.6 1.3 broadcast_in_dim.4
  1.9 8.4 %all-to-all-start = ((s32[16,1,15]{2,1,0:T(1,128)}), s32[16,1,15]{2,1,0:T(1,128)S(1)}, u32[]{:S(2)}, u32[]{:S(2)}) async-start(s32[16,1,15]{2,1,0:T(1,128)} %broadcast_in_dim.4), calls=%async_computation | async-start | bytes 16384 | tf_op jit(solution)/shard_map/all_to_all | solution.py:547
  10.3 5.5 %cut_windows.2.windows_hbm = bf16[240,64,128]{2,1,0:T(8,128)(2,1)} custom-call(bf16[4,240,1440]{2,1,0:T(8,128)(2,1)} %field_hbm.2), custom_call_target="tpu_custom_call" | custom-call | flops 3000000000 | bytes 9000000 | tf_op jit(solution)/shard_map/cut_windows/pallas_call | solution.py:95
  15.8 1.4 %all-to-all-done = s32[16,1,15]{2,1,0:T(1,128)S(1)} async-done(((s32[16,1,15]{2,1,0:T(1,128)}), s32[16,1,15]{2,1,0:T(1,128)S(1)}, u32[]{:S(2)}, u32[]{:S(2)}) %all-to-all-start) | async-done | bytes 992 | tf_op jit(solution)/shard_map/all_to_all | solution.py:547
  17.2 0.0 copy-start
  17.2 0.6 copy-done
  17.8 10.0 %smooth_early.1 = (bf16[8,16,48,128]{3,2,1,0:T(8,128)(2,1)}, bf16[16,3,32,128]{3,2,1,0:T(8,128)(2,1)}, f32[256,128]{1,0:T(8,128)}) custom-call(s32[16,15]{1,0:T(8,128)} %bitcast.16, bf16[240,64,128]{2,1,0:T(8,128)(2,1)} %cut_windows.2.windows_hbm), custom_call_target="tpu_custom_call" | custom-call | tf_op jit(solution)/shard_map/smooth_early/pallas_call | solution.py:268
  27.9 8.9 %all-to-all-start.1 = ((bf16[128,48,128]{2,1,0:T(8,128)(2,1)}), bf16[128,48,128]{2,1,0:T(8,128)(2,1)S(1)}, u32[]{:S(2)}, u32[]{:S(2)}) async-start(bf16[128,48,128]{2,1,0:T(8,128)(2,1)} %bitcast.13), calls=%async_computation.1 | async-start | bytes 3145728 | tf_op jit(solution)/shard_map/all_to_all | solution.py:547
  36.8 4.5 %cut_windows.3.third_hbm = bf16[240,32,128]{2,1,0:T(8,128)(2,1)} custom-call(bf16[4,240,1440]{2,1,0:T(8,128)(2,1)} %field_hbm.2), custom_call_target="tpu_custom_call" | custom-call | flops 3000000000 | bytes 9000000 | tf_op jit(solution)/shard_map/cut_windows/pallas_call | solution.py:95
  41.3 0.0 copy-start.1
  41.3 10.8 %smooth_late.1 = bf16[8,16,40,128]{3,2,1,0:T(8,128)(2,1)} custom-call(f32[256,128]{1,0:T(8,128)} %get-tuple-element.15.taps, bf16[16,3,32,128]{3,2,1,0:T(8,128)(2,1)} %get-tuple-element.17.extra, bf16[240,64,128]{2,1,0:T(8,128)(2,1)} %cut_windows.2.windows_hbm, bf16[240,32,128]{2,1,0:T(8,128)(2,1)} %cut_windows.3.third_hbm), custom_call_target="tpu_custom_call" | custom-call | flops 8000000000 | bytes 9000000 | tf_op jit(solution)/shard_map/smooth_late/pallas_call | solution.py:287
  52.1 9.4 %all-to-all-done.1.early = bf16[128,48,128]{2,1,0:T(8,128)(2,1)S(1)} async-done(((bf16[128,48,128]{2,1,0:T(8,128)(2,1)}), bf16[128,48,128]{2,1,0:T(8,128)(2,1)S(1)}, u32[]{:S(2)}, u32[]{:S(2)}) %all-to-all-start.1) | async-done | bytes 1572896 | tf_op jit(solution)/shard_map/all_to_all | solution.py:547
  61.5 4.3 %all-to-all-start.2 = ((bf16[128,40,128]{2,1,0:T(8,128)(2,1)}), bf16[128,40,128]{2,1,0:T(8,128)(2,1)S(1)}, u32[]{:S(2)}, u32[]{:S(2)}) async-start(bf16[128,40,128]{2,1,0:T(8,128)(2,1)} %bitcast.14), calls=%async_computation.2 | async-start | bytes 2621440 | tf_op jit(solution)/shard_map/all_to_all | solution.py:547
  65.8 0.1 cosine_sqrt_fusion
  65.9 0.0 copy-done.1
  65.9 0.1 convert_multiply_fusion
  66.0 21.9 %all-to-all-done.2.late = bf16[128,40,128]{2,1,0:T(8,128)(2,1)S(1)} async-done(((bf16[128,40,128]{2,1,0:T(8,128)(2,1)}), bf16[128,40,128]{2,1,0:T(8,128)(2,1)S(1)}, u32[]{:S(2)}, u32[]{:S(2)}) %all-to-all-start.2) | async-done | bytes 1310752 | tf_op jit(solution)/shard_map/all_to_all | solution.py:547
  87.9 2.4 %gram_terms.1 = (f32[640,128]{1,0:T(8,128)S(1)}, f32[640,128]{1,0:T(8,128)S(1)}, bf16[512,2816]{1,0:T(8,128)(2,1)S(1)}) custom-call(s32[1]{0:T(128)} %bitcast.core, bf16[128,48,128]{2,1,0:T(8,128)(2,1)S(1)} %all-to-all-done.1.early, bf16[128,40,128]{2,1,0:T(8,128)(2,1)S(1)} %all-to-all-done.2.late, f32[15,256]{1,0:T(8,128)S(1)} %pad.4.weight), custom_call_target="tpu_custom_call" | custom-call | tf_op jit(solution)/shard_map/gram_terms/pallas_call | solution.py:347
  90.3 0.8 collective-permute-start
  91.1 1.3 collective-permute-done
  92.4 14.1 %all_to_all.25 = f32[64,5,2,128]{3,2,1,0:T(2,128)S(1)} all-to-all(f32[64,5,2,128]{3,2,1,0:T(2,128)S(1)} %bitcast.15), channel_id=1, replica_groups=mesh['lon'=8,'chip'=8,'core'=2] {'lon','chip'}, dimensions={0} | all-to-all | bytes 655360 | tf_op jit(solution)/shard_map/all_to_all | solution.py:547
  106.6 14.9 %all_to_all.26 = f32[64,5,2,128]{3,2,1,0:T(2,128)S(1)} all-to-all(f32[64,5,2,128]{3,2,1,0:T(2,128)S(1)} %bitcast.10), channel_id=1, replica_groups=mesh['lon'=8,'chip'=8,'core'=2] {'lon','chip'}, dimensions={0} | all-to-all | bytes 655360 | tf_op jit(solution)/shard_map/all_to_all | solution.py:547
  121.5 3.0 %collective-permute-start.1 = (f32[640,128]{1,0:T(8,128)S(1)}, f32[640,128]{1,0:T(8,128)S(1)}, u32[]{:S(2)}, u32[]{:S(2)}) collective-permute-start(f32[640,128]{1,0:T(8,128)S(1)} %bitcast.11), channel_id=1, source_target_pairs={{0,1},{1,0},{2,3},{3,2},{4,5},{5,4},{6,7},{7,6},{8,9},{9,8},{10,11... | collective-permute-start | bytes 983048 | tf_op jit(solution)/shard_map/ppermute | solution.py:556
  124.5 0.8 turn.1.anomaly
  125.3 0.5 collective-permute-done.1.theirs
  125.7 15.6 %root_and_patterns.1 = (bf16[15,180,512]{2,1,0:T(8,128)(2,1)}, f32[512,512]{1,0:T(8,128)}) custom-call(s32[1]{0:T(128)} %bitcast.core, f32[640,128]{1,0:T(8,128)S(1)} %bitcast.12, f32[640,128]{1,0:T(8,128)S(1)} %collective-permute-done.1.theirs, bf16[2816,512]{1,0:T(8,128)(2,1)S(1)} %turn.1.anomaly), custom_call_target="tpu_custom_call" | custom-call | tf_op jit(solution)/shard_map/root_and_patterns/pallas_call | solution.py:517
  (3 shorter events, 0.1 us)
Async XLA Ops:
  1.9 15.4 %all-to-all-start = ((s32[16,1,15]{2,1,0:T(1,128)}), s32[16,1,15]{2,1,0:T(1,128)S(1)}, u32[]{:S(2)}, u32[]{:S(2)}) async-start(s32[16,1,15]{2,1,0:T(1,128)} %broadcast_in_dim.4), calls=%async_computation | async-start | bytes 16384 | tf_op jit(solution)/shard_map/all_to_all | solution.py:547
  17.2 0.6 copy-start
  27.9 33.6 %all-to-all-start.1 = ((bf16[128,48,128]{2,1,0:T(8,128)(2,1)}), bf16[128,48,128]{2,1,0:T(8,128)(2,1)S(1)}, u32[]{:S(2)}, u32[]{:S(2)}) async-start(bf16[128,48,128]{2,1,0:T(8,128)(2,1)} %bitcast.13), calls=%async_computation.1 | async-start | bytes 3145728 | tf_op jit(solution)/shard_map/all_to_all | solution.py:547
  41.3 24.6 %copy-start.1 = (s32[15,180]{1,0:T(8,128)S(1)}, s32[15,180]{1,0:T(8,128)}, u32[]{:S(2)}) copy-start(s32[15,180]{1,0:T(8,128)} %param.5) | copy-start | bytes 32404
  61.5 26.3 %all-to-all-start.2 = ((bf16[128,40,128]{2,1,0:T(8,128)(2,1)}), bf16[128,40,128]{2,1,0:T(8,128)(2,1)S(1)}, u32[]{:S(2)}, u32[]{:S(2)}) async-start(bf16[128,40,128]{2,1,0:T(8,128)(2,1)} %bitcast.14), calls=%async_computation.2 | async-start | bytes 2621440 | tf_op jit(solution)/shard_map/all_to_all | solution.py:547
  90.3 2.0 %collective-permute-start = (f32[640,128]{1,0:T(8,128)S(1)}, f32[640,128]{1,0:T(8,128)S(1)}, u32[]{:S(2)}, u32[]{:S(2)}) collective-permute-start(f32[640,128]{1,0:T(8,128)S(1)} %get-tuple-element.22), channel_id=1, source_target_pairs={{0,1},{1,0},{2,3},{3,2},{4,5},{5,4},{6,7},{7,6},{8,9},{9,8},{10,11... | collective-permute-start | bytes 983048 | tf_op jit(solution)/shard_map/ppermute | solution.py:556
  121.5 4.2 %collective-permute-start.1 = (f32[640,128]{1,0:T(8,128)S(1)}, f32[640,128]{1,0:T(8,128)S(1)}, u32[]{:S(2)}, u32[]{:S(2)}) collective-permute-start(f32[640,128]{1,0:T(8,128)S(1)} %bitcast.11), channel_id=1, source_target_pairs={{0,1},{1,0},{2,3},{3,2},{4,5},{5,4},{6,7},{7,6},{8,9},{9,8},{10,11... | collective-permute-start | bytes 983048 | tf_op jit(solution)/shard_map/ppermute | solution.py:556

commit v7 on v5

--- a/solution.py
+++ b/solution.py
@@ -107,7 +107,7 @@
     )(field)
 
 
-def smooth_kernel(widths, windows_hbm, out_hbm, windows, out, taps, passed, staged, in_sems, out_sems):
+def smooth_kernel(widths, windows_hbm, out_hbm, windows, out, taps, table, passed, staged, in_sems, out_sems):
 
     def fetch(i):
         rows = pl.ds(pl.multiple_of(i * 16, 16), 16)
@@ -118,41 +118,36 @@
 
     for i in range(NLAT // 16):
         fetch(i).start()
-    lane8 = lax.broadcasted_iota(jnp.int32, (8, LANES), 1)
-    sub8 = lax.broadcasted_iota(jnp.int32, (8, LANES), 0)
-    offset = (lane8 - HMAX).astype(jnp.float32)
-
-    def build_taps(i, carry):
-        reach = jnp.zeros((8, LANES), jnp.int32)
-        for s in range(8):
-            r = i * 8 + s
-            reach = jnp.where(sub8 == s, widths[r // LAT_DEV, r % LAT_DEV], reach)
-        reach = reach.astype(jnp.float32)
-        spread = 0.5 * reach
-        value = jnp.exp(-(offset * offset) / (2.0 * spread * spread))
-        value = jnp.where(jnp.abs(offset) <= reach, value, 0.0)
-        total = jnp.sum(value, axis=1, keepdims=True) + value[:, 0:1]
-        value = (value / total).astype(jnp.bfloat16).astype(jnp.float32)
-        taps[pl.ds(pl.multiple_of(i * 8, 8), 8), :] = value
-        return carry
-
-    lax.fori_loop(0, NLAT // 8, build_taps, 0, unroll=10)
-    edge = jnp.zeros((HL, 2 * WINDOWS, LANES), jnp.float32)
-    passed[0:HL] = edge
-    passed[NLAT + HL : NLAT + 2 * HL] = edge
+    reach = (lax.broadcasted_iota(jnp.int32, (HMAX, LANES), 0) + 1).astype(jnp.float32)
+    offset = (lax.broadcasted_iota(jnp.int32, (HMAX, LANES), 1) - HMAX).astype(jnp.float32)
+    spread = 0.5 * reach
+    value = jnp.exp(-(offset * offset) / (2.0 * spread * spread))
+    value = jnp.where(jnp.abs(offset) <= reach, value, 0.0)
+    total = jnp.sum(value, axis=1, keepdims=True) + value[:, 0:1]
+    taps[...] = (value / total).astype(jnp.bfloat16).astype(jnp.float32)
     sub = lax.broadcasted_iota(jnp.int32, (LANES, LANES), 0)
     lane = lax.broadcasted_iota(jnp.int32, (LANES, LANES), 1)
     upper = jnp.where(sub >= lane, 1.0, 0.0).astype(jnp.bfloat16)
     lower = jnp.where(sub <= lane, 1.0, 0.0).astype(jnp.bfloat16)
 
+    def build_matrix(h, carry):
+        spread_taps = jnp.broadcast_to(taps[pl.ds(h, 1), :], (LANES, LANES))
+        ring = pltpu.roll(spread_taps, 0, 1, stride=1, stride_axis=0).astype(jnp.bfloat16)
+        table[h, 0:LANES, :] = ring * upper
+        table[h, LANES:, :] = ring * lower
+        return carry
+
+    lax.fori_loop(0, HMAX, build_matrix, 0, unroll=8)
+    edge = jnp.zeros((HL, 2 * WINDOWS, LANES), jnp.float32)
+    passed[0:HL] = edge
+    passed[NLAT + HL : NLAT + 2 * HL] = edge
+
     def lon_band(b):
         for rr in range(LAT_DEV):
             r = b * LAT_DEV + rr
             lhs = windows[r]
-            spread_taps = jnp.broadcast_to(taps[pl.ds(r, 1), :], (LANES, LANES))
-            ring = pltpu.roll(spread_taps, 0, 1, stride=1, stride_axis=0).astype(jnp.bfloat16)
             left = jnp.concatenate([lhs[: 2 * WINDOWS], lhs[WINDOWS:]], axis=1)
-            right = jnp.concatenate([ring * upper, ring * lower], axis=0)
+            right = table[widths[b, rr] - 1]
             res = jnp.dot(left, right, preferred_element_type=jnp.float32)
             passed[r + HL] = res.astype(jnp.bfloat16).astype(jnp.float32)
 
@@ -212,7 +207,8 @@
         scratch_shapes=[
             pltpu.VMEM((NLAT, SROWS, LANES), jnp.bfloat16),
             pltpu.VMEM((N_LON, N_LAT, CHUNK, LANES), jnp.bfloat16),
-            pltpu.VMEM((NLAT, LANES), jnp.float32),
+            pltpu.VMEM((HMAX, LANES), jnp.float32),
+            pltpu.VMEM((HMAX, 2 * LANES, LANES), jnp.bfloat16),
             pltpu.VMEM((NLAT + 2 * HL, 2 * WINDOWS, LANES), jnp.float32),
             pltpu.VMEM((N_LON * VSTRIDE + 8, LANES), jnp.float32),
             pltpu.SemaphoreType.DMA((NLAT // 16,)),
@@ -474,8 +470,7 @@
 
 
 def local(monthly_field, half_width, land_mask):
-    widths = jnp.broadcast_to(jnp.pad(half_width, (0, LANES - LAT_DEV)), (N_LAT, 1, LANES))
-    widths = exchange(widths, LAT).reshape(N_LAT, LANES)
+    widths = exchange(jnp.broadcast_to(half_width, (N_LAT, 1, LAT_DEV)), LAT).reshape(N_LAT, LAT_DEV)
     windows = cut_windows(monthly_field)
     landed = exchange(smooth(widths, windows), BOTH)
     row_index = lax.axis_index(LAT) * LAT_DEV + jnp.arange(LAT_DEV)

time: 134 us -> 132 us (0.985)
  Pallas kernels: 38 us -> 36.2 us
    pallas_call x1, Pallas kernels: 12.3 us -> 10.5 us  [smooth(): pl.pallas_call(smooth_kernel, out_shape=jax.ShapeDtypeStruct((N_LON, N_LA...]
where the time goes in v7:
time: 132 us
  waiting for transfers between devices  40.1 us (30%)
  Pallas kernels  36.2 us (27%)
  blocking collectives  30.1 us (23%)
  starting transfers between devices  22.3 us (17%)
  local copies, waits for them, and re-layouts  1.87 us (1%)
    all_to_all x2, waiting for transfers between devices, exchange(): return lax.all_to_all(pieces, axes, split_axis=0, concat_axis=0, tiled=True)  38.4 us
    all_to_all x2, blocking collectives, exchange(): return lax.all_to_all(pieces, axes, split_axis=0, concat_axis=0, tiled=True)  30.1 us
    all_to_all x2, starting transfers between devices, exchange(): return lax.all_to_all(pieces, axes, split_axis=0, concat_axis=0, tiled=True)  18.7 us
    pallas_call x1, Pallas kernels, root_and_patterns(): pl.pallas_call(root_kernel, out_shape=(jax.ShapeDtypeStruct((LAT_DEV, LON...  15.6 us
    pallas_call x1, Pallas kernels, smooth(): pl.pallas_call(smooth_kernel, out_shape=jax.ShapeDtypeStruct((N_LON, N_LA...  10.5 us
    pallas_call x1, Pallas kernels, cut_windows(): pl.pallas_call(windows_kernel, out_shape=jax.ShapeDtypeStruct((steps * 16...  7 us
    ppermute x2, starting transfers between devices, swap_cores(): return lax.ppermute(x, 'core', [(0, 1), (1, 0)])  3.6 us
  transfers between devices with their start and end apart: 4, of which 3 were waited for; matrix products, arithmetic and copies ran while one was open for 0% of the time, Pallas kernels for 6%

profile of v7, /device:TPU:1, one launch (start us, length us, event | category | flops | bytes accessed | tf_op | source)
XLA Modules:
  0.0 131.6 jit_solution(12151597970846962982)
XLA Ops:
  0.6 1.3 broadcast_in_dim.4
  1.9 8.4 %all-to-all-start = ((s32[16,1,15]{2,1,0:T(1,128)}), s32[16,1,15]{2,1,0:T(1,128)S(1)}, u32[]{:S(2)}, u32[]{:S(2)}) async-start(s32[16,1,15]{2,1,0:T(1,128)} %broadcast_in_dim.4), calls=%async_computation | async-start | bytes 16384 | tf_op jit(solution)/shard_map/all_to_all | solution.py:460
  10.3 7.0 %cut_windows.1.windows_hbm = bf16[240,96,128]{2,1,0:T(8,128)(2,1)} custom-call(bf16[4,240,1440]{2,1,0:T(8,128)(2,1)} %field_hbm.1), custom_call_target="tpu_custom_call" | custom-call | flops 3000000000 | bytes 9000000 | tf_op jit(solution)/shard_map/cut_windows/pallas_call | solution.py:92
  17.3 0.0 all-to-all-done
  17.4 0.0 copy-start
  17.4 0.6 copy-done
  18.0 10.5 %smooth.1 = bf16[8,16,88,128]{3,2,1,0:T(8,128)(2,1)} custom-call(s32[16,15]{1,0:T(8,128)} %bitcast.14, bf16[240,96,128]{2,1,0:T(8,128)(2,1)} %cut_windows.1.windows_hbm), custom_call_target="tpu_custom_call" | custom-call | tf_op jit(solution)/shard_map/smooth/pallas_call | solution.py:202
  28.5 0.0 copy-start.1
  28.5 10.3 %all-to-all-start.1 = ((bf16[128,88,128]{2,1,0:T(8,128)(2,1)}), bf16[128,88,128]{2,1,0:T(8,128)(2,1)S(1)}, u32[]{:S(2)}, u32[]{:S(2)}) async-start(bf16[128,88,128]{2,1,0:T(8,128)(2,1)} %bitcast.12), calls=%async_computation.1 | async-start | bytes 5767168 | tf_op jit(solution)/shard_map/all_to_all | solution.py:460
  38.8 0.1 cosine_sqrt_fusion
  38.8 0.0 copy-done.1
  38.8 0.1 convert_multiply_fusion
  38.9 38.4 %all-to-all-done.1.landed = bf16[128,88,128]{2,1,0:T(8,128)(2,1)S(1)} async-done(((bf16[128,88,128]{2,1,0:T(8,128)(2,1)}), bf16[128,88,128]{2,1,0:T(8,128)(2,1)S(1)}, u32[]{:S(2)}, u32[]{:S(2)}) %all-to-all-start.1) | async-done | bytes 2883616 | tf_op jit(solution)/shard_map/all_to_all | solution.py:460
  77.3 2.3 %gram_terms.1 = (f32[640,128]{1,0:T(8,128)S(1)}, f32[640,128]{1,0:T(8,128)S(1)}, bf16[512,2816]{1,0:T(8,128)(2,1)S(1)}) custom-call(s32[1]{0:T(128)} %bitcast.core, bf16[128,88,128]{2,1,0:T(8,128)(2,1)S(1)} %all-to-all-done.1.landed, f32[15,256]{1,0:T(8,128)S(1)} %pad.4.weight), custom_call_target="tpu_custom_call" | custom-call | tf_op jit(solution)/shard_map/gram_terms/pallas_call | solution.py:262
  79.6 0.6 collective-permute-start
  80.2 1.3 collective-permute-done
  81.5 15.2 %all_to_all.20 = f32[64,5,2,128]{3,2,1,0:T(2,128)S(1)} all-to-all(f32[64,5,2,128]{3,2,1,0:T(2,128)S(1)} %bitcast.13), channel_id=1, replica_groups=mesh['lon'=8,'chip'=8,'core'=2] {'lon','chip'}, dimensions={0} | all-to-all | bytes 655360 | tf_op jit(solution)/shard_map/all_to_all | solution.py:460
  96.7 14.9 %all_to_all.21 = f32[64,5,2,128]{3,2,1,0:T(2,128)S(1)} all-to-all(f32[64,5,2,128]{3,2,1,0:T(2,128)S(1)} %bitcast.9), channel_id=1, replica_groups=mesh['lon'=8,'chip'=8,'core'=2] {'lon','chip'}, dimensions={0} | all-to-all | bytes 655360 | tf_op jit(solution)/shard_map/all_to_all | solution.py:460
  111.6 3.0 %collective-permute-start.1 = (f32[640,128]{1,0:T(8,128)S(1)}, f32[640,128]{1,0:T(8,128)S(1)}, u32[]{:S(2)}, u32[]{:S(2)}) collective-permute-start(f32[640,128]{1,0:T(8,128)S(1)} %bitcast.10), channel_id=1, source_target_pairs={{0,1},{1,0},{2,3},{3,2},{4,5},{5,4},{6,7},{7,6},{8,9},{9,8},{10,11... | collective-permute-start | bytes 983048 | tf_op jit(solution)/shard_map/ppermute | solution.py:469
  114.6 0.8 turn.1.anomaly
  115.4 0.5 collective-permute-done.1.theirs
  115.9 15.6 %root_and_patterns.1 = (bf16[15,180,512]{2,1,0:T(8,128)(2,1)}, f32[512,512]{1,0:T(8,128)}) custom-call(s32[1]{0:T(128)} %bitcast.core, f32[640,128]{1,0:T(8,128)S(1)} %bitcast.11, f32[640,128]{1,0:T(8,128)S(1)} %collective-permute-done.1.theirs, bf16[2816,512]{1,0:T(8,128)(2,1)S(1)} %turn.1.anomaly), custom_call_target="tpu_custom_call" | custom-call | tf_op jit(solution)/shard_map/root_and_patterns/pallas_call | solution.py:430
  (3 shorter events, 0.1 us)
Async XLA Ops:
  1.9 15.5 %all-to-all-start = ((s32[16,1,15]{2,1,0:T(1,128)}), s32[16,1,15]{2,1,0:T(1,128)S(1)}, u32[]{:S(2)}, u32[]{:S(2)}) async-start(s32[16,1,15]{2,1,0:T(1,128)} %broadcast_in_dim.4), calls=%async_computation | async-start | bytes 16384 | tf_op jit(solution)/shard_map/all_to_all | solution.py:460
  17.4 0.6 copy-start
  28.5 10.4 %copy-start.1 = (s32[15,180]{1,0:T(8,128)S(1)}, s32[15,180]{1,0:T(8,128)}, u32[]{:S(2)}) copy-start(s32[15,180]{1,0:T(8,128)} %param.5) | copy-start | bytes 32404
  28.5 48.8 %all-to-all-start.1 = ((bf16[128,88,128]{2,1,0:T(8,128)(2,1)}), bf16[128,88,128]{2,1,0:T(8,128)(2,1)S(1)}, u32[]{:S(2)}, u32[]{:S(2)}) async-start(bf16[128,88,128]{2,1,0:T(8,128)(2,1)} %bitcast.12), calls=%async_computation.1 | async-start | bytes 5767168 | tf_op jit(solution)/shard_map/all_to_all | solution.py:460
  79.6 1.9 %collective-permute-start = (f32[640,128]{1,0:T(8,128)S(1)}, f32[640,128]{1,0:T(8,128)S(1)}, u32[]{:S(2)}, u32[]{:S(2)}) collective-permute-start(f32[640,128]{1,0:T(8,128)S(1)} %get-tuple-element.8), channel_id=1, source_target_pairs={{0,1},{1,0},{2,3},{3,2},{4,5},{5,4},{6,7},{7,6},{8,9},{9,8},{10,11... | collective-permute-start | bytes 983048 | tf_op jit(solution)/shard_map/ppermute | solution.py:469
  111.6 4.2 %collective-permute-start.1 = (f32[640,128]{1,0:T(8,128)S(1)}, f32[640,128]{1,0:T(8,128)S(1)}, u32[]{:S(2)}, u32[]{:S(2)}) collective-permute-start(f32[640,128]{1,0:T(8,128)S(1)} %bitcast.10), channel_id=1, source_target_pairs={{0,1},{1,0},{2,3},{3,2},{4,5},{5,4},{6,7},{7,6},{8,9},{9,8},{10,11... | collective-permute-start | bytes 983048 | tf_op jit(solution)/shard_map/ppermute | solution.py:469

commit v8 on v7

--- a/solution.py
+++ b/solution.py
@@ -107,7 +107,10 @@
     )(field)
 
 
-def smooth_kernel(widths, windows_hbm, out_hbm, windows, out, taps, table, passed, staged, in_sems, out_sems):
+def smooth_kernel(widths_in, windows_hbm, out_hbm, widths, windows, out, taps, table, passed, staged, in_sems, out_sems, sem):
+    bring = pltpu.make_async_copy(widths_in, widths, sem)
+    bring.start()
+
 
     def fetch(i):
         rows = pl.ds(pl.multiple_of(i * 16, 16), 16)
@@ -179,18 +182,22 @@
         for l in range(N_LON):
             out[l, b] = staged[l * VSTRIDE : l * VSTRIDE + CHUNK, :].astype(jnp.bfloat16)
 
-    fetch(0).wait()
-    lon_band(0)
+    bring.wait()
+    for b in range(2):
+        fetch(b).wait()
+        lon_band(b)
 
     def band(b, carry):
         fetch(b).wait()
+        lat_band(b - 2)
         lon_band(b)
-        lat_band(b - 1)
-        store(b - 1).start()
+        store(b - 2).start()
         return carry
 
-    lax.fori_loop(1, N_LAT - 1, band, 0)
+    lax.fori_loop(2, N_LAT - 1, band, 0)
+    lat_band(N_LAT - 3)
     lon_band(N_LAT - 1)
+    store(N_LAT - 3).start()
     for b in (N_LAT - 2, N_LAT - 1):
         lat_band(b)
         store(b).start()
@@ -202,9 +209,10 @@
     out = pl.pallas_call(
         smooth_kernel,
         out_shape=jax.ShapeDtypeStruct((N_LON, N_LAT, CHUNK, LANES), jnp.bfloat16),
-        in_specs=[pl.BlockSpec(memory_space=pltpu.SMEM), pl.BlockSpec(memory_space=pl.ANY)],
+        in_specs=[pl.BlockSpec(memory_space=pltpu.VMEM), pl.BlockSpec(memory_space=pl.ANY)],
         out_specs=pl.BlockSpec(memory_space=pl.ANY),
         scratch_shapes=[
+            pltpu.SMEM((N_LAT, LAT_DEV), jnp.int32),
             pltpu.VMEM((NLAT, SROWS, LANES), jnp.bfloat16),
             pltpu.VMEM((N_LON, N_LAT, CHUNK, LANES), jnp.bfloat16),
             pltpu.VMEM((HMAX, LANES), jnp.float32),
@@ -213,6 +221,7 @@
             pltpu.VMEM((N_LON * VSTRIDE + 8, LANES), jnp.float32),
             pltpu.SemaphoreType.DMA((NLAT // 16,)),
             pltpu.SemaphoreType.DMA((N_LAT,)),
+            pltpu.SemaphoreType.DMA,
         ],
         compiler_params=pltpu.CompilerParams(vmem_limit_bytes=VMEM_LIMIT),
         name="smooth",

time: 132 us -> 131 us (level)
  no operation moved by 1% of the time
where the time goes in v8:
time: 131 us; the launch traced here: 130 us
  waiting for transfers between devices  40.1 us (31%)
  Pallas kernels  35.1 us (27%)
  blocking collectives  30.1 us (23%)
  starting transfers between devices  22.3 us (17%)
  local copies, waits for them, and re-layouts  1.87 us (1%)
    all_to_all x2, waiting for transfers between devices, exchange(): return lax.all_to_all(pieces, axes, split_axis=0, concat_axis=0, tiled=True)  38.4 us
    all_to_all x2, blocking collectives, exchange(): return lax.all_to_all(pieces, axes, split_axis=0, concat_axis=0, tiled=True)  30.1 us
    all_to_all x2, starting transfers between devices, exchange(): return lax.all_to_all(pieces, axes, split_axis=0, concat_axis=0, tiled=True)  18.7 us
    pallas_call x1, Pallas kernels, root_and_patterns(): pl.pallas_call(root_kernel, out_shape=(jax.ShapeDtypeStruct((LAT_DEV, LON...  15.6 us
    pallas_call x1, Pallas kernels, smooth(): pl.pallas_call(smooth_kernel, out_shape=jax.ShapeDtypeStruct((N_LON, N_LA...  9.34 us
    pallas_call x1, Pallas kernels, cut_windows(): pl.pallas_call(windows_kernel, out_shape=jax.ShapeDtypeStruct((steps * 16...  7 us
    ppermute x2, starting transfers between devices, swap_cores(): return lax.ppermute(x, 'core', [(0, 1), (1, 0)])  3.6 us
  transfers between devices with their start and end apart: 4, of which 3 were waited for; matrix products, arithmetic and copies ran while one was open for 0% of the time, Pallas kernels for 6%

profile of v8, /device:TPU:1, one launch (start us, length us, event | category | flops | bytes accessed | tf_op | source)
XLA Modules:
  0.0 130.5 jit_solution(18108997513502375386)
XLA Ops:
  0.6 1.3 broadcast_in_dim.4
  1.9 8.4 %all-to-all-start = ((s32[16,1,15]{2,1,0:T(1,128)}), s32[16,1,15]{2,1,0:T(1,128)S(1)}, u32[]{:S(2)}, u32[]{:S(2)}) async-start(s32[16,1,15]{2,1,0:T(1,128)} %broadcast_in_dim.4), calls=%async_computation | async-start | bytes 16384 | tf_op jit(solution)/shard_map/all_to_all | solution.py:469
  10.3 7.0 %cut_windows.1.windows_hbm = bf16[240,96,128]{2,1,0:T(8,128)(2,1)} custom-call(bf16[4,240,1440]{2,1,0:T(8,128)(2,1)} %field_hbm.1), custom_call_target="tpu_custom_call" | custom-call | flops 3000000000 | bytes 9000000 | tf_op jit(solution)/shard_map/cut_windows/pallas_call | solution.py:92
  17.3 0.0 all-to-all-done
  17.4 0.0 copy-start
  17.4 0.6 copy-done
  18.0 9.3 %smooth.1 = bf16[8,16,88,128]{3,2,1,0:T(8,128)(2,1)} custom-call(s32[16,15]{1,0:T(8,128)} %bitcast.14, bf16[240,96,128]{2,1,0:T(8,128)(2,1)} %cut_windows.1.windows_hbm), custom_call_target="tpu_custom_call" | custom-call | tf_op jit(solution)/shard_map/smooth/pallas_call | solution.py:209
  27.3 0.0 copy-start.1
  27.3 10.3 %all-to-all-start.1 = ((bf16[128,88,128]{2,1,0:T(8,128)(2,1)}), bf16[128,88,128]{2,1,0:T(8,128)(2,1)S(1)}, u32[]{:S(2)}, u32[]{:S(2)}) async-start(bf16[128,88,128]{2,1,0:T(8,128)(2,1)} %bitcast.12), calls=%async_computation.1 | async-start | bytes 5767168 | tf_op jit(solution)/shard_map/all_to_all | solution.py:469
  37.6 0.1 cosine_sqrt_fusion
  37.6 0.0 copy-done.1
  37.7 0.1 convert_multiply_fusion
  37.7 38.4 %all-to-all-done.1.landed = bf16[128,88,128]{2,1,0:T(8,128)(2,1)S(1)} async-done(((bf16[128,88,128]{2,1,0:T(8,128)(2,1)}), bf16[128,88,128]{2,1,0:T(8,128)(2,1)S(1)}, u32[]{:S(2)}, u32[]{:S(2)}) %all-to-all-start.1) | async-done | bytes 2883616 | tf_op jit(solution)/shard_map/all_to_all | solution.py:469
  76.1 2.3 %gram_terms.1 = (f32[640,128]{1,0:T(8,128)S(1)}, f32[640,128]{1,0:T(8,128)S(1)}, bf16[512,2816]{1,0:T(8,128)(2,1)S(1)}) custom-call(s32[1]{0:T(128)} %bitcast.core, bf16[128,88,128]{2,1,0:T(8,128)(2,1)S(1)} %all-to-all-done.1.landed, f32[15,256]{1,0:T(8,128)S(1)} %pad.4.weight), custom_call_target="tpu_custom_call" | custom-call | tf_op jit(solution)/shard_map/gram_terms/pallas_call | solution.py:271
  78.4 0.6 collective-permute-start
  79.0 1.3 collective-permute-done
  80.3 15.2 %all_to_all.20 = f32[64,5,2,128]{3,2,1,0:T(2,128)S(1)} all-to-all(f32[64,5,2,128]{3,2,1,0:T(2,128)S(1)} %bitcast.13), channel_id=1, replica_groups=mesh['lon'=8,'chip'=8,'core'=2] {'lon','chip'}, dimensions={0} | all-to-all | bytes 655360 | tf_op jit(solution)/shard_map/all_to_all | solution.py:469
  95.5 14.9 %all_to_all.21 = f32[64,5,2,128]{3,2,1,0:T(2,128)S(1)} all-to-all(f32[64,5,2,128]{3,2,1,0:T(2,128)S(1)} %bitcast.9), channel_id=1, replica_groups=mesh['lon'=8,'chip'=8,'core'=2] {'lon','chip'}, dimensions={0} | all-to-all | bytes 655360 | tf_op jit(solution)/shard_map/all_to_all | solution.py:469
  110.5 3.0 %collective-permute-start.1 = (f32[640,128]{1,0:T(8,128)S(1)}, f32[640,128]{1,0:T(8,128)S(1)}, u32[]{:S(2)}, u32[]{:S(2)}) collective-permute-start(f32[640,128]{1,0:T(8,128)S(1)} %bitcast.10), channel_id=1, source_target_pairs={{0,1},{1,0},{2,3},{3,2},{4,5},{5,4},{6,7},{7,6},{8,9},{9,8},{10,11... | collective-permute-start | bytes 983048 | tf_op jit(solution)/shard_map/ppermute | solution.py:478
  113.4 0.8 turn.1.anomaly
  114.2 0.5 collective-permute-done.1.theirs
  114.7 15.6 %root_and_patterns.1 = (bf16[15,180,512]{2,1,0:T(8,128)(2,1)}, f32[512,512]{1,0:T(8,128)}) custom-call(s32[1]{0:T(128)} %bitcast.core, f32[640,128]{1,0:T(8,128)S(1)} %bitcast.11, f32[640,128]{1,0:T(8,128)S(1)} %collective-permute-done.1.theirs, bf16[2816,512]{1,0:T(8,128)(2,1)S(1)} %turn.1.anomaly), custom_call_target="tpu_custom_call" | custom-call | tf_op jit(solution)/shard_map/root_and_patterns/pallas_call | solution.py:439
  (3 shorter events, 0.1 us)
Async XLA Ops:
  1.9 15.5 %all-to-all-start = ((s32[16,1,15]{2,1,0:T(1,128)}), s32[16,1,15]{2,1,0:T(1,128)S(1)}, u32[]{:S(2)}, u32[]{:S(2)}) async-start(s32[16,1,15]{2,1,0:T(1,128)} %broadcast_in_dim.4), calls=%async_computation | async-start | bytes 16384 | tf_op jit(solution)/shard_map/all_to_all | solution.py:469
  17.4 0.6 copy-start
  27.3 10.3 %copy-start.1 = (s32[15,180]{1,0:T(8,128)S(1)}, s32[15,180]{1,0:T(8,128)}, u32[]{:S(2)}) copy-start(s32[15,180]{1,0:T(8,128)} %param.5) | copy-start | bytes 32404
  27.3 48.8 %all-to-all-start.1 = ((bf16[128,88,128]{2,1,0:T(8,128)(2,1)}), bf16[128,88,128]{2,1,0:T(8,128)(2,1)S(1)}, u32[]{:S(2)}, u32[]{:S(2)}) async-start(bf16[128,88,128]{2,1,0:T(8,128)(2,1)} %bitcast.12), calls=%async_computation.1 | async-start | bytes 5767168 | tf_op jit(solution)/shard_map/all_to_all | solution.py:469
  78.4 1.9 %collective-permute-start = (f32[640,128]{1,0:T(8,128)S(1)}, f32[640,128]{1,0:T(8,128)S(1)}, u32[]{:S(2)}, u32[]{:S(2)}) collective-permute-start(f32[640,128]{1,0:T(8,128)S(1)} %get-tuple-element.8), channel_id=1, source_target_pairs={{0,1},{1,0},{2,3},{3,2},{4,5},{5,4},{6,7},{7,6},{8,9},{9,8},{10,11... | collective-permute-start | bytes 983048 | tf_op jit(solution)/shard_map/ppermute | solution.py:478
  110.5 4.2 %collective-permute-start.1 = (f32[640,128]{1,0:T(8,128)S(1)}, f32[640,128]{1,0:T(8,128)S(1)}, u32[]{:S(2)}, u32[]{:S(2)}) collective-permute-start(f32[640,128]{1,0:T(8,128)S(1)} %bitcast.10), channel_id=1, source_target_pairs={{0,1},{1,0},{2,3},{3,2},{4,5},{5,4},{6,7},{7,6},{8,9},{9,8},{10,11... | collective-permute-start | bytes 983048 | tf_op jit(solution)/shard_map/ppermute | solution.py:478

commit v9 on v8

--- a/solution.py
+++ b/solution.py
@@ -372,7 +372,7 @@
         column = lax.broadcasted_iota(jnp.int32, value.shape, 1)
         return jnp.where(row == column, value + scale, value)
 
-    split(ws, 0, gram / frobenius)
+    split(ws, 0, gram * (1.0 / frobenius))
     c0, c1, c2, c3, c4 = STEP
     last = ITERS // 2 - 1
 
@@ -383,15 +383,17 @@
             split(hs, start, plus_eye(c3 * join(ws, start) + c4 * square, start, c2))
         for n, value in enumerate(product(ss, hs)):
             start = n * ROWB
-            split(ps, start, plus_eye(value + c1 * join(ws, start), start, c0))
-
-        if k == 0:
-            zs[...] = ps[0 : 2 * MONTHS, :]
+            value = plus_eye(value + c1 * join(ws, start), start, c0)
+            split(ps, start, value)
+            if k == 0:
+                split(zs, start, value)
 
         if k > 0:
             for n, value in enumerate(product(zs, ps)):
-                split(zs, n * ROWB, value)
-                whitener[n * ROWB : (n + 1) * ROWB, :] = value * final_scale
+                if k < last:
+                    split(zs, n * ROWB, value)
+                else:
+                    whitener[n * ROWB : (n + 1) * ROWB, :] = value * final_scale
 
         if k < last:
             for n, value in enumerate(product(ws, ps)):

time: 131 us -> 131 us (level)
  no operation moved by 1% of the time
where the time goes in v9:
time: 131 us; the launch traced here: 130 us
  waiting for transfers between devices  40.1 us (31%)
  Pallas kernels  35.1 us (27%)
  blocking collectives  30.1 us (23%)
  starting transfers between devices  22.3 us (17%)
  local copies, waits for them, and re-layouts  1.87 us (1%)
    all_to_all x2, waiting for transfers between devices, exchange(): return lax.all_to_all(pieces, axes, split_axis=0, concat_axis=0, tiled=True)  38.4 us
    all_to_all x2, blocking collectives, exchange(): return lax.all_to_all(pieces, axes, split_axis=0, concat_axis=0, tiled=True)  30.1 us
    all_to_all x2, starting transfers between devices, exchange(): return lax.all_to_all(pieces, axes, split_axis=0, concat_axis=0, tiled=True)  18.7 us
    pallas_call x1, Pallas kernels, root_and_patterns(): pl.pallas_call(root_kernel, out_shape=(jax.ShapeDtypeStruct((LAT_DEV, LON...  15.6 us
    pallas_call x1, Pallas kernels, smooth(): pl.pallas_call(smooth_kernel, out_shape=jax.ShapeDtypeStruct((N_LON, N_LA...  9.34 us
    pallas_call x1, Pallas kernels, cut_windows(): pl.pallas_call(windows_kernel, out_shape=jax.ShapeDtypeStruct((steps * 16...  7 us
    ppermute x2, starting transfers between devices, swap_cores(): return lax.ppermute(x, 'core', [(0, 1), (1, 0)])  3.6 us
  transfers between devices with their start and end apart: 4, of which 3 were waited for; matrix products, arithmetic and copies ran while one was open for 0% of the time, Pallas kernels for 6%

profile of v9, /device:TPU:1, one launch (start us, length us, event | category | flops | bytes accessed | tf_op | source)
XLA Modules:
  0.0 130.5 jit_solution(6422705517820050622)
XLA Ops:
  0.6 1.3 broadcast_in_dim.4
  1.9 8.4 %all-to-all-start = ((s32[16,1,15]{2,1,0:T(1,128)}), s32[16,1,15]{2,1,0:T(1,128)S(1)}, u32[]{:S(2)}, u32[]{:S(2)}) async-start(s32[16,1,15]{2,1,0:T(1,128)} %broadcast_in_dim.4), calls=%async_computation | async-start | bytes 16384 | tf_op jit(solution)/shard_map/all_to_all | solution.py:471
  10.3 7.0 %cut_windows.1.windows_hbm = bf16[240,96,128]{2,1,0:T(8,128)(2,1)} custom-call(bf16[4,240,1440]{2,1,0:T(8,128)(2,1)} %field_hbm.1), custom_call_target="tpu_custom_call" | custom-call | flops 3000000000 | bytes 9000000 | tf_op jit(solution)/shard_map/cut_windows/pallas_call | solution.py:92
  17.3 0.0 all-to-all-done
  17.4 0.0 copy-start
  17.4 0.6 copy-done
  18.0 9.3 %smooth.1 = bf16[8,16,88,128]{3,2,1,0:T(8,128)(2,1)} custom-call(s32[16,15]{1,0:T(8,128)} %bitcast.14, bf16[240,96,128]{2,1,0:T(8,128)(2,1)} %cut_windows.1.windows_hbm), custom_call_target="tpu_custom_call" | custom-call | tf_op jit(solution)/shard_map/smooth/pallas_call | solution.py:209
  27.3 0.0 copy-start.1
  27.3 10.3 %all-to-all-start.1 = ((bf16[128,88,128]{2,1,0:T(8,128)(2,1)}), bf16[128,88,128]{2,1,0:T(8,128)(2,1)S(1)}, u32[]{:S(2)}, u32[]{:S(2)}) async-start(bf16[128,88,128]{2,1,0:T(8,128)(2,1)} %bitcast.12), calls=%async_computation.1 | async-start | bytes 5767168 | tf_op jit(solution)/shard_map/all_to_all | solution.py:471
  37.6 0.1 cosine_sqrt_fusion
  37.6 0.0 copy-done.1
  37.7 0.1 convert_multiply_fusion
  37.7 38.4 %all-to-all-done.1.landed = bf16[128,88,128]{2,1,0:T(8,128)(2,1)S(1)} async-done(((bf16[128,88,128]{2,1,0:T(8,128)(2,1)}), bf16[128,88,128]{2,1,0:T(8,128)(2,1)S(1)}, u32[]{:S(2)}, u32[]{:S(2)}) %all-to-all-start.1) | async-done | bytes 2883616 | tf_op jit(solution)/shard_map/all_to_all | solution.py:471
  76.1 2.3 %gram_terms.1 = (f32[640,128]{1,0:T(8,128)S(1)}, f32[640,128]{1,0:T(8,128)S(1)}, bf16[512,2816]{1,0:T(8,128)(2,1)S(1)}) custom-call(s32[1]{0:T(128)} %bitcast.core, bf16[128,88,128]{2,1,0:T(8,128)(2,1)S(1)} %all-to-all-done.1.landed, f32[15,256]{1,0:T(8,128)S(1)} %pad.4.weight), custom_call_target="tpu_custom_call" | custom-call | tf_op jit(solution)/shard_map/gram_terms/pallas_call | solution.py:271
  78.4 0.6 collective-permute-start
  79.0 1.3 collective-permute-done
  80.3 15.2 %all_to_all.20 = f32[64,5,2,128]{3,2,1,0:T(2,128)S(1)} all-to-all(f32[64,5,2,128]{3,2,1,0:T(2,128)S(1)} %bitcast.13), channel_id=1, replica_groups=mesh['lon'=8,'chip'=8,'core'=2] {'lon','chip'}, dimensions={0} | all-to-all | bytes 655360 | tf_op jit(solution)/shard_map/all_to_all | solution.py:471
  95.5 14.9 %all_to_all.21 = f32[64,5,2,128]{3,2,1,0:T(2,128)S(1)} all-to-all(f32[64,5,2,128]{3,2,1,0:T(2,128)S(1)} %bitcast.9), channel_id=1, replica_groups=mesh['lon'=8,'chip'=8,'core'=2] {'lon','chip'}, dimensions={0} | all-to-all | bytes 655360 | tf_op jit(solution)/shard_map/all_to_all | solution.py:471
  110.5 3.0 %collective-permute-start.1 = (f32[640,128]{1,0:T(8,128)S(1)}, f32[640,128]{1,0:T(8,128)S(1)}, u32[]{:S(2)}, u32[]{:S(2)}) collective-permute-start(f32[640,128]{1,0:T(8,128)S(1)} %bitcast.10), channel_id=1, source_target_pairs={{0,1},{1,0},{2,3},{3,2},{4,5},{5,4},{6,7},{7,6},{8,9},{9,8},{10,11... | collective-permute-start | bytes 983048 | tf_op jit(solution)/shard_map/ppermute | solution.py:480
  113.4 0.8 turn.1.anomaly
  114.2 0.5 collective-permute-done.1.theirs
  114.7 15.6 %root_and_patterns.1 = (bf16[15,180,512]{2,1,0:T(8,128)(2,1)}, f32[512,512]{1,0:T(8,128)}) custom-call(s32[1]{0:T(128)} %bitcast.core, f32[640,128]{1,0:T(8,128)S(1)} %bitcast.11, f32[640,128]{1,0:T(8,128)S(1)} %collective-permute-done.1.theirs, bf16[2816,512]{1,0:T(8,128)(2,1)S(1)} %turn.1.anomaly), custom_call_target="tpu_custom_call" | custom-call | tf_op jit(solution)/shard_map/root_and_patterns/pallas_call | solution.py:441
  (3 shorter events, 0.1 us)
Async XLA Ops:
  1.9 15.5 %all-to-all-start = ((s32[16,1,15]{2,1,0:T(1,128)}), s32[16,1,15]{2,1,0:T(1,128)S(1)}, u32[]{:S(2)}, u32[]{:S(2)}) async-start(s32[16,1,15]{2,1,0:T(1,128)} %broadcast_in_dim.4), calls=%async_computation | async-start | bytes 16384 | tf_op jit(solution)/shard_map/all_to_all | solution.py:471
  17.4 0.6 copy-start
  27.3 10.3 %copy-start.1 = (s32[15,180]{1,0:T(8,128)S(1)}, s32[15,180]{1,0:T(8,128)}, u32[]{:S(2)}) copy-start(s32[15,180]{1,0:T(8,128)} %param.5) | copy-start | bytes 32404
  27.3 48.8 %all-to-all-start.1 = ((bf16[128,88,128]{2,1,0:T(8,128)(2,1)}), bf16[128,88,128]{2,1,0:T(8,128)(2,1)S(1)}, u32[]{:S(2)}, u32[]{:S(2)}) async-start(bf16[128,88,128]{2,1,0:T(8,128)(2,1)} %bitcast.12), calls=%async_computation.1 | async-start | bytes 5767168 | tf_op jit(solution)/shard_map/all_to_all | solution.py:471
  78.4 1.9 %collective-permute-start = (f32[640,128]{1,0:T(8,128)S(1)}, f32[640,128]{1,0:T(8,128)S(1)}, u32[]{:S(2)}, u32[]{:S(2)}) collective-permute-start(f32[640,128]{1,0:T(8,128)S(1)} %get-tuple-element.8), channel_id=1, source_target_pairs={{0,1},{1,0},{2,3},{3,2},{4,5},{5,4},{6,7},{7,6},{8,9},{9,8},{10,11... | collective-permute-start | bytes 983048 | tf_op jit(solution)/shard_map/ppermute | solution.py:480
  110.5 4.2 %collective-permute-start.1 = (f32[640,128]{1,0:T(8,128)S(1)}, f32[640,128]{1,0:T(8,128)S(1)}, u32[]{:S(2)}, u32[]{:S(2)}) collective-permute-start(f32[640,128]{1,0:T(8,128)S(1)} %bitcast.10), channel_id=1, source_target_pairs={{0,1},{1,0},{2,3},{3,2},{4,5},{5,4},{6,7},{7,6},{8,9},{9,8},{10,11... | collective-permute-start | bytes 983048 | tf_op jit(solution)/shard_map/ppermute | solution.py:480

commit v10 on v9

--- a/solution.py
+++ b/solution.py
@@ -36,6 +36,7 @@
 BLOCKS = [(i, j) for i in range(4) for j in range(i, 4)]
 PACK = len(BLOCKS)
 VMEM_LIMIT = 60 * 1024 * 1024
+SMOOTH_LIMIT = 52 * 1024 * 1024
 
 
 def lat_taps():
@@ -223,7 +224,7 @@
             pltpu.SemaphoreType.DMA((N_LAT,)),
             pltpu.SemaphoreType.DMA,
         ],
-        compiler_params=pltpu.CompilerParams(vmem_limit_bytes=VMEM_LIMIT),
+        compiler_params=pltpu.CompilerParams(vmem_limit_bytes=SMOOTH_LIMIT),
         name="smooth",
     )(widths, windows)
     return out.reshape(N_LON * N_LAT, CHUNK, LANES)

time: 131 us -> 130 us (level)
  no operation moved by 1% of the time
where the time goes in v10:
time: 130 us; the launch traced here: 129 us
  waiting for transfers between devices  40.1 us (31%)
  Pallas kernels  34.4 us (26%)
  blocking collectives  30.1 us (23%)
  starting transfers between devices  22.3 us (17%)
    all_to_all x2, waiting for transfers between devices, exchange(): return lax.all_to_all(pieces, axes, split_axis=0, concat_axis=0, tiled=True)  38.4 us
    all_to_all x2, blocking collectives, exchange(): return lax.all_to_all(pieces, axes, split_axis=0, concat_axis=0, tiled=True)  30.1 us
    all_to_all x2, starting transfers between devices, exchange(): return lax.all_to_all(pieces, axes, split_axis=0, concat_axis=0, tiled=True)  18.7 us
    pallas_call x1, Pallas kernels, root_and_patterns(): pl.pallas_call(root_kernel, out_shape=(jax.ShapeDtypeStruct((LAT_DEV, LON...  15.6 us
    pallas_call x1, Pallas kernels, smooth(): pl.pallas_call(smooth_kernel, out_shape=jax.ShapeDtypeStruct((N_LON, N_LA...  8.68 us
    pallas_call x1, Pallas kernels, cut_windows(): pl.pallas_call(windows_kernel, out_shape=jax.ShapeDtypeStruct((steps * 16...  7 us
    ppermute x2, starting transfers between devices, swap_cores(): return lax.ppermute(x, 'core', [(0, 1), (1, 0)])  3.6 us
  transfers between devices with their start and end apart: 4, of which 3 were waited for; matrix products, arithmetic and copies ran while one was open for 0% of the time, Pallas kernels for 6%

profile of v10, /device:TPU:1, one launch (start us, length us, event | category | flops | bytes accessed | tf_op | source)
XLA Modules:
  0.0 129.3 jit_solution(2983936259931846814)
XLA Ops:
  0.6 1.3 broadcast_in_dim.4
  1.9 8.4 %all-to-all-start = ((s32[16,1,15]{2,1,0:T(1,128)}), s32[16,1,15]{2,1,0:T(1,128)S(1)}, u32[]{:S(2)}, u32[]{:S(2)}) async-start(s32[16,1,15]{2,1,0:T(1,128)} %broadcast_in_dim.4), calls=%async_computation | async-start | bytes 16384 | tf_op jit(solution)/shard_map/all_to_all | solution.py:472
  10.3 7.0 %cut_windows.1.windows_hbm = bf16[240,96,128]{2,1,0:T(8,128)(2,1)} custom-call(bf16[4,240,1440]{2,1,0:T(8,128)(2,1)} %field_hbm.1), custom_call_target="tpu_custom_call" | custom-call | flops 3000000000 | bytes 9000000 | tf_op jit(solution)/shard_map/cut_windows/pallas_call | solution.py:93
  17.3 0.0 all-to-all-done
  17.4 8.7 %smooth.1 = bf16[8,16,88,128]{3,2,1,0:T(8,128)(2,1)} custom-call(s32[16,15]{1,0:T(8,128)S(1)} %bitcast.12, bf16[240,96,128]{2,1,0:T(8,128)(2,1)} %cut_windows.1.windows_hbm), custom_call_target="tpu_custom_call" | custom-call | tf_op jit(solution)/shard_map/smooth/pallas_call | solution.py:210
  26.0 0.0 copy-start
  26.1 10.3 %all-to-all-start.1 = ((bf16[128,88,128]{2,1,0:T(8,128)(2,1)}), bf16[128,88,128]{2,1,0:T(8,128)(2,1)S(1)}, u32[]{:S(2)}, u32[]{:S(2)}) async-start(bf16[128,88,128]{2,1,0:T(8,128)(2,1)} %bitcast.13), calls=%async_computation.1 | async-start | bytes 5767168 | tf_op jit(solution)/shard_map/all_to_all | solution.py:472
  36.4 0.1 cosine_sqrt_fusion
  36.4 0.0 copy-done
  36.4 0.1 convert_multiply_fusion
  36.5 38.4 %all-to-all-done.1.landed = bf16[128,88,128]{2,1,0:T(8,128)(2,1)S(1)} async-done(((bf16[128,88,128]{2,1,0:T(8,128)(2,1)}), bf16[128,88,128]{2,1,0:T(8,128)(2,1)S(1)}, u32[]{:S(2)}, u32[]{:S(2)}) %all-to-all-start.1) | async-done | bytes 2883616 | tf_op jit(solution)/shard_map/all_to_all | solution.py:472
  74.9 2.3 %gram_terms.1 = (f32[640,128]{1,0:T(8,128)S(1)}, f32[640,128]{1,0:T(8,128)S(1)}, bf16[512,2816]{1,0:T(8,128)(2,1)S(1)}) custom-call(s32[1]{0:T(128)} %bitcast.core, bf16[128,88,128]{2,1,0:T(8,128)(2,1)S(1)} %all-to-all-done.1.landed, f32[15,256]{1,0:T(8,128)S(1)} %pad.4.weight), custom_call_target="tpu_custom_call" | custom-call | tf_op jit(solution)/shard_map/gram_terms/pallas_call | solution.py:272
  77.2 0.6 collective-permute-start
  77.8 1.3 collective-permute-done
  79.1 15.2 %all_to_all.20 = f32[64,5,2,128]{3,2,1,0:T(2,128)S(1)} all-to-all(f32[64,5,2,128]{3,2,1,0:T(2,128)S(1)} %bitcast.14), channel_id=1, replica_groups=mesh['lon'=8,'chip'=8,'core'=2] {'lon','chip'}, dimensions={0} | all-to-all | bytes 655360 | tf_op jit(solution)/shard_map/all_to_all | solution.py:472
  94.3 14.9 %all_to_all.21 = f32[64,5,2,128]{3,2,1,0:T(2,128)S(1)} all-to-all(f32[64,5,2,128]{3,2,1,0:T(2,128)S(1)} %bitcast.9), channel_id=1, replica_groups=mesh['lon'=8,'chip'=8,'core'=2] {'lon','chip'}, dimensions={0} | all-to-all | bytes 655360 | tf_op jit(solution)/shard_map/all_to_all | solution.py:472
  109.2 3.0 %collective-permute-start.1 = (f32[640,128]{1,0:T(8,128)S(1)}, f32[640,128]{1,0:T(8,128)S(1)}, u32[]{:S(2)}, u32[]{:S(2)}) collective-permute-start(f32[640,128]{1,0:T(8,128)S(1)} %bitcast.10), channel_id=1, source_target_pairs={{0,1},{1,0},{2,3},{3,2},{4,5},{5,4},{6,7},{7,6},{8,9},{9,8},{10,11... | collective-permute-start | bytes 983048 | tf_op jit(solution)/shard_map/ppermute | solution.py:481
  112.2 0.8 turn.1.anomaly
  113.0 0.5 collective-permute-done.1.theirs
  113.5 15.6 %root_and_patterns.1 = (bf16[15,180,512]{2,1,0:T(8,128)(2,1)}, f32[512,512]{1,0:T(8,128)}) custom-call(s32[1]{0:T(128)} %bitcast.core, f32[640,128]{1,0:T(8,128)S(1)} %bitcast.11, f32[640,128]{1,0:T(8,128)S(1)} %collective-permute-done.1.theirs, bf16[2816,512]{1,0:T(8,128)(2,1)S(1)} %turn.1.anomaly), custom_call_target="tpu_custom_call" | custom-call | tf_op jit(solution)/shard_map/root_and_patterns/pallas_call | solution.py:442
  (3 shorter events, 0.1 us)
Async XLA Ops:
  1.9 15.5 %all-to-all-start = ((s32[16,1,15]{2,1,0:T(1,128)}), s32[16,1,15]{2,1,0:T(1,128)S(1)}, u32[]{:S(2)}, u32[]{:S(2)}) async-start(s32[16,1,15]{2,1,0:T(1,128)} %broadcast_in_dim.4), calls=%async_computation | async-start | bytes 16384 | tf_op jit(solution)/shard_map/all_to_all | solution.py:472
  26.0 10.4 %copy-start = (s32[15,180]{1,0:T(8,128)S(1)}, s32[15,180]{1,0:T(8,128)}, u32[]{:S(2)}) copy-start(s32[15,180]{1,0:T(8,128)} %param.5) | copy-start | bytes 32404
  26.1 48.8 %all-to-all-start.1 = ((bf16[128,88,128]{2,1,0:T(8,128)(2,1)}), bf16[128,88,128]{2,1,0:T(8,128)(2,1)S(1)}, u32[]{:S(2)}, u32[]{:S(2)}) async-start(bf16[128,88,128]{2,1,0:T(8,128)(2,1)} %bitcast.13), calls=%async_computation.1 | async-start | bytes 5767168 | tf_op jit(solution)/shard_map/all_to_all | solution.py:472
  77.2 1.9 %collective-permute-start = (f32[640,128]{1,0:T(8,128)S(1)}, f32[640,128]{1,0:T(8,128)S(1)}, u32[]{:S(2)}, u32[]{:S(2)}) collective-permute-start(f32[640,128]{1,0:T(8,128)S(1)} %get-tuple-element.8), channel_id=1, source_target_pairs={{0,1},{1,0},{2,3},{3,2},{4,5},{5,4},{6,7},{7,6},{8,9},{9,8},{10,11... | collective-permute-start | bytes 983048 | tf_op jit(solution)/shard_map/ppermute | solution.py:481
  109.2 4.2 %collective-permute-start.1 = (f32[640,128]{1,0:T(8,128)S(1)}, f32[640,128]{1,0:T(8,128)S(1)}, u32[]{:S(2)}, u32[]{:S(2)}) collective-permute-start(f32[640,128]{1,0:T(8,128)S(1)} %bitcast.10), channel_id=1, source_target_pairs={{0,1},{1,0},{2,3},{3,2},{4,5},{5,4},{6,7},{7,6},{8,9},{9,8},{10,11... | collective-permute-start | bytes 983048 | tf_op jit(solution)/shard_map/ppermute | solution.py:481

commit v11 on v10

--- a/solution.py
+++ b/solution.py
@@ -408,9 +408,9 @@
     copies[0].start()
     wb[...] = whitener[...].astype(jnp.bfloat16)
 
-    def group(g):
+    def group(g, count=1):
         return lax.dot_general(
-            anomaly[g * LANES : (g + 1) * LANES, :],
+            anomaly[g * LANES : (g + count) * LANES, :],
             wb[...],
             (((1,), (0,)), ((), ())),
             preferred_element_type=jnp.float32,
@@ -429,9 +429,10 @@
             first = LANES + 16 * q
             size = min(16, LON_DEV - first)
             patterns[LAT_DEV - 1, first : first + size, :] = value[TAIL : TAIL + size]
-        for r in (2 * q, 2 * q + 1):
-            patterns[r, 0:LANES, :] = group(r)
-            finish(r)
+        pair = group(2 * q, 2)
+        for n in range(2):
+            patterns[2 * q + n, 0:LANES, :] = pair[n * LANES : (n + 1) * LANES]
+            finish(2 * q + n)
     patterns[LAT_DEV - 1, 0:LANES, :] = group(LAT_DEV - 1)
     finish(LAT_DEV - 1)
     for copy in copies:

time: 130 us -> 130 us (level)
  no operation moved by 1% of the time
where the time goes in v11:
time: 130 us; the launch traced here: 129 us
  waiting for transfers between devices  40.1 us (31%)
  Pallas kernels  34.5 us (27%)
  blocking collectives  30.1 us (23%)
  starting transfers between devices  22.3 us (17%)
    all_to_all x2, waiting for transfers between devices, exchange(): return lax.all_to_all(pieces, axes, split_axis=0, concat_axis=0, tiled=True)  38.4 us
    all_to_all x2, blocking collectives, exchange(): return lax.all_to_all(pieces, axes, split_axis=0, concat_axis=0, tiled=True)  30.1 us
    all_to_all x2, starting transfers between devices, exchange(): return lax.all_to_all(pieces, axes, split_axis=0, concat_axis=0, tiled=True)  18.7 us
    pallas_call x1, Pallas kernels, root_and_patterns(): pl.pallas_call(root_kernel, out_shape=(jax.ShapeDtypeStruct((LAT_DEV, LON...  15.7 us
    pallas_call x1, Pallas kernels, smooth(): pl.pallas_call(smooth_kernel, out_shape=jax.ShapeDtypeStruct((N_LON, N_LA...  8.68 us
    pallas_call x1, Pallas kernels, cut_windows(): pl.pallas_call(windows_kernel, out_shape=jax.ShapeDtypeStruct((steps * 16...  7 us
    ppermute x2, starting transfers between devices, swap_cores(): return lax.ppermute(x, 'core', [(0, 1), (1, 0)])  3.6 us
  transfers between devices with their start and end apart: 4, of which 3 were waited for; matrix products, arithmetic and copies ran while one was open for 0% of the time, Pallas kernels for 6%

profile of v11, /device:TPU:1, one launch (start us, length us, event | category | flops | bytes accessed | tf_op | source)
XLA Modules:
  0.0 129.3 jit_solution(1814822772871599076)
XLA Ops:
  0.6 1.3 broadcast_in_dim.4
  1.9 8.4 %all-to-all-start = ((s32[16,1,15]{2,1,0:T(1,128)}), s32[16,1,15]{2,1,0:T(1,128)S(1)}, u32[]{:S(2)}, u32[]{:S(2)}) async-start(s32[16,1,15]{2,1,0:T(1,128)} %broadcast_in_dim.4), calls=%async_computation | async-start | bytes 16384 | tf_op jit(solution)/shard_map/all_to_all | solution.py:473
  10.3 7.0 %cut_windows.1.windows_hbm = bf16[240,96,128]{2,1,0:T(8,128)(2,1)} custom-call(bf16[4,240,1440]{2,1,0:T(8,128)(2,1)} %field_hbm.1), custom_call_target="tpu_custom_call" | custom-call | flops 3000000000 | bytes 9000000 | tf_op jit(solution)/shard_map/cut_windows/pallas_call | solution.py:93
  17.3 0.0 all-to-all-done
  17.4 8.7 %smooth.1 = bf16[8,16,88,128]{3,2,1,0:T(8,128)(2,1)} custom-call(s32[16,15]{1,0:T(8,128)S(1)} %bitcast.12, bf16[240,96,128]{2,1,0:T(8,128)(2,1)} %cut_windows.1.windows_hbm), custom_call_target="tpu_custom_call" | custom-call | tf_op jit(solution)/shard_map/smooth/pallas_call | solution.py:210
  26.0 0.0 copy-start
  26.1 10.3 %all-to-all-start.1 = ((bf16[128,88,128]{2,1,0:T(8,128)(2,1)}), bf16[128,88,128]{2,1,0:T(8,128)(2,1)S(1)}, u32[]{:S(2)}, u32[]{:S(2)}) async-start(bf16[128,88,128]{2,1,0:T(8,128)(2,1)} %bitcast.13), calls=%async_computation.1 | async-start | bytes 5767168 | tf_op jit(solution)/shard_map/all_to_all | solution.py:473
  36.4 0.1 cosine_sqrt_fusion
  36.4 0.0 copy-done
  36.4 0.1 convert_multiply_fusion
  36.5 38.4 %all-to-all-done.1.landed = bf16[128,88,128]{2,1,0:T(8,128)(2,1)S(1)} async-done(((bf16[128,88,128]{2,1,0:T(8,128)(2,1)}), bf16[128,88,128]{2,1,0:T(8,128)(2,1)S(1)}, u32[]{:S(2)}, u32[]{:S(2)}) %all-to-all-start.1) | async-done | bytes 2883616 | tf_op jit(solution)/shard_map/all_to_all | solution.py:473
  74.9 2.3 %gram_terms.1 = (f32[640,128]{1,0:T(8,128)S(1)}, f32[640,128]{1,0:T(8,128)S(1)}, bf16[512,2816]{1,0:T(8,128)(2,1)S(1)}) custom-call(s32[1]{0:T(128)} %bitcast.core, bf16[128,88,128]{2,1,0:T(8,128)(2,1)S(1)} %all-to-all-done.1.landed, f32[15,256]{1,0:T(8,128)S(1)} %pad.4.weight), custom_call_target="tpu_custom_call" | custom-call | tf_op jit(solution)/shard_map/gram_terms/pallas_call | solution.py:272
  77.2 0.6 collective-permute-start
  77.8 1.3 collective-permute-done
  79.1 15.2 %all_to_all.20 = f32[64,5,2,128]{3,2,1,0:T(2,128)S(1)} all-to-all(f32[64,5,2,128]{3,2,1,0:T(2,128)S(1)} %bitcast.14), channel_id=1, replica_groups=mesh['lon'=8,'chip'=8,'core'=2] {'lon','chip'}, dimensions={0} | all-to-all | bytes 655360 | tf_op jit(solution)/shard_map/all_to_all | solution.py:473
  94.3 14.9 %all_to_all.21 = f32[64,5,2,128]{3,2,1,0:T(2,128)S(1)} all-to-all(f32[64,5,2,128]{3,2,1,0:T(2,128)S(1)} %bitcast.9), channel_id=1, replica_groups=mesh['lon'=8,'chip'=8,'core'=2] {'lon','chip'}, dimensions={0} | all-to-all | bytes 655360 | tf_op jit(solution)/shard_map/all_to_all | solution.py:473
  109.2 3.0 %collective-permute-start.1 = (f32[640,128]{1,0:T(8,128)S(1)}, f32[640,128]{1,0:T(8,128)S(1)}, u32[]{:S(2)}, u32[]{:S(2)}) collective-permute-start(f32[640,128]{1,0:T(8,128)S(1)} %bitcast.10), channel_id=1, source_target_pairs={{0,1},{1,0},{2,3},{3,2},{4,5},{5,4},{6,7},{7,6},{8,9},{9,8},{10,11... | collective-permute-start | bytes 983048 | tf_op jit(solution)/shard_map/ppermute | solution.py:482
  112.2 0.8 turn.1.anomaly
  113.0 0.5 collective-permute-done.1.theirs
  113.5 15.7 %root_and_patterns.1 = (bf16[15,180,512]{2,1,0:T(8,128)(2,1)}, f32[512,512]{1,0:T(8,128)}) custom-call(s32[1]{0:T(128)} %bitcast.core, f32[640,128]{1,0:T(8,128)S(1)} %bitcast.11, f32[640,128]{1,0:T(8,128)S(1)} %collective-permute-done.1.theirs, bf16[2816,512]{1,0:T(8,128)(2,1)S(1)} %turn.1.anomaly), custom_call_target="tpu_custom_call" | custom-call | tf_op jit(solution)/shard_map/root_and_patterns/pallas_call | solution.py:443
  (3 shorter events, 0.1 us)
Async XLA Ops:
  1.9 15.5 %all-to-all-start = ((s32[16,1,15]{2,1,0:T(1,128)}), s32[16,1,15]{2,1,0:T(1,128)S(1)}, u32[]{:S(2)}, u32[]{:S(2)}) async-start(s32[16,1,15]{2,1,0:T(1,128)} %broadcast_in_dim.4), calls=%async_computation | async-start | bytes 16384 | tf_op jit(solution)/shard_map/all_to_all | solution.py:473
  26.0 10.4 %copy-start = (s32[15,180]{1,0:T(8,128)S(1)}, s32[15,180]{1,0:T(8,128)}, u32[]{:S(2)}) copy-start(s32[15,180]{1,0:T(8,128)} %param.5) | copy-start | bytes 32404
  26.1 48.8 %all-to-all-start.1 = ((bf16[128,88,128]{2,1,0:T(8,128)(2,1)}), bf16[128,88,128]{2,1,0:T(8,128)(2,1)S(1)}, u32[]{:S(2)}, u32[]{:S(2)}) async-start(bf16[128,88,128]{2,1,0:T(8,128)(2,1)} %bitcast.13), calls=%async_computation.1 | async-start | bytes 5767168 | tf_op jit(solution)/shard_map/all_to_all | solution.py:473
  77.2 1.9 %collective-permute-start = (f32[640,128]{1,0:T(8,128)S(1)}, f32[640,128]{1,0:T(8,128)S(1)}, u32[]{:S(2)}, u32[]{:S(2)}) collective-permute-start(f32[640,128]{1,0:T(8,128)S(1)} %get-tuple-element.8), channel_id=1, source_target_pairs={{0,1},{1,0},{2,3},{3,2},{4,5},{5,4},{6,7},{7,6},{8,9},{9,8},{10,11... | collective-permute-start | bytes 983048 | tf_op jit(solution)/shard_map/ppermute | solution.py:482
  109.2 4.2 %collective-permute-start.1 = (f32[640,128]{1,0:T(8,128)S(1)}, f32[640,128]{1,0:T(8,128)S(1)}, u32[]{:S(2)}, u32[]{:S(2)}) collective-permute-start(f32[640,128]{1,0:T(8,128)S(1)} %bitcast.10), channel_id=1, source_target_pairs={{0,1},{1,0},{2,3},{3,2},{4,5},{5,4},{6,7},{7,6},{8,9},{9,8},{10,11... | collective-permute-start | bytes 983048 | tf_op jit(solution)/shard_map/ppermute | solution.py:482

commit v12 on v10

--- a/solution.py
+++ b/solution.py
@@ -235,7 +235,7 @@
         wide[pl.ds(pl.multiple_of(s * CHUNK, 8), CHUNK), :] = landed[s].astype(jnp.float32)
         return carry
 
-    lax.fori_loop(0, N_LON * N_LAT, widen, 0, unroll=4)
+    lax.fori_loop(0, N_LON * N_LAT, widen, 0, unroll=16)
     lane = lax.broadcasted_iota(jnp.int32, (1, LANES), 1)
     for g in range(GROUPS):
         if g < LAT_DEV:

time: 130 us -> 130 us (level)
  no operation moved by 1% of the time
where the time goes in v12:
time: 130 us; the launch traced here: 129 us
  waiting for transfers between devices  40.1 us (31%)
  Pallas kernels  34.4 us (26%)
  blocking collectives  30.1 us (23%)
  starting transfers between devices  22.3 us (17%)
    all_to_all x2, waiting for transfers between devices, exchange(): return lax.all_to_all(pieces, axes, split_axis=0, concat_axis=0, tiled=True)  38.4 us
    all_to_all x2, blocking collectives, exchange(): return lax.all_to_all(pieces, axes, split_axis=0, concat_axis=0, tiled=True)  30.1 us
    all_to_all x2, starting transfers between devices, exchange(): return lax.all_to_all(pieces, axes, split_axis=0, concat_axis=0, tiled=True)  18.7 us
    pallas_call x1, Pallas kernels, root_and_patterns(): pl.pallas_call(root_kernel, out_shape=(jax.ShapeDtypeStruct((LAT_DEV, LON...  15.6 us
    pallas_call x1, Pallas kernels, smooth(): pl.pallas_call(smooth_kernel, out_shape=jax.ShapeDtypeStruct((N_LON, N_LA...  8.68 us
    pallas_call x1, Pallas kernels, cut_windows(): pl.pallas_call(windows_kernel, out_shape=jax.ShapeDtypeStruct((steps * 16...  7 us
    ppermute x2, starting transfers between devices, swap_cores(): return lax.ppermute(x, 'core', [(0, 1), (1, 0)])  3.6 us
  transfers between devices with their start and end apart: 4, of which 3 were waited for; matrix products, arithmetic and copies ran while one was open for 0% of the time, Pallas kernels for 6%

profile of v12, /device:TPU:1, one launch (start us, length us, event | category | flops | bytes accessed | tf_op | source)
XLA Modules:
  0.0 129.2 jit_solution(13147901251561650649)
XLA Ops:
  0.6 1.3 broadcast_in_dim.4
  1.9 8.4 %all-to-all-start = ((s32[16,1,15]{2,1,0:T(1,128)}), s32[16,1,15]{2,1,0:T(1,128)S(1)}, u32[]{:S(2)}, u32[]{:S(2)}) async-start(s32[16,1,15]{2,1,0:T(1,128)} %broadcast_in_dim.4), calls=%async_computation | async-start | bytes 16384 | tf_op jit(solution)/shard_map/all_to_all | solution.py:472
  10.3 7.0 %cut_windows.1.windows_hbm = bf16[240,96,128]{2,1,0:T(8,128)(2,1)} custom-call(bf16[4,240,1440]{2,1,0:T(8,128)(2,1)} %field_hbm.1), custom_call_target="tpu_custom_call" | custom-call | flops 3000000000 | bytes 9000000 | tf_op jit(solution)/shard_map/cut_windows/pallas_call | solution.py:93
  17.3 0.0 all-to-all-done
  17.4 8.7 %smooth.1 = bf16[8,16,88,128]{3,2,1,0:T(8,128)(2,1)} custom-call(s32[16,15]{1,0:T(8,128)S(1)} %bitcast.12, bf16[240,96,128]{2,1,0:T(8,128)(2,1)} %cut_windows.1.windows_hbm), custom_call_target="tpu_custom_call" | custom-call | tf_op jit(solution)/shard_map/smooth/pallas_call | solution.py:210
  26.0 0.0 copy-start
  26.1 10.3 %all-to-all-start.1 = ((bf16[128,88,128]{2,1,0:T(8,128)(2,1)}), bf16[128,88,128]{2,1,0:T(8,128)(2,1)S(1)}, u32[]{:S(2)}, u32[]{:S(2)}) async-start(bf16[128,88,128]{2,1,0:T(8,128)(2,1)} %bitcast.13), calls=%async_computation.1 | async-start | bytes 5767168 | tf_op jit(solution)/shard_map/all_to_all | solution.py:472
  36.4 0.1 cosine_sqrt_fusion
  36.4 0.0 copy-done
  36.4 0.1 convert_multiply_fusion
  36.5 38.4 %all-to-all-done.1.landed = bf16[128,88,128]{2,1,0:T(8,128)(2,1)S(1)} async-done(((bf16[128,88,128]{2,1,0:T(8,128)(2,1)}), bf16[128,88,128]{2,1,0:T(8,128)(2,1)S(1)}, u32[]{:S(2)}, u32[]{:S(2)}) %all-to-all-start.1) | async-done | bytes 2883616 | tf_op jit(solution)/shard_map/all_to_all | solution.py:472
  74.9 2.2 %gram_terms.1 = (f32[640,128]{1,0:T(8,128)S(1)}, f32[640,128]{1,0:T(8,128)S(1)}, bf16[512,2816]{1,0:T(8,128)(2,1)S(1)}) custom-call(s32[1]{0:T(128)} %bitcast.core, bf16[128,88,128]{2,1,0:T(8,128)(2,1)S(1)} %all-to-all-done.1.landed, f32[15,256]{1,0:T(8,128)S(1)} %pad.4.weight), custom_call_target="tpu_custom_call" | custom-call | tf_op jit(solution)/shard_map/gram_terms/pallas_call | solution.py:272
  77.1 0.6 collective-permute-start
  77.7 1.3 collective-permute-done
  79.0 15.2 %all_to_all.20 = f32[64,5,2,128]{3,2,1,0:T(2,128)S(1)} all-to-all(f32[64,5,2,128]{3,2,1,0:T(2,128)S(1)} %bitcast.14), channel_id=1, replica_groups=mesh['lon'=8,'chip'=8,'core'=2] {'lon','chip'}, dimensions={0} | all-to-all | bytes 655360 | tf_op jit(solution)/shard_map/all_to_all | solution.py:472
  94.2 14.9 %all_to_all.21 = f32[64,5,2,128]{3,2,1,0:T(2,128)S(1)} all-to-all(f32[64,5,2,128]{3,2,1,0:T(2,128)S(1)} %bitcast.9), channel_id=1, replica_groups=mesh['lon'=8,'chip'=8,'core'=2] {'lon','chip'}, dimensions={0} | all-to-all | bytes 655360 | tf_op jit(solution)/shard_map/all_to_all | solution.py:472
  109.1 3.0 %collective-permute-start.1 = (f32[640,128]{1,0:T(8,128)S(1)}, f32[640,128]{1,0:T(8,128)S(1)}, u32[]{:S(2)}, u32[]{:S(2)}) collective-permute-start(f32[640,128]{1,0:T(8,128)S(1)} %bitcast.10), channel_id=1, source_target_pairs={{0,1},{1,0},{2,3},{3,2},{4,5},{5,4},{6,7},{7,6},{8,9},{9,8},{10,11... | collective-permute-start | bytes 983048 | tf_op jit(solution)/shard_map/ppermute | solution.py:481
  112.1 0.8 turn.1.anomaly
  112.9 0.5 collective-permute-done.1.theirs
  113.4 15.6 %root_and_patterns.1 = (bf16[15,180,512]{2,1,0:T(8,128)(2,1)}, f32[512,512]{1,0:T(8,128)}) custom-call(s32[1]{0:T(128)} %bitcast.core, f32[640,128]{1,0:T(8,128)S(1)} %bitcast.11, f32[640,128]{1,0:T(8,128)S(1)} %collective-permute-done.1.theirs, bf16[2816,512]{1,0:T(8,128)(2,1)S(1)} %turn.1.anomaly), custom_call_target="tpu_custom_call" | custom-call | tf_op jit(solution)/shard_map/root_and_patterns/pallas_call | solution.py:442
  (3 shorter events, 0.1 us)
Async XLA Ops:
  1.9 15.5 %all-to-all-start = ((s32[16,1,15]{2,1,0:T(1,128)}), s32[16,1,15]{2,1,0:T(1,128)S(1)}, u32[]{:S(2)}, u32[]{:S(2)}) async-start(s32[16,1,15]{2,1,0:T(1,128)} %broadcast_in_dim.4), calls=%async_computation | async-start | bytes 16384 | tf_op jit(solution)/shard_map/all_to_all | solution.py:472
  26.0 10.4 %copy-start = (s32[15,180]{1,0:T(8,128)S(1)}, s32[15,180]{1,0:T(8,128)}, u32[]{:S(2)}) copy-start(s32[15,180]{1,0:T(8,128)} %param.5) | copy-start | bytes 32404
  26.1 48.8 %all-to-all-start.1 = ((bf16[128,88,128]{2,1,0:T(8,128)(2,1)}), bf16[128,88,128]{2,1,0:T(8,128)(2,1)S(1)}, u32[]{:S(2)}, u32[]{:S(2)}) async-start(bf16[128,88,128]{2,1,0:T(8,128)(2,1)} %bitcast.13), calls=%async_computation.1 | async-start | bytes 5767168 | tf_op jit(solution)/shard_map/all_to_all | solution.py:472
  77.1 1.9 %collective-permute-start = (f32[640,128]{1,0:T(8,128)S(1)}, f32[640,128]{1,0:T(8,128)S(1)}, u32[]{:S(2)}, u32[]{:S(2)}) collective-permute-start(f32[640,128]{1,0:T(8,128)S(1)} %get-tuple-element.8), channel_id=1, source_target_pairs={{0,1},{1,0},{2,3},{3,2},{4,5},{5,4},{6,7},{7,6},{8,9},{9,8},{10,11... | collective-permute-start | bytes 983048 | tf_op jit(solution)/shard_map/ppermute | solution.py:481
  109.1 4.2 %collective-permute-start.1 = (f32[640,128]{1,0:T(8,128)S(1)}, f32[640,128]{1,0:T(8,128)S(1)}, u32[]{:S(2)}, u32[]{:S(2)}) collective-permute-start(f32[640,128]{1,0:T(8,128)S(1)} %bitcast.10), channel_id=1, source_target_pairs={{0,1},{1,0},{2,3},{3,2},{4,5},{5,4},{6,7},{7,6},{8,9},{9,8},{10,11... | collective-permute-start | bytes 983048 | tf_op jit(solution)/shard_map/ppermute | solution.py:481
